TPU v7x, 32 devices: a whole 2x2x4 slice. The times are simulated.
32 devices in a mesh: groups: 2 (over y), cand: 4 (over z), tensor: 4 (over x, core).
Axes of the slice: x: 2, y: 2, z: 4, core: 2. Of those that a mesh axis runs over, the one named last changes fastest.
Arguments:
- response_latest_embeddings: bfloat16 [16, 384, 8192], P(('groups', 'cand'), None, 'tensor'), parts along dimension 0, may hold values from -6 to 6
- critic_probe_projector: bfloat16 [8192, 4096], P('cand', 'tensor'), may hold values from -0.0625 to 0.0625
- critic_pair_projector: bfloat16 [8192, 2048], P('cand', 'tensor'), may hold values from -0.0625 to 0.0625
- critic_stored_pairs: bfloat16 [16, 2048, 2048], P(('groups', 'cand'), None, 'tensor'), parts along dimension 0, may hold values from -1000 to 1000
- critic_grading_vector: float32 [4096], P('tensor'), may hold values from -6 to 6
- actor_stored_pairs: bfloat16 [16, 2048, 8, 256], P(('groups', 'cand'), None, 'tensor'), parts along dimension 0, may hold values from -1000 to 1000
- filled_extents: int32 [16], P('groups'), parts along dimension 0, may hold values from 1 to 2048, as said below
- kept_responses: int32 [8], P('groups'), parts along dimension 0, may hold values from 0 to 7, as said below
- actor_latest_probes: bfloat16 [8, 4, 4096], P(('groups', 'cand'), None, 'tensor'), parts along dimension 0, may hold values from -6 to 6
- actor_latest_pairs: bfloat16 [8, 4, 2048], P(('groups', 'cand'), None, 'tensor'), parts along dimension 0, may hold values from -6 to 6
Outputs:
- token_rewards: float32 [16, 384], P(('groups', 'cand')), parts along dimension 0
- actor_mixing_result: bfloat16 [8, 4, 4096], P(('groups', 'cand'), None, 'tensor'), parts along dimension 0
There are 2 independent parts, one for each index of `groups`. A program takes and returns all parts, laid end to end along the dimension named above; an argument that names none is the same for every part. Nothing has to cross between parts.
Inputs may be any that keep to these rules, and one draw needn't show every extreme that they name: `kept_responses`: distinct candidate ids, always including 0 and 7. `filled_extents`: some candidate has exactly 2048 live tokens.
All inputs are finite; a program needn't handle non-finite values.
Results may differ from a plain program's by a relative error of at most 0.012.
The roundings to bfloat16 on the way count: a program that leaves them out, or rounds other values in their place, can miss the bound.
Values may be sent and summed in bfloat16 or wider, within the bound.
No kernel may reach another device: no remote copies, remote signals or barrier semaphores. Data moves between devices by JAX's collectives and lax.ppermute only.
A program may use at most 128 MiB of HBM per device.

v0:
```python
import functools
import math

import jax
import jax.numpy as jnp
from jax import lax
from jax.experimental import pallas as pl
from jax.experimental.pallas import tpu as pltpu
from jax.sharding import PartitionSpec as P

HD = 128
masked_value = -1e30
bf16, f32 = jnp.bfloat16, jnp.float32


def after(value, *earlier):
    return lax.optimization_barrier((value, *earlier))[0]


def shifted(value, axis, step):
    size = lax.axis_size(axis)
    return lax.ppermute(value, axis, [(i, (i + step) % size) for i in range(size)])


def partner(value, axis, bits):
    size = lax.axis_size(axis)
    return lax.ppermute(value, axis, [(i, i ^ bits) for i in range(size)])


def gather_rows(states, rows):
    tensor = lax.axis_size("tensor")
    share = states.reshape(rows, -1)
    half = rows // 2
    own, other = {0: share}, {}
    far_bits = [1 << b for b in range(1, int(math.log2(tensor)))]
    for bit in reversed(far_bits[1:]):
        for off, piece in list(own.items()):
            own[off ^ bit] = partner(piece, "tensor", bit)
    near = far_bits[0]
    corners = {}
    for off, piece in list(own.items()):
        across = partner(piece, "tensor", near)
        other[off] = partner(piece, "groups", 1)
        low = partner(other[off][:half], "tensor", near)
        high = partner(across[half:], "groups", 1)
        own[off ^ near] = across
        corners[off ^ near] = (low, high)
    for pieces in (own, other):
        for off, piece in list(pieces.items()):
            pieces[off ^ 1] = partner(piece, "tensor", 1)
    for off, (low, high) in list(corners.items()):
        corners[off ^ 1] = (partner(low, "tensor", 1), partner(high, "tensor", 1))
    tiles = [[], [], [], []]
    for off in range(tensor):
        low, high = corners.get(off, (None, None))
        tiles[0].append((own[off], 0))
        tiles[1].append((own[off], half))
        tiles[2].append((other[off], 0) if low is None else (low, 0))
        tiles[3].append((other[off], half) if low is None else (high, 0))
    return tiles


def project_kernel(plan, where_ref, *refs):
    sources, tile_of, blocks, widths, has_sum, final = plan
    arrays, refs = refs[:sources], refs[sources:]
    weights, refs = refs[: blocks * len(widths)], refs[blocks * len(widths) :]
    before, refs = (refs[0], refs[1:]) if has_sum else (None, refs)
    out, (tile_buf, weight_buf, sum_buf, tile_sem, weight_sem, sum_sem) = refs[0], refs[1:]
    tile_rows, depth = tile_buf.shape[1:]
    slots = tile_buf.shape[0]
    steps = 4 * blocks

    def load(item):
        block, tile = item // 4, item % 4
        off, column = where_ref[2 * block], where_ref[2 * block + 1]
        column = pl.multiple_of(column, depth)
        slot = lax.rem(item, slots)
        for i, row in enumerate(tile_of):
            for j, (number, start) in enumerate(row):

                @pl.when((tile == i) & (off == j))
                def _():
                    pltpu.make_async_copy(
                        arrays[number].at[pl.ds(start, tile_rows), pl.ds(column, depth)],
                        tile_buf.at[slot],
                        tile_sem.at[slot],
                    ).start()

    copies = []
    for block in range(blocks):
        at = 0
        for j, width in enumerate(widths):
            number = block * len(widths) + j
            copies.append(
                pltpu.make_async_copy(
                    weights[number],
                    weight_buf.at[block, :, at : at + width],
                    weight_sem.at[number],
                )
            )
            at += width
    first = len(widths)
    for copy in copies[:first]:
        copy.start()
    for item in range(slots - 1):
        load(item)
    for copy in copies[first:]:
        copy.start()
    if has_sum:
        sum_copy = pltpu.make_async_copy(before, sum_buf, sum_sem)
        sum_copy.start()
        sum_copy.wait()
    for copy in copies:
        copy.wait()

    def step(item, _):
        @pl.when(item + slots - 1 < steps)
        def _():
            load(item + slots - 1)

        slot = lax.rem(item, slots)
        block, tile = item // 4, item % 4
        pltpu.make_async_copy(
            arrays[0].at[pl.ds(0, tile_rows), pl.ds(0, depth)], tile_buf.at[slot], tile_sem.at[slot]
        ).wait()
        term = jnp.dot(tile_buf[slot], weight_buf[block], preferred_element_type=f32)
        if has_sum:
            term = term + sum_buf[tile]
        else:
            term = jnp.where(block > 0, term + sum_buf[tile], term)
        if final:

            @pl.when(block == blocks - 1)
            def _():
                out[tile] = term.astype(bf16)

        if not final or blocks > 1:
            sum_buf[tile] = term
        return 0

    lax.fori_loop(0, steps, step, 0)
    if not final:
        out[...] = sum_buf[...]


def project(tiles, numbers, weights, before, final):
    arrays, tile_of = [], []
    for row in tiles:
        tile_of.append([])
        for array, start in row:
            known = [i for i, a in enumerate(arrays) if a is array]
            if not known:
                known = [len(arrays)]
                arrays.append(array)
            tile_of[-1].append((known[0], start))
    blocks = len(weights)
    widths = [w.shape[1] for w in weights[0]]
    depth = weights[0][0].shape[0]
    columns = sum(widths)
    tile_rows = tiles[0][1][1] + tiles[1][0][1]
    per_piece = arrays[0].shape[1] // depth
    here = lax.axis_index("tensor")
    where = []
    for number in numbers:
        where += [(number // per_piece) ^ here, number % per_piece * depth]
    where = jnp.stack(where).astype(jnp.int32)
    flat = [w for block in weights for w in block]
    operands = arrays + flat + ([] if before is None else [before])
    plan = (len(arrays), tile_of, blocks, widths, before is not None, final)
    slots = 3
    return pl.pallas_call(
        functools.partial(project_kernel, plan),
        grid_spec=pltpu.PrefetchScalarGridSpec(
            num_scalar_prefetch=1,
            grid=(1,),
            in_specs=[pl.BlockSpec(memory_space=pl.ANY)] * len(operands),
            out_specs=pl.BlockSpec((4, tile_rows, columns), lambda i, w: (0, 0, 0)),
            scratch_shapes=[
                pltpu.VMEM((slots, tile_rows, depth), bf16),
                pltpu.VMEM((blocks, depth, columns), bf16),
                pltpu.VMEM((4, tile_rows, columns), f32),
                pltpu.SemaphoreType.DMA((slots,)),
                pltpu.SemaphoreType.DMA((len(flat),)),
                pltpu.SemaphoreType.DMA,
            ],
        ),
        out_shape=jax.ShapeDtypeStruct((4, tile_rows, columns), bf16 if final else f32),
        compiler_params=pltpu.CompilerParams(vmem_limit_bytes=48 * 1024 * 1024),
        cost_estimate=pl.CostEstimate(
            flops=8 * tile_rows * depth * blocks * columns,
            bytes_accessed=8 * tile_rows * depth * blocks,
            transcendentals=0,
        ),
        name="project",
    )(where, *operands)


def reward_kernel(kg_ref, q_ref, old_key_ref, old_value_ref, key_ref, value_ref, grade_ref, so_far_ref, out_ref):
    span = q_ref.shape[0]
    context = old_key_ref.shape[1]
    rate = HD**-0.5 * math.log2(math.e)
    queries = q_ref[...]
    grade = grade_ref[0]
    block = math.gcd(512, context)
    peak = jnp.full((8, span), -jnp.inf, f32)
    total = jnp.zeros((8, span), f32)
    graded = jnp.zeros((8, span), f32)
    places = [(old_key_ref.at[0], old_value_ref.at[0], i, block) for i in range(0, context, block)]
    places.append((key_ref, value_ref, 0, span))
    for keys, values, start, size in places:
        scores = lax.dot_general(
            keys[start : start + size, :],
            queries,
            (((1,), (1,)), ((), ())),
            preferred_element_type=f32,
        )
        worth = jnp.dot(values[start : start + size, :], grade, preferred_element_type=f32)
        worth = worth[:, :HD] + worth[:, HD:]
        if keys is key_ref:
            shape = (size, span)
            visible = lax.broadcasted_iota(jnp.int32, shape, 0) <= lax.broadcasted_iota(
                jnp.int32, shape, 1
            )
            scores = jnp.where(visible, scores, masked_value)
        scores = scores.reshape(size // 8, 8, span)
        worth = worth.reshape(size // 8, 8, HD)
        new_peak = jnp.maximum(peak, jnp.max(scores, axis=0))
        fade = jnp.exp2((peak - new_peak) * rate)
        weights = jnp.exp2((scores - new_peak[None]) * rate)
        total = total * fade + jnp.sum(weights, axis=0)
        worth = jnp.concatenate([worth] * (span // HD), axis=2)
        graded = graded * fade + jnp.sum(weights * worth, axis=0)
        peak = new_peak
    top = jnp.max(peak, axis=0, keepdims=True)
    fade = jnp.exp2((peak - top) * rate)
    total = jnp.sum(total * fade, axis=0, keepdims=True)
    graded = jnp.sum(graded * fade, axis=0, keepdims=True)
    result = jnp.broadcast_to(graded / total, (8, span))

    @pl.when(pl.program_id(1) == 0)
    def _():
        out_ref[0] = so_far_ref[0] + result

    @pl.when(pl.program_id(1) != 0)
    def _():
        out_ref[0] += result


def grading_columns(grading):
    high = lax.reduce_precision(grading, 8, 7)
    parts = []
    for part in (high, grading - high):
        part = part.astype(bf16).reshape(-1, HD)
        parts.append(jnp.broadcast_to(part[:, :, None], (part.shape[0], HD, HD)))
    return jnp.concatenate(parts, axis=2)


def reward_share(queries, first_head, per_group, stored, fresh, grades, so_far):
    cands, context, _ = stored.shape
    span = queries.shape[0] // cands
    heads = queries.shape[1] // HD
    numbers = first_head + lax.broadcasted_iota(jnp.int32, (heads,), 0)
    groups = numbers // per_group
    grade = lax.dynamic_slice_in_dim(grades, first_head, heads, 0)
    spec = pltpu.PrefetchScalarGridSpec(
        num_scalar_prefetch=1,
        grid=(cands, heads),
        in_specs=[
            pl.BlockSpec((span, HD), lambda c, h, g: (c, h)),
            pl.BlockSpec((1, context, HD), lambda c, h, g: (c, 0, 2 * g[h])),
            pl.BlockSpec((1, context, HD), lambda c, h, g: (c, 0, 2 * g[h] + 1)),
            pl.BlockSpec((span, HD), lambda c, h, g: (c, 2 * g[h])),
            pl.BlockSpec((span, HD), lambda c, h, g: (c, 2 * g[h] + 1)),
            pl.BlockSpec((1, HD, 2 * HD), lambda c, h, g: (h, 0, 0)),
            pl.BlockSpec((1, 8, span), lambda c, h, g: (c, 0, 0)),
        ],
        out_specs=pl.BlockSpec((1, 8, span), lambda c, h, g: (c, 0, 0)),
    )
    cells = cands * heads * span * (context + span)
    return pl.pallas_call(
        reward_kernel,
        grid_spec=spec,
        out_shape=jax.ShapeDtypeStruct((cands, 8, span), f32),
        compiler_params=pltpu.CompilerParams(vmem_limit_bytes=40 * 1024 * 1024),
        cost_estimate=pl.CostEstimate(
            flops=6 * HD * cells, bytes_accessed=4 * stored.size, transcendentals=cells
        ),
        name="reward_share",
    )(groups, queries, stored, stored, fresh, fresh, grade, so_far)


def policy(stored, extents, kept, probes, pairs):
    cand_here = stored.shape[0]
    device_here = lax.axis_index("cand")
    devices = lax.axis_size("cand")
    key_scale = HD ** (-0.5)
    slots_here = probes.shape[0]
    lane_number = kept.shape[0]
    new_count = probes.shape[1]
    kv_here = stored.shape[2]
    policy_heads = probes.shape[2] // HD
    policy_group = policy_heads // kv_here
    cache_len = stored.shape[1]
    own = jnp.concatenate([probes, pairs], axis=2)
    everyone = jnp.zeros((lane_number,) + own.shape[1:], own.dtype)
    for step in range(devices):
        part = shifted(own, "cand", step) if step else own
        at = (device_here - step) % devices * slots_here
        everyone = lax.dynamic_update_slice(everyone, part, (at, 0, 0))
    causal_new = lax.broadcasted_iota(jnp.int32, (new_count, new_count), 0) >= lax.broadcasted_iota(
        jnp.int32, (new_count, new_count), 1
    )
    ids_here = device_here * cand_here + lax.broadcasted_iota(jnp.int32, (cand_here,), 0)
    matched = kept[None, :] == ids_here[:, None]
    slot_index = jnp.sum(
        jnp.where(matched, lax.broadcasted_iota(jnp.int32, (cand_here, lane_number), 1), 0), axis=1
    )
    chosen = jnp.take(everyone, slot_index, axis=0)
    own_queries = chosen[:, :, : policy_heads * HD].reshape(
        cand_here, new_count, kv_here, policy_group, HD
    )
    own_fresh = chosen[:, :, policy_heads * HD :].reshape(cand_here, new_count, kv_here, 2 * HD)
    living = lax.broadcasted_iota(jnp.int32, (cand_here, cache_len), 1)
    living = living < jnp.take(extents, ids_here)[:, None]
    living = living[:, None, None, None, :]
    scores = (
        jnp.einsum("cikgd,ctkd->ckgit", own_queries, stored[..., :HD], preferred_element_type=f32)
        * key_scale
    )
    scores = jnp.where(living, scores, masked_value)
    fresh_scores = (
        jnp.einsum("cikgd,cjkd->ckgij", own_queries, own_fresh[..., :HD], preferred_element_type=f32)
        * key_scale
    )
    fresh_scores = jnp.where(causal_new, fresh_scores, masked_value)
    peak_score = jnp.maximum(jnp.max(scores, axis=-1), jnp.max(fresh_scores, axis=-1))
    old_weights = jnp.where(living, jnp.exp(scores - peak_score[..., None]), 0.0)
    fresh_weights = jnp.where(causal_new, jnp.exp(fresh_scores - peak_score[..., None]), 0.0)
    denominator = jnp.sum(old_weights, axis=-1) + jnp.sum(fresh_weights, axis=-1)
    numerator = jnp.einsum(
        "ckgit,ctkd->ckgid", old_weights, stored[..., HD:], preferred_element_type=f32
    )
    numerator = numerator + jnp.einsum(
        "ckgij,cjkd->ckgid", fresh_weights, own_fresh[..., HD:], preferred_element_type=f32
    )
    result = numerator / denominator[..., None]
    flattened = jnp.transpose(result, (0, 3, 1, 2, 4)).reshape(
        cand_here, new_count * policy_heads * HD
    )
    placed = jnp.einsum(
        "cs,cx->sx", matched.astype(f32), flattened, precision=lax.Precision.HIGHEST
    )
    placed = placed.reshape(lane_number, new_count, policy_heads * HD).astype(bf16)
    rows = jnp.zeros((slots_here,) + placed.shape[1:], f32)
    for step in range(devices):
        at = (device_here + step) % devices * slots_here
        part = lax.dynamic_slice_in_dim(placed, at, slots_here, 0)
        rows = rows + (shifted(part, "cand", step) if step else part).astype(f32)
    return rows.astype(bf16)


def local(
    response_latest_embeddings,
    critic_probe_projector,
    critic_pair_projector,
    critic_stored_pairs,
    critic_grading_vector,
    actor_stored_pairs,
    filled_extents,
    kept_responses,
    actor_latest_probes,
    actor_latest_pairs,
):
    cand_here, span_len, _ = response_latest_embeddings.shape
    rows = cand_here * span_len
    devices = lax.axis_size("cand")
    group = lax.axis_index("groups")
    place = lax.axis_index("cand")
    depth, query_cols = critic_probe_projector.shape
    keyval_cols = critic_pair_projector.shape[1]
    heads_here = query_cols // HD
    per_group = heads_here // (keyval_cols // (2 * HD))
    query_half, keyval_half = query_cols // 2, keyval_cols // 2

    heads_half = heads_here // 2
    own_keyval = lax.dynamic_slice(
        critic_pair_projector, (0, group * keyval_half), (depth, keyval_half)
    )
    own_query = lax.dynamic_slice(
        critic_probe_projector, (0, group * query_half), (depth, query_half)
    )
    chunks = [own_keyval] + [own_query[:, h * HD : (h + 1) * HD] for h in range(heads_half)]
    rings = [chunks]
    tiles = gather_rows(response_latest_embeddings, rows)
    last = devices - 1
    for step in range(last - 1):
        rings.append([shifted(w, "cand", 1) for w in rings[-1]])
    numbers = [(place - step) % devices for step in range(devices)]
    early = project(tiles, numbers[:2], rings[:2], None, False)
    sums = project(tiles, numbers[2:last], rings[2:last], early, False) if last > 2 else early
    waiting = list(rings[-1])
    waiting[-1] = after(waiting[-1], sums)
    rings.append([shifted(w, "cand", 1) for w in waiting])

    grades = grading_columns(critic_grading_vector)
    starts = [0]
    for w in chunks:
        starts.append(starts[-1] + w.shape[1])

    def finish(index, *earlier):
        weights = rings[last][index]
        if earlier:
            weights = after(weights, *earlier)
        before = sums[:, :, starts[index] : starts[index + 1]]
        done = project(tiles, numbers[last:], [[weights]], before, True)
        mine = done[:2].reshape(rows, -1)
        return mine, partner(done[2:].reshape(rows, -1), "groups", 1)

    kept, sent = finish(0)
    keyval = jnp.where(
        group == 0,
        jnp.concatenate([kept, sent], axis=1),
        jnp.concatenate([sent, kept], axis=1),
    )
    share = jnp.zeros((cand_here, 8, span_len), f32)

    def score(queries, owner, head, share):
        return reward_share(
            queries, owner * heads_half + head, per_group, critic_stored_pairs, keyval, grades, share
        )

    kept, sent = finish(1)
    for head in range(heads_half):
        share = score(kept, group, head, share)
        if head + 1 < heads_half:
            kept, next_sent = finish(head + 2, share)
            sent = after(sent, kept)
        share = score(sent, 1 - group, head, share)
        sent = next_sent
    share = share[:, 0, :]
    tensor = lax.axis_size("tensor")
    terms = [share] + [partner(share, "tensor", bits) for bits in range(1, tensor)]
    while len(terms) > 1:
        terms = [a + b for a, b in zip(terms[::2], terms[1::2])]
    slot_rows = policy(
        actor_stored_pairs, filled_extents, kept_responses, actor_latest_probes, actor_latest_pairs
    )
    return terms[0], slot_rows


def solution(mesh):
    placed = (
        P(("groups", "cand"), None, "tensor"),
        P("cand", "tensor"),
        P("cand", "tensor"),
        P(("groups", "cand"), None, "tensor"),
        P("tensor"),
        P(("groups", "cand"), None, "tensor", None),
        P("groups"),
        P("groups"),
        P(("groups", "cand"), None, "tensor"),
        P(("groups", "cand"), None, "tensor"),
    )
    return jax.shard_map(
        local,
        mesh=mesh,
        in_specs=placed,
        out_specs=(P(("groups", "cand"), None), P(("groups", "cand"), None, "tensor")),
        check_vma=False,
    )
```

profile of v0, /device:TPU:0, one launch (start us, length us, event | category | flops | bytes accessed | tf_op | source)
XLA Modules:
  0.0 285.9 jit_solution(9736579081246121796)
XLA Ops:
  0.7 3.0 %collective-permute-start.3 = (bf16[768,2048]{1,0:T(8,128)(2,1)}, bf16[768,2048]{1,0:T(8,128)(2,1)}, u32[]{:S(2)}, u32[]{:S(2)}) collective-permute-start(bf16[768,2048]{1,0:T(8,128)(2,1)} %bitcast.2.refs_0_), channel_id=1, source_target_pairs={{0,16},{16,0},{1,17},{17,1},{2,18},{18,2},{3,19},{19,3},{4,20},{20... | collective-permute-start | bytes 9437192 | tf_op jit(solution)/shard_map/ppermute | solution.py:27
  3.7 1.5 collective-permute-start.1
  6.6 1.6 collective-permute-start.32
  8.2 2.6 collective-permute-start.33
  15.8 6.2 %fusion.36 = (bf16[2,2048,2,128]{3,2,1,0:T(2,128)(2,1)}, bf16[2,2048,2,128]{3,2,1,0:T(2,128)(2,1)}) fusion(bf16[2,2048,2,256]{3,2,1,0:T(2,128)(2,1)} %param.15), kind=kLoop, calls=%fused_computation.102 | loop fusion | bytes 8388608 | tf_op jit(solution)/shard_map/slice | solution.py:327
  22.0 14.6 %collective-permute-done.11.refs_15_ = bf16[2048,256]{1,0:T(8,128)(2,1)} collective-permute-done((bf16[2048,256]{1,0:T(8,128)(2,1)S(1)}, bf16[2048,256]{1,0:T(8,128)(2,1)}, u32[]{:S(2)}, u32[]{:S(2)}) %collective-permute-start.11) | collective-permute-done | bytes 1048608 | tf_op jit(solution)/shard_map/ppermute | solution.py:22
  37.8 3.8 %collective-permute-start.34 = (bf16[1,4,1536]{2,1,0:T(4,128)(2,1)S(1)}, bf16[1,4,1536]{2,1,0:T(4,128)(2,1)S(1)}, u32[]{:S(2)}, u32[]{:S(2)}) collective-permute-start(bf16[1,4,1536]{2,1,0:T(4,128)(2,1)S(1)} %constant_dynamic-update-slice_fusion.4), channel_id=1, source_target_pairs={{0,12},{4,0},{8,4},{12,8},{1,13},{5,1},{9,5},{13,9},{2,14},{6,2},{... | collective-permute-start | bytes 36872 | tf_op jit(solution)/shard_map/ppermute | solution.py:22
  41.7 19.0 %collective-permute-done.34 = bf16[1,4,1536]{2,1,0:T(4,128)(2,1)S(1)} collective-permute-done((bf16[1,4,1536]{2,1,0:T(4,128)(2,1)S(1)}, bf16[1,4,1536]{2,1,0:T(4,128)(2,1)S(1)}, u32[]{:S(2)}, u32[]{:S(2)}) %collective-permute-start.34) | collective-permute-done | bytes 12320 | tf_op jit(solution)/shard_map/ppermute | solution.py:22
  60.7 11.4 %collective-permute-done.3.refs_4_ = bf16[768,2048]{1,0:T(8,128)(2,1)} collective-permute-done((bf16[768,2048]{1,0:T(8,128)(2,1)}, bf16[768,2048]{1,0:T(8,128)(2,1)}, u32[]{:S(2)}, u32[]{:S(2)}) %collective-permute-start.3) | collective-permute-done | bytes 3145760 | tf_op jit(solution)/shard_map/ppermute | solution.py:27
  72.1 1.8 collective-permute-start.17
  73.9 1.6 collective-permute-start.9
  76.3 2.8 slice.116
  79.0 2.8 slice.117
  82.0 5.6 %collective-permute-done.15.refs_17_ = bf16[2048,128]{1,0:T(8,128)(2,1)} collective-permute-done((bf16[2048,128]{1,0:T(8,128)(2,1)S(1)}, bf16[2048,128]{1,0:T(8,128)(2,1)}, u32[]{:S(2)}, u32[]{:S(2)}) %collective-permute-start.15) | collective-permute-done | bytes 524320 | tf_op jit(solution)/shard_map/ppermute | solution.py:22
  88.1 10.7 %collective-permute-done.17.refs_18_ = bf16[2048,128]{1,0:T(8,128)(2,1)} collective-permute-done((bf16[2048,128]{1,0:T(8,128)(2,1)S(1)}, bf16[2048,128]{1,0:T(8,128)(2,1)}, u32[]{:S(2)}, u32[]{:S(2)}) %collective-permute-start.17) | collective-permute-done | bytes 524320 | tf_op jit(solution)/shard_map/ppermute | solution.py:22
  99.3 7.5 %collective-permute-done.9.refs_19_ = bf16[2048,128]{1,0:T(8,128)(2,1)} collective-permute-done((bf16[2048,128]{1,0:T(8,128)(2,1)S(1)}, bf16[2048,128]{1,0:T(8,128)(2,1)}, u32[]{:S(2)}, u32[]{:S(2)}) %collective-permute-start.9) | collective-permute-done | bytes 524320 | tf_op jit(solution)/shard_map/ppermute | solution.py:22
  112.1 1.4 gather_fusion.1
  114.9 2.5 fusion.42
  117.4 1.6 collective-permute-done.5.refs_6_
  119.0 10.1 %collective-permute-done.7.refs_8_ = bf16[384,2048]{1,0:T(8,128)(2,1)} collective-permute-done((bf16[384,2048]{1,0:T(8,128)(2,1)}, bf16[384,2048]{1,0:T(8,128)(2,1)}, u32[]{:S(2)}, u32[]{:S(2)}) %collective-permute-start.7) | collective-permute-done | bytes 1572896 | tf_op jit(solution)/shard_map/ppermute | solution.py:27
  134.2 1.4 reshape.170
  138.0 4.4 %collective-permute-start.18 = (bf16[2048,128]{1,0:T(8,128)(2,1)}, bf16[2048,128]{1,0:T(8,128)(2,1)S(1)}, u32[]{:S(2)}, u32[]{:S(2)}) collective-permute-start(bf16[2048,128]{1,0:T(8,128)(2,1)} %collective-permute-done.17.refs_18_), channel_id=1, source_target_pairs={{0,4},{4,8},{8,12},{12,0},{1,5},{5,9},{9,13},{13,1},{2,6},{6,10},{... | collective-permute-start | bytes 1572872 | tf_op jit(solution)/shard_map/ppermute | solution.py:22
  147.8 17.7 %project.7.refs_15_ = f32[4,384,768]{2,1,0:T(8,128)} custom-call(s32[4]{0:T(128)S(1)} %pad_add_fusion.2.where_ref, bf16[768,2048]{1,0:T(8,128)(2,1)} %bitcast.2.refs_0_, bf16[768,2048]{1,0:T(8,128)(2,1)} %collective-permute-done.refs_1_, bf16[768,2048]{1,0:T(8,128)(2,1)} %collective-permute-done.1.refs_2_, bf16[768,2048]{1,0:T(8,128)(2,1)} %collective-permute-done.2.refs_3_, ...), custom_call_target="tpu_custom_call" | custom-call | flops 9663676416 | bytes 12582912 | tf_op jit(solution)/shard_map/project/pallas_call | solution.py:171
  165.7 4.3 %collective-permute-start.36 = (bf16[1,4,1024]{2,0,1:T(2,128)(2,1)}, bf16[1,4,1024]{2,0,1:T(2,128)(2,1)S(1)}, u32[]{:S(2)}, u32[]{:S(2)}) collective-permute-start(bf16[1,4,1024]{2,0,1:T(2,128)(2,1)} %get-tuple-element.52), channel_id=1, source_target_pairs={{0,8},{4,12},{8,0},{12,4},{1,9},{5,13},{9,1},{13,5},{2,10},{6,14},... | collective-permute-start | bytes 24584 | tf_op jit(solution)/shard_map/ppermute | solution.py:22
  170.0 6.7 %collective-permute-done.16.refs_12_ = bf16[2048,128]{1,0:T(8,128)(2,1)S(1)} collective-permute-done((bf16[2048,128]{1,0:T(8,128)(2,1)}, bf16[2048,128]{1,0:T(8,128)(2,1)S(1)}, u32[]{:S(2)}, u32[]{:S(2)}) %collective-permute-start.16) | collective-permute-done | bytes 524320 | tf_op jit(solution)/shard_map/ppermute | solution.py:22
  176.7 11.3 %collective-permute-done.18.refs_13_ = bf16[2048,128]{1,0:T(8,128)(2,1)S(1)} collective-permute-done((bf16[2048,128]{1,0:T(8,128)(2,1)}, bf16[2048,128]{1,0:T(8,128)(2,1)S(1)}, u32[]{:S(2)}, u32[]{:S(2)}) %collective-permute-start.18) | collective-permute-done | bytes 524320 | tf_op jit(solution)/shard_map/ppermute | solution.py:22
  188.0 12.0 %project.8 = f32[4,384,768]{2,1,0:T(8,128)} custom-call(s32[2]{0:T(128)S(1)} %pad_add_fusion.where_ref, bf16[768,2048]{1,0:T(8,128)(2,1)} %bitcast.2.refs_0_, bf16[768,2048]{1,0:T(8,128)(2,1)} %collective-permute-done.refs_1_, bf16[768,2048]{1,0:T(8,128)(2,1)} %collective-permute-done.1.refs_2_, bf16[768,2048]{1,0:T(8,128)(2,1)} %collective-permute-done.2.refs_3_, ...), custom_call_target="tpu_custom_call" | custom-call | flops 4831838208 | bytes 6291456 | tf_op jit(solution)/shard_map/project/pallas_call | solution.py:171
  200.0 2.8 slice.120.refs_11_
  202.8 7.6 %collective-permute-done.23.refs_10_ = bf16[2048,256]{1,0:T(8,128)(2,1)S(1)} collective-permute-done((bf16[2048,256]{1,0:T(8,128)(2,1)}, bf16[2048,256]{1,0:T(8,128)(2,1)S(1)}, u32[]{:S(2)}, u32[]{:S(2)}) %collective-permute-start.23) | collective-permute-done | bytes 1048608 | tf_op jit(solution)/shard_map/ppermute | solution.py:22
  210.4 5.3 %project.10 = bf16[4,384,256]{2,1,0:T(8,128)(2,1)S(1)} custom-call(s32[2]{0:T(128)S(1)} %pad_add_fusion.1.where_ref, bf16[768,2048]{1,0:T(8,128)(2,1)} %bitcast.2.refs_0_, bf16[768,2048]{1,0:T(8,128)(2,1)} %collective-permute-done.refs_1_, bf16[768,2048]{1,0:T(8,128)(2,1)} %collective-permute-done.1.refs_2_, ...), custom_call_target="tpu_custom_call" | custom-call | flops 1610612736 | bytes 6291456 | tf_op jit(solution)/shard_map/project/pallas_call | solution.py:171
  216.3 2.2 fusion.35
  218.5 3.8 %collective-permute-done.22.refs_10_ = bf16[2048,128]{1,0:T(8,128)(2,1)S(1)} collective-permute-done((bf16[2048,128]{1,0:T(8,128)(2,1)S(1)}, bf16[2048,128]{1,0:T(8,128)(2,1)S(1)}, u32[]{:S(2)}, u32[]{:S(2)}) %collective-permute-start.22) | collective-permute-done | bytes 524320 | tf_op jit(solution)/shard_map/ppermute | solution.py:22
  222.3 5.0 %project.9 = bf16[4,384,128]{2,1,0:T(8,128)(2,1)S(1)} custom-call(s32[2]{0:T(128)S(1)} %pad_add_fusion.1.where_ref, bf16[768,2048]{1,0:T(8,128)(2,1)} %bitcast.2.refs_0_, bf16[768,2048]{1,0:T(8,128)(2,1)} %collective-permute-done.refs_1_, bf16[768,2048]{1,0:T(8,128)(2,1)} %collective-permute-done.1.refs_2_, ...), custom_call_target="tpu_custom_call" | custom-call | flops 805306368 | bytes 6291456 | tf_op jit(solution)/shard_map/project/pallas_call | solution.py:171
  228.1 3.4 %reward_share.8.so_far_ref = f32[2,8,384]{2,1,0:T(8,128)S(1)} custom-call(s32[1]{0:T(128)S(6)} %select_n.228.kg_ref, bf16[768,128]{1,0:T(8,128)(2,1)S(1)} %bitcast.82, bf16[2,2048,512]{2,1,0:T(8,128)(2,1)S(1)} %copy-done.2, bf16[2,2048,512]{2,1,0:T(8,128)(2,1)S(1)} %copy-done.2, bf16[768,512]{1,0:T(8,128)(2,1)S(1)} %maximum_select_fusion.key_ref.value_ref, ...), custom_call_target="tpu_custom_call" | custom-call | flops 1434451968 | bytes 8388608 | tf_op jit(solution)/shard_map/reward_share/pallas_call | solution.py:280
  231.5 7.4 %collective-permute-done.21.refs_10_ = bf16[2048,128]{1,0:T(8,128)(2,1)S(1)} collective-permute-done((bf16[2048,128]{1,0:T(8,128)(2,1)S(1)}, bf16[2048,128]{1,0:T(8,128)(2,1)S(1)}, u32[]{:S(2)}, u32[]{:S(2)}) %collective-permute-start.21) | collective-permute-done | bytes 524320 | tf_op jit(solution)/shard_map/ppermute | solution.py:22
  239.4 4.7 %project.11 = bf16[4,384,128]{2,1,0:T(8,128)(2,1)S(1)} custom-call(s32[2]{0:T(128)S(1)} %pad_add_fusion.1.where_ref, bf16[768,2048]{1,0:T(8,128)(2,1)} %bitcast.2.refs_0_, bf16[768,2048]{1,0:T(8,128)(2,1)} %collective-permute-done.refs_1_, bf16[768,2048]{1,0:T(8,128)(2,1)} %collective-permute-done.1.refs_2_, ...), custom_call_target="tpu_custom_call" | custom-call | flops 805306368 | bytes 6291456 | tf_op jit(solution)/shard_map/project/pallas_call | solution.py:171
  244.6 3.4 %reward_share.9.so_far_ref = f32[2,8,384]{2,1,0:T(8,128)S(1)} custom-call(s32[1]{0:T(128)S(6)} %select_n.233.kg_ref, bf16[768,128]{1,0:T(8,128)(2,1)S(1)} %collective-permute-done.25.q_ref, bf16[2,2048,512]{2,1,0:T(8,128)(2,1)S(1)} %copy-done.2, bf16[2,2048,512]{2,1,0:T(8,128)(2,1)S(1)} %copy-done.2, ...), custom_call_target="tpu_custom_call" | custom-call | flops 1434451968 | bytes 8388608 | tf_op jit(solution)/shard_map/reward_share/pallas_call | solution.py:280
  248.0 3.4 %reward_share.10.so_far_ref = f32[2,8,384]{2,1,0:T(8,128)S(1)} custom-call(s32[1]{0:T(128)S(6)} %select_n.227.kg_ref, bf16[768,128]{1,0:T(8,128)(2,1)S(1)} %bitcast.84, bf16[2,2048,512]{2,1,0:T(8,128)(2,1)S(1)} %copy-done.2, bf16[2,2048,512]{2,1,0:T(8,128)(2,1)S(1)} %copy-done.2, bf16[768,512]{1,0:T(8,128)(2,1)S(1)} %maximum_select_fusion.key_ref.value_ref, ...), custom_call_target="tpu_custom_call" | custom-call | flops 1434451968 | bytes 8388608 | tf_op jit(solution)/shard_map/reward_share/pallas_call | solution.py:280
  251.4 1.5 collective-permute-start.26
  252.9 4.7 %project.12 = bf16[4,384,128]{2,1,0:T(8,128)(2,1)S(1)} custom-call(s32[2]{0:T(128)S(1)} %pad_add_fusion.1.where_ref, bf16[768,2048]{1,0:T(8,128)(2,1)} %bitcast.2.refs_0_, bf16[768,2048]{1,0:T(8,128)(2,1)} %collective-permute-done.refs_1_, bf16[768,2048]{1,0:T(8,128)(2,1)} %collective-permute-done.1.refs_2_, ...), custom_call_target="tpu_custom_call" | custom-call | flops 805306368 | bytes 6291456 | tf_op jit(solution)/shard_map/project/pallas_call | solution.py:171
  257.7 1.5 collective-permute-start.28
  259.2 3.4 %reward_share.11.so_far_ref = f32[2,8,384]{2,1,0:T(8,128)S(1)} custom-call(s32[1]{0:T(128)S(6)} %select_n.236.kg_ref, bf16[768,128]{1,0:T(8,128)(2,1)S(1)} %collective-permute-done.26.q_ref, bf16[2,2048,512]{2,1,0:T(8,128)(2,1)S(1)} %copy-done.2, bf16[2,2048,512]{2,1,0:T(8,128)(2,1)S(1)} %copy-done.2, ...), custom_call_target="tpu_custom_call" | custom-call | flops 1434451968 | bytes 8388608 | tf_op jit(solution)/shard_map/reward_share/pallas_call | solution.py:280
  262.6 3.4 %reward_share.12.so_far_ref = f32[2,8,384]{2,1,0:T(8,128)S(1)} custom-call(s32[1]{0:T(128)S(6)} %select_n.226.kg_ref, bf16[768,128]{1,0:T(8,128)(2,1)S(1)} %bitcast.85, bf16[2,2048,512]{2,1,0:T(8,128)(2,1)S(1)} %copy-done.2, bf16[2,2048,512]{2,1,0:T(8,128)(2,1)S(1)} %copy-done.2, bf16[768,512]{1,0:T(8,128)(2,1)S(1)} %maximum_select_fusion.key_ref.value_ref, ...), custom_call_target="tpu_custom_call" | custom-call | flops 1434451968 | bytes 8388608 | tf_op jit(solution)/shard_map/reward_share/pallas_call | solution.py:280
  266.0 4.7 %project.13 = bf16[4,384,128]{2,1,0:T(8,128)(2,1)S(1)} custom-call(s32[2]{0:T(128)S(1)} %pad_add_fusion.1.where_ref, bf16[768,2048]{1,0:T(8,128)(2,1)} %bitcast.2.refs_0_, bf16[768,2048]{1,0:T(8,128)(2,1)} %collective-permute-done.refs_1_, bf16[768,2048]{1,0:T(8,128)(2,1)} %collective-permute-done.1.refs_2_, ...), custom_call_target="tpu_custom_call" | custom-call | flops 805306368 | bytes 6291456 | tf_op jit(solution)/shard_map/project/pallas_call | solution.py:171
  271.4 3.3 %reward_share.13.so_far_ref = f32[2,8,384]{2,1,0:T(8,128)S(1)} custom-call(s32[1]{0:T(128)S(6)} %select_n.241.kg_ref, bf16[768,128]{1,0:T(8,128)(2,1)S(1)} %collective-permute-done.28.q_ref, bf16[2,2048,512]{2,1,0:T(8,128)(2,1)S(1)} %copy-done.2, bf16[2,2048,512]{2,1,0:T(8,128)(2,1)S(1)} %copy-done.2, ...), custom_call_target="tpu_custom_call" | custom-call | flops 1434451968 | bytes 8388608 | tf_op jit(solution)/shard_map/reward_share/pallas_call | solution.py:280
  274.8 3.4 %reward_share.14.so_far_ref = f32[2,8,384]{2,1,0:T(8,128)S(1)} custom-call(s32[1]{0:T(128)S(6)} %select_n.239.kg_ref, bf16[768,128]{1,0:T(8,128)(2,1)S(1)} %bitcast.83, bf16[2,2048,512]{2,1,0:T(8,128)(2,1)S(1)} %copy-done.2, bf16[2,2048,512]{2,1,0:T(8,128)(2,1)S(1)} %copy-done.2, bf16[768,512]{1,0:T(8,128)(2,1)S(1)} %maximum_select_fusion.key_ref.value_ref, ...), custom_call_target="tpu_custom_call" | custom-call | flops 1434451968 | bytes 8388608 | tf_op jit(solution)/shard_map/reward_share/pallas_call | solution.py:280
  278.2 3.4 %reward_share.15 = f32[2,8,384]{2,1,0:T(8,128)S(1)} custom-call(s32[1]{0:T(128)S(6)} %select_n.219.kg_ref, bf16[768,128]{1,0:T(8,128)(2,1)S(1)} %collective-permute-done.27.q_ref, bf16[2,2048,512]{2,1,0:T(8,128)(2,1)S(1)} %copy-done.2, bf16[2,2048,512]{2,1,0:T(8,128)(2,1)S(1)} %copy-done.2, bf16[768,512]{1,0:T(8,128)(2,1)S(1)} %maximum_select_fusion.key_ref.value_ref, ...), custom_call_target="tpu_custom_call" | custom-call | flops 1434451968 | bytes 8388608 | tf_op jit(solution)/shard_map/reward_share/pallas_call | solution.py:280
  282.0 1.5 collective-permute-start.31
  (180 shorter events, 34.8 us)
Async XLA Ops:
  0.7 71.5 %collective-permute-start.3 = (bf16[768,2048]{1,0:T(8,128)(2,1)}, bf16[768,2048]{1,0:T(8,128)(2,1)}, u32[]{:S(2)}, u32[]{:S(2)}) collective-permute-start(bf16[768,2048]{1,0:T(8,128)(2,1)} %bitcast.2.refs_0_), channel_id=1, source_target_pairs={{0,16},{16,0},{1,17},{17,1},{2,18},{18,2},{3,19},{19,3},{4,20},{20... | collective-permute-start | bytes 9437192 | tf_op jit(solution)/shard_map/ppermute | solution.py:27
  3.7 70.2 %collective-permute-start.1 = (bf16[768,2048]{1,0:T(8,128)(2,1)}, bf16[768,2048]{1,0:T(8,128)(2,1)}, u32[]{:S(2)}, u32[]{:S(2)}) collective-permute-start(bf16[768,2048]{1,0:T(8,128)(2,1)} %bitcast.2.refs_0_), channel_id=1, source_target_pairs={{0,2},{1,3},{2,0},{3,1},{4,6},{5,7},{6,4},{7,5},{8,10},{9,11},{10,... | collective-permute-start | bytes 9437192 | tf_op jit(solution)/shard_map/ppermute | solution.py:27
  6.6 31.1 %collective-permute-start.32 = (bf16[1,4,1536]{2,1,0:T(4,128)(2,1)S(1)}, bf16[1,4,1536]{2,1,0:T(4,128)(2,1)S(1)}, u32[]{:S(2)}, u32[]{:S(2)}) collective-permute-start(bf16[1,4,1536]{2,1,0:T(4,128)(2,1)S(1)} %constant_dynamic-update-slice_fusion.4), channel_id=1, source_target_pairs={{0,4},{4,8},{8,12},{12,0},{1,5},{5,9},{9,13},{13,1},{2,6},{6,10},{... | collective-permute-start | bytes 36872 | tf_op jit(solution)/shard_map/ppermute | solution.py:22
  8.2 33.5 %collective-permute-start.33 = (bf16[1,4,1536]{2,1,0:T(4,128)(2,1)S(1)}, bf16[1,4,1536]{2,1,0:T(4,128)(2,1)S(1)}, u32[]{:S(2)}, u32[]{:S(2)}) collective-permute-start(bf16[1,4,1536]{2,1,0:T(4,128)(2,1)S(1)} %constant_dynamic-update-slice_fusion.4), channel_id=1, source_target_pairs={{0,8},{4,12},{8,0},{12,4},{1,9},{5,13},{9,1},{13,5},{2,10},{6,14},... | collective-permute-start | bytes 36872 | tf_op jit(solution)/shard_map/ppermute | solution.py:22
  10.9 25.7 %collective-permute-start.11 = (bf16[2048,256]{1,0:T(8,128)(2,1)S(1)}, bf16[2048,256]{1,0:T(8,128)(2,1)}, u32[]{:S(2)}, u32[]{:S(2)}) collective-permute-start(bf16[2048,256]{1,0:T(8,128)(2,1)S(1)} %constant_dynamic-slice_fusion.6.refs_10_), channel_id=1, source_target_pairs={{0,4},{4,8},{8,12},{12,0},{1,5},{5,9},{9,13},{13,1},{2,6},{6,10},{... | collective-permute-start | bytes 3145736 | tf_op jit(solution)/shard_map/ppermute | solution.py:22
  36.6 70.3 %collective-permute-start.12 = (bf16[2048,256]{1,0:T(8,128)(2,1)}, bf16[2048,256]{1,0:T(8,128)(2,1)}, u32[]{:S(2)}, u32[]{:S(2)}) collective-permute-start(bf16[2048,256]{1,0:T(8,128)(2,1)} %collective-permute-done.11.refs_15_), channel_id=1, source_target_pairs={{0,4},{4,8},{8,12},{12,0},{1,5},{5,9},{9,13},{13,1},{2,6},{6,10},{... | collective-permute-start | bytes 3145736 | tf_op jit(solution)/shard_map/ppermute | solution.py:22
  37.1 44.7 %copy-start.9 = (bf16[2048,128]{1,0:T(8,128)(2,1)}, bf16[2048,128]{1,0:T(8,128)(2,1)S(1)}, u32[]{:S(2)}) copy-start(bf16[2048,128]{1,0:T(8,128)(2,1)S(1)} %get-tuple-element.28.refs_13_) | copy-start | bytes 1572868
  37.1 44.7 %copy-start.11 = (bf16[2048,128]{1,0:T(8,128)(2,1)}, bf16[2048,128]{1,0:T(8,128)(2,1)S(1)}, u32[]{:S(2)}) copy-start(bf16[2048,128]{1,0:T(8,128)(2,1)S(1)} %get-tuple-element.29.refs_12_) | copy-start | bytes 1572868
  37.2 44.7 %copy-start.13 = (bf16[2048,128]{1,0:T(8,128)(2,1)}, bf16[2048,128]{1,0:T(8,128)(2,1)S(1)}, u32[]{:S(2)}) copy-start(bf16[2048,128]{1,0:T(8,128)(2,1)S(1)} %get-tuple-element.30.refs_11_) | copy-start | bytes 1572868
  37.2 44.7 %copy-start.15 = (bf16[2048,128]{1,0:T(8,128)(2,1)}, bf16[2048,128]{1,0:T(8,128)(2,1)S(1)}, u32[]{:S(2)}) copy-start(bf16[2048,128]{1,0:T(8,128)(2,1)S(1)} %get-tuple-element.31.refs_14_) | copy-start | bytes 1572868
  37.8 44.1 %copy-start.29 = (bf16[1,4,1536]{2,1,0:T(4,128)(2,1)}, bf16[1,4,1536]{2,1,0:T(4,128)(2,1)S(1)}, u32[]{:S(2)}) copy-start(bf16[1,4,1536]{2,1,0:T(4,128)(2,1)S(1)} %collective-permute-done.32) | copy-start | bytes 36868
  37.8 22.9 %collective-permute-start.34 = (bf16[1,4,1536]{2,1,0:T(4,128)(2,1)S(1)}, bf16[1,4,1536]{2,1,0:T(4,128)(2,1)S(1)}, u32[]{:S(2)}, u32[]{:S(2)}) collective-permute-start(bf16[1,4,1536]{2,1,0:T(4,128)(2,1)S(1)} %constant_dynamic-update-slice_fusion.4), channel_id=1, source_target_pairs={{0,12},{4,0},{8,4},{12,8},{1,13},{5,1},{9,5},{13,9},{2,14},{6,2},{... | collective-permute-start | bytes 36872 | tf_op jit(solution)/shard_map/ppermute | solution.py:22
  41.7 40.2 %copy-start.30 = (bf16[1,4,1536]{2,1,0:T(4,128)(2,1)}, bf16[1,4,1536]{2,1,0:T(4,128)(2,1)S(1)}, u32[]{:S(2)}) copy-start(bf16[1,4,1536]{2,1,0:T(4,128)(2,1)S(1)} %collective-permute-done.33) | copy-start | bytes 36868
  41.7 40.3 %collective-permute-start.13 = (bf16[2048,128]{1,0:T(8,128)(2,1)S(1)}, bf16[2048,128]{1,0:T(8,128)(2,1)}, u32[]{:S(2)}, u32[]{:S(2)}) collective-permute-start(bf16[2048,128]{1,0:T(8,128)(2,1)S(1)} %get-tuple-element.30.refs_11_), channel_id=1, source_target_pairs={{0,4},{4,8},{8,12},{12,0},{1,5},{5,9},{9,13},{13,1},{2,6},{6,10},{... | collective-permute-start | bytes 1572872 | tf_op jit(solution)/shard_map/ppermute | solution.py:22
  60.7 21.2 %copy-start.31 = (bf16[1,4,1536]{2,1,0:T(4,128)(2,1)}, bf16[1,4,1536]{2,1,0:T(4,128)(2,1)S(1)}, u32[]{:S(2)}) copy-start(bf16[1,4,1536]{2,1,0:T(4,128)(2,1)S(1)} %collective-permute-done.34) | copy-start | bytes 36868
  60.7 26.9 %collective-permute-start.15 = (bf16[2048,128]{1,0:T(8,128)(2,1)S(1)}, bf16[2048,128]{1,0:T(8,128)(2,1)}, u32[]{:S(2)}, u32[]{:S(2)}) collective-permute-start(bf16[2048,128]{1,0:T(8,128)(2,1)S(1)} %get-tuple-element.29.refs_12_), channel_id=1, source_target_pairs={{0,4},{4,8},{8,12},{12,0},{1,5},{5,9},{9,13},{13,1},{2,6},{6,10},{... | collective-permute-start | bytes 1572872 | tf_op jit(solution)/shard_map/ppermute | solution.py:22
  72.1 26.7 %collective-permute-start.17 = (bf16[2048,128]{1,0:T(8,128)(2,1)S(1)}, bf16[2048,128]{1,0:T(8,128)(2,1)}, u32[]{:S(2)}, u32[]{:S(2)}) collective-permute-start(bf16[2048,128]{1,0:T(8,128)(2,1)S(1)} %get-tuple-element.28.refs_13_), channel_id=1, source_target_pairs={{0,4},{4,8},{8,12},{12,0},{1,5},{5,9},{9,13},{13,1},{2,6},{6,10},{... | collective-permute-start | bytes 1572872 | tf_op jit(solution)/shard_map/ppermute | solution.py:22
  73.9 32.9 %collective-permute-start.9 = (bf16[2048,128]{1,0:T(8,128)(2,1)S(1)}, bf16[2048,128]{1,0:T(8,128)(2,1)}, u32[]{:S(2)}, u32[]{:S(2)}) collective-permute-start(bf16[2048,128]{1,0:T(8,128)(2,1)S(1)} %get-tuple-element.31.refs_14_), channel_id=1, source_target_pairs={{0,4},{4,8},{8,12},{12,0},{1,5},{5,9},{9,13},{13,1},{2,6},{6,10},{... | collective-permute-start | bytes 1572872 | tf_op jit(solution)/shard_map/ppermute | solution.py:22
  79.0 28.5 %copy-start.21 = (bf16[8,128,128]{2,1,0:T(8,128)(2,1)S(1)}, bf16[8,128,128]{2,1,0:T(8,128)(2,1)}, u32[]{:S(2)}) copy-start(bf16[8,128,128]{2,1,0:T(8,128)(2,1)} %copy-done.20) | copy-start | bytes 786436
  79.0 28.5 %copy-start.23 = (bf16[8,128,128]{2,1,0:T(8,128)(2,1)S(1)}, bf16[8,128,128]{2,1,0:T(8,128)(2,1)}, u32[]{:S(2)}) copy-start(bf16[8,128,128]{2,1,0:T(8,128)(2,1)} %copy-done.22) | copy-start | bytes 786436
  81.9 55.4 %collective-permute-start = (bf16[768,2048]{1,0:T(8,128)(2,1)}, bf16[768,2048]{1,0:T(8,128)(2,1)}, u32[]{:S(2)}, u32[]{:S(2)}) collective-permute-start(bf16[768,2048]{1,0:T(8,128)(2,1)} %bitcast.2.refs_0_), channel_id=1, source_target_pairs={{0,1},{1,0},{2,3},{3,2},{4,5},{5,4},{6,7},{7,6},{8,9},{9,8},{10,11... | collective-permute-start | bytes 9437192 | tf_op jit(solution)/shard_map/ppermute | solution.py:27
  87.6 31.4 %collective-permute-start.5 = (bf16[384,2048]{1,0:T(8,128)(2,1)}, bf16[384,2048]{1,0:T(8,128)(2,1)S(1)}, u32[]{:S(2)}, u32[]{:S(2)}) collective-permute-start(bf16[384,2048]{1,0:T(8,128)(2,1)} %slice.116), channel_id=1, source_target_pairs={{0,2},{1,3},{2,0},{3,1},{4,6},{5,7},{6,4},{7,5},{8,10},{9,11},{10,... | collective-permute-start | bytes 4718600 | tf_op jit(solution)/shard_map/ppermute | solution.py:27
  98.8 30.3 %collective-permute-start.7 = (bf16[384,2048]{1,0:T(8,128)(2,1)}, bf16[384,2048]{1,0:T(8,128)(2,1)}, u32[]{:S(2)}, u32[]{:S(2)}) collective-permute-start(bf16[384,2048]{1,0:T(8,128)(2,1)} %slice.117), channel_id=1, source_target_pairs={{0,16},{16,0},{1,17},{17,1},{2,18},{18,2},{3,19},{19,3},{4,20},{20... | collective-permute-start | bytes 4718600 | tf_op jit(solution)/shard_map/ppermute | solution.py:27
  106.8 31.1 %collective-permute-start.2 = (bf16[768,2048]{1,0:T(8,128)(2,1)}, bf16[768,2048]{1,0:T(8,128)(2,1)}, u32[]{:S(2)}, u32[]{:S(2)}) collective-permute-start(bf16[768,2048]{1,0:T(8,128)(2,1)} %collective-permute-done.1.refs_2_), channel_id=1, source_target_pairs={{0,1},{1,0},{2,3},{3,2},{4,5},{5,4},{6,7},{7,6},{8,9},{9,8},{10,11... | collective-permute-start | bytes 9437192 | tf_op jit(solution)/shard_map/ppermute | solution.py:27
  106.8 35.5 %collective-permute-start.4 = (bf16[768,2048]{1,0:T(8,128)(2,1)}, bf16[768,2048]{1,0:T(8,128)(2,1)}, u32[]{:S(2)}, u32[]{:S(2)}) collective-permute-start(bf16[768,2048]{1,0:T(8,128)(2,1)} %collective-permute-done.3.refs_4_), channel_id=1, source_target_pairs={{0,1},{1,0},{2,3},{3,2},{4,5},{5,4},{6,7},{7,6},{8,9},{9,8},{10,11... | collective-permute-start | bytes 9437192 | tf_op jit(solution)/shard_map/ppermute | solution.py:27
  119.0 18.4 %collective-permute-start.6 = (bf16[384,2048]{1,0:T(8,128)(2,1)S(1)}, bf16[384,2048]{1,0:T(8,128)(2,1)S(1)}, u32[]{:S(2)}, u32[]{:S(2)}) collective-permute-start(bf16[384,2048]{1,0:T(8,128)(2,1)S(1)} %collective-permute-done.5.refs_6_), channel_id=1, source_target_pairs={{0,1},{1,0},{2,3},{3,2},{4,5},{5,4},{6,7},{7,6},{8,9},{9,8},{10,11... | collective-permute-start | bytes 4718600 | tf_op jit(solution)/shard_map/ppermute | solution.py:27
  129.1 8.4 %collective-permute-start.8 = (bf16[384,2048]{1,0:T(8,128)(2,1)}, bf16[384,2048]{1,0:T(8,128)(2,1)}, u32[]{:S(2)}, u32[]{:S(2)}) collective-permute-start(bf16[384,2048]{1,0:T(8,128)(2,1)} %collective-permute-done.7.refs_8_), channel_id=1, source_target_pairs={{0,1},{1,0},{2,3},{3,2},{4,5},{5,4},{6,7},{7,6},{8,9},{9,8},{10,11... | collective-permute-start | bytes 4718600 | tf_op jit(solution)/shard_map/ppermute | solution.py:27
  137.4 50.6 %copy-start.4 = (bf16[384,2048]{1,0:T(8,128)(2,1)S(1)}, bf16[384,2048]{1,0:T(8,128)(2,1)}, u32[]{:S(2)}) copy-start(bf16[384,2048]{1,0:T(8,128)(2,1)} %copy-done.3) | copy-start | bytes 4718596
  137.4 28.2 %collective-permute-start.10 = (bf16[2048,128]{1,0:T(8,128)(2,1)}, bf16[2048,128]{1,0:T(8,128)(2,1)S(1)}, u32[]{:S(2)}, u32[]{:S(2)}) collective-permute-start(bf16[2048,128]{1,0:T(8,128)(2,1)} %collective-permute-done.9.refs_19_), channel_id=1, source_target_pairs={{0,4},{4,8},{8,12},{12,0},{1,5},{5,9},{9,13},{13,1},{2,6},{6,10},{... | collective-permute-start | bytes 1572872 | tf_op jit(solution)/shard_map/ppermute | solution.py:22
  137.4 28.3 %collective-permute-start.14 = (bf16[2048,128]{1,0:T(8,128)(2,1)}, bf16[2048,128]{1,0:T(8,128)(2,1)S(1)}, u32[]{:S(2)}, u32[]{:S(2)}) collective-permute-start(bf16[2048,128]{1,0:T(8,128)(2,1)} %collective-permute-done.13.refs_16_), channel_id=1, source_target_pairs={{0,4},{4,8},{8,12},{12,0},{1,5},{5,9},{9,13},{13,1},{2,6},{6,10},{... | collective-permute-start | bytes 1572872 | tf_op jit(solution)/shard_map/ppermute | solution.py:22
  137.5 39.2 %collective-permute-start.16 = (bf16[2048,128]{1,0:T(8,128)(2,1)}, bf16[2048,128]{1,0:T(8,128)(2,1)S(1)}, u32[]{:S(2)}, u32[]{:S(2)}) collective-permute-start(bf16[2048,128]{1,0:T(8,128)(2,1)} %collective-permute-done.15.refs_17_), channel_id=1, source_target_pairs={{0,4},{4,8},{8,12},{12,0},{1,5},{5,9},{9,13},{13,1},{2,6},{6,10},{... | collective-permute-start | bytes 1572872 | tf_op jit(solution)/shard_map/ppermute | solution.py:22
  138.0 50.0 %collective-permute-start.18 = (bf16[2048,128]{1,0:T(8,128)(2,1)}, bf16[2048,128]{1,0:T(8,128)(2,1)S(1)}, u32[]{:S(2)}, u32[]{:S(2)}) collective-permute-start(bf16[2048,128]{1,0:T(8,128)(2,1)} %collective-permute-done.17.refs_18_), channel_id=1, source_target_pairs={{0,4},{4,8},{8,12},{12,0},{1,5},{5,9},{9,13},{13,1},{2,6},{6,10},{... | collective-permute-start | bytes 1572872 | tf_op jit(solution)/shard_map/ppermute | solution.py:22
  142.4 68.0 %collective-permute-start.23 = (bf16[2048,256]{1,0:T(8,128)(2,1)}, bf16[2048,256]{1,0:T(8,128)(2,1)S(1)}, u32[]{:S(2)}, u32[]{:S(2)}) collective-permute-start(bf16[2048,256]{1,0:T(8,128)(2,1)} %collective-permute-done.12.refs_10_), channel_id=1, source_target_pairs={{0,4},{4,8},{8,12},{12,0},{1,5},{5,9},{9,13},{13,1},{2,6},{6,10},{... | collective-permute-start | bytes 3145736 | tf_op jit(solution)/shard_map/ppermute | solution.py:22
  165.6 116.4 %collective-permute-start.35 = (bf16[1,4,1024]{2,0,1:T(2,128)(2,1)}, bf16[1,4,1024]{2,0,1:T(2,128)(2,1)S(1)}, u32[]{:S(2)}, u32[]{:S(2)}) collective-permute-start(bf16[1,4,1024]{2,0,1:T(2,128)(2,1)} %get-tuple-element.50), channel_id=1, source_target_pairs={{0,4},{4,8},{8,12},{12,0},{1,5},{5,9},{9,13},{13,1},{2,6},{6,10},{... | collective-permute-start | bytes 24584 | tf_op jit(solution)/shard_map/ppermute | solution.py:22
  165.7 117.9 %collective-permute-start.36 = (bf16[1,4,1024]{2,0,1:T(2,128)(2,1)}, bf16[1,4,1024]{2,0,1:T(2,128)(2,1)S(1)}, u32[]{:S(2)}, u32[]{:S(2)}) collective-permute-start(bf16[1,4,1024]{2,0,1:T(2,128)(2,1)} %get-tuple-element.52), channel_id=1, source_target_pairs={{0,8},{4,12},{8,0},{12,4},{1,9},{5,13},{9,1},{13,5},{2,10},{6,14},... | collective-permute-start | bytes 24584 | tf_op jit(solution)/shard_map/ppermute | solution.py:22
  176.7 106.9 %collective-permute-start.37 = (bf16[1,4,1024]{2,0,1:T(2,128)(2,1)}, bf16[1,4,1024]{2,0,1:T(2,128)(2,1)S(1)}, u32[]{:S(2)}, u32[]{:S(2)}) collective-permute-start(bf16[1,4,1024]{2,0,1:T(2,128)(2,1)} %get-tuple-element.51), channel_id=1, source_target_pairs={{0,12},{4,0},{8,4},{12,8},{1,13},{5,1},{9,5},{13,9},{2,14},{6,2},{... | collective-permute-start | bytes 24584 | tf_op jit(solution)/shard_map/ppermute | solution.py:22
  188.0 34.3 %collective-permute-start.22 = (bf16[2048,128]{1,0:T(8,128)(2,1)S(1)}, bf16[2048,128]{1,0:T(8,128)(2,1)S(1)}, u32[]{:S(2)}, u32[]{:S(2)}) collective-permute-start(bf16[2048,128]{1,0:T(8,128)(2,1)S(1)} %collective-permute-done.14.refs_11_), channel_id=1, source_target_pairs={{0,4},{4,8},{8,12},{12,0},{1,5},{5,9},{9,13},{13,1},{2,6},{6,10},{... | collective-permute-start | bytes 1572872 | tf_op jit(solution)/shard_map/ppermute | solution.py:22
  215.7 11.6 %collective-permute-start.24 = (bf16[768,256]{1,0:T(8,128)(2,1)S(1)}, bf16[768,256]{1,0:T(8,128)(2,1)S(1)}, u32[]{:S(2)}, u32[]{:S(2)}) collective-permute-start(bf16[768,256]{1,0:T(8,128)(2,1)S(1)} %bitcast.87), channel_id=1, source_target_pairs={{0,16},{16,0},{1,17},{17,1},{2,18},{18,2},{3,19},{19,3},{4,20},{20... | collective-permute-start | bytes 1179656 | tf_op jit(solution)/shard_map/ppermute | solution.py:27
  222.3 16.6 %collective-permute-start.21 = (bf16[2048,128]{1,0:T(8,128)(2,1)S(1)}, bf16[2048,128]{1,0:T(8,128)(2,1)S(1)}, u32[]{:S(2)}, u32[]{:S(2)}) collective-permute-start(bf16[2048,128]{1,0:T(8,128)(2,1)S(1)} %collective-permute-done.16.refs_12_), channel_id=1, source_target_pairs={{0,4},{4,8},{8,12},{12,0},{1,5},{5,9},{9,13},{13,1},{2,6},{6,10},{... | collective-permute-start | bytes 1572872 | tf_op jit(solution)/shard_map/ppermute | solution.py:22
  227.4 24.0 %collective-permute-start.20 = (bf16[2048,128]{1,0:T(8,128)(2,1)S(1)}, bf16[2048,128]{1,0:T(8,128)(2,1)S(1)}, u32[]{:S(2)}, u32[]{:S(2)}) collective-permute-start(bf16[2048,128]{1,0:T(8,128)(2,1)S(1)} %collective-permute-done.18.refs_13_), channel_id=1, source_target_pairs={{0,4},{4,8},{8,12},{12,0},{1,5},{5,9},{9,13},{13,1},{2,6},{6,10},{... | collective-permute-start | bytes 1572872 | tf_op jit(solution)/shard_map/ppermute | solution.py:22
  238.9 5.7 %collective-permute-start.25 = (bf16[768,128]{1,0:T(8,128)(2,1)S(1)}, bf16[768,128]{1,0:T(8,128)(2,1)S(1)}, u32[]{:S(2)}, u32[]{:S(2)}) collective-permute-start(bf16[768,128]{1,0:T(8,128)(2,1)S(1)} %bitcast.89), channel_id=1, source_target_pairs={{0,16},{16,0},{1,17},{17,1},{2,18},{18,2},{3,19},{19,3},{4,20},{20... | collective-permute-start | bytes 589832 | tf_op jit(solution)/shard_map/ppermute | solution.py:27
  244.6 21.4 %collective-permute-start.19 = (bf16[2048,128]{1,0:T(8,128)(2,1)S(1)}, bf16[2048,128]{1,0:T(8,128)(2,1)S(1)}, u32[]{:S(2)}, u32[]{:S(2)}) collective-permute-start(bf16[2048,128]{1,0:T(8,128)(2,1)S(1)} %collective-permute-done.10.refs_14_), channel_id=1, source_target_pairs={{0,4},{4,8},{8,12},{12,0},{1,5},{5,9},{9,13},{13,1},{2,6},{6,10},{... | collective-permute-start | bytes 1572872 | tf_op jit(solution)/shard_map/ppermute | solution.py:22
  251.4 6.3 %collective-permute-start.26 = (bf16[768,128]{1,0:T(8,128)(2,1)S(1)}, bf16[768,128]{1,0:T(8,128)(2,1)S(1)}, u32[]{:S(2)}, u32[]{:S(2)}) collective-permute-start(bf16[768,128]{1,0:T(8,128)(2,1)S(1)} %bitcast.90), channel_id=1, source_target_pairs={{0,16},{16,0},{1,17},{17,1},{2,18},{18,2},{3,19},{19,3},{4,20},{20... | collective-permute-start | bytes 589832 | tf_op jit(solution)/shard_map/ppermute | solution.py:27
  257.7 13.1 %collective-permute-start.28 = (bf16[768,128]{1,0:T(8,128)(2,1)S(1)}, bf16[768,128]{1,0:T(8,128)(2,1)S(1)}, u32[]{:S(2)}, u32[]{:S(2)}) collective-permute-start(bf16[768,128]{1,0:T(8,128)(2,1)S(1)} %bitcast.88), channel_id=1, source_target_pairs={{0,16},{16,0},{1,17},{17,1},{2,18},{18,2},{3,19},{19,3},{4,20},{20... | collective-permute-start | bytes 589832 | tf_op jit(solution)/shard_map/ppermute | solution.py:27
  270.8 7.4 %collective-permute-start.27 = (bf16[768,128]{1,0:T(8,128)(2,1)S(1)}, bf16[768,128]{1,0:T(8,128)(2,1)S(1)}, u32[]{:S(2)}, u32[]{:S(2)}) collective-permute-start(bf16[768,128]{1,0:T(8,128)(2,1)S(1)} %bitcast.91), channel_id=1, source_target_pairs={{0,16},{16,0},{1,17},{17,1},{2,18},{18,2},{3,19},{19,3},{4,20},{20... | collective-permute-start | bytes 589832 | tf_op jit(solution)/shard_map/ppermute | solution.py:27
  281.6 2.6 collective-permute-start.29
  281.7 3.7 %collective-permute-start.30 = (f32[2,384]{1,0:T(2,128)S(1)}, f32[2,384]{1,0:T(2,128)S(1)}, u32[]{:S(2)}, u32[]{:S(2)}) collective-permute-start(f32[2,384]{1,0:T(2,128)S(1)} %bitcast.96), channel_id=1, source_target_pairs={{0,2},{1,3},{2,0},{3,1},{4,6},{5,7},{6,4},{7,5},{8,10},{9,11},{10,... | collective-permute-start | bytes 9224 | tf_op jit(solution)/shard_map/ppermute | solution.py:27
  282.0 3.3 %collective-permute-start.31 = (f32[2,384]{1,0:T(2,128)S(1)}, f32[2,384]{1,0:T(2,128)S(1)}, u32[]{:S(2)}, u32[]{:S(2)}) collective-permute-start(f32[2,384]{1,0:T(2,128)S(1)} %bitcast.97), channel_id=1, source_target_pairs={{0,3},{1,2},{2,1},{3,0},{4,7},{5,6},{6,5},{7,4},{8,11},{9,10},{10,... | collective-permute-start | bytes 9224 | tf_op jit(solution)/shard_map/ppermute | solution.py:27
  (28 other events, 197.5 us)
where the time goes:
time: 287 us; the launch traced here: 286 us
  waiting for transfers between devices  119 us (41%)
  Pallas kernels  81.1 us (28%)
  local copies, waits for them, and re-layouts  38 us (13%)
  starting transfers between devices  34 us (12%)
  other arithmetic  6.31 us (2%)
  matrix products  6.16 us (2%)
    ppermute x21, waiting for transfers between devices, shifted(): lax.ppermute(value, axis, [(i, (i + step) % size) for i in range(size)])  94.2 us
    pallas_call x7, Pallas kernels, project(): pl.pallas_call(functools.partial(project_kernel, plan), grid_spec=pltpu.P...  54.1 us
    pallas_call x8, Pallas kernels, reward_share(): pl.pallas_call(reward_kernel, grid_spec=spec, out_shape=jax.ShapeDtypeStr...  27 us
    ppermute x17, waiting for transfers between devices, partner(): return lax.ppermute(value, axis, [(i, i ^ bits) for i in range(size)])  24.7 us
    ppermute x21, starting transfers between devices, shifted(): lax.ppermute(value, axis, [(i, (i + step) % size) for i in range(size)])  21.2 us
    ppermute x17, starting transfers between devices, partner(): return lax.ppermute(value, axis, [(i, i ^ bits) for i in range(size)])  12.8 us
    unnamed x79, local copies, waits for them, and re-layouts  8.88 us
    slice x1, local copies, waits for them, and re-layouts, policy(): stored[..., :HD]  6.19 us
  transfers between devices with their start and end apart: 38, of which 15 were waited for; matrix products, arithmetic and copies ran while one was open for 15% of the time, Pallas kernels for 28%

commit v1 on v0

v1 whole, which is shorter than its diff:
```python
import functools
import math

import jax
import jax.numpy as jnp
from jax import lax
from jax.experimental import pallas as pl
from jax.experimental.pallas import tpu as pltpu
from jax.sharding import PartitionSpec as P

HD = 128
masked_value = -1e30
bf16, f32 = jnp.bfloat16, jnp.float32


def touch(arrays):
    anywhere = pl.BlockSpec(memory_space=pl.ANY)
    return pl.pallas_call(
        lambda *refs: None,
        in_specs=[anywhere] * len(arrays),
        out_specs=[anywhere] * len(arrays),
        out_shape=[jax.ShapeDtypeStruct(v.shape, v.dtype) for v in arrays],
        input_output_aliases={i: i for i in range(len(arrays))},
        compiler_params=pltpu.CompilerParams(vmem_limit_bytes=60 * 1024 * 1024),
        cost_estimate=pl.CostEstimate(flops=0, bytes_accessed=0, transcendentals=0),
        name="touch",
    )(*arrays)


def shifted(value, axis, step):
    size = lax.axis_size(axis)
    return lax.ppermute(value, axis, [(i, (i + step) % size) for i in range(size)])


def partner(value, axis, bits):
    size = lax.axis_size(axis)
    return lax.ppermute(value, axis, [(i, i ^ bits) for i in range(size)])


def project_kernel(plan, where_ref, *refs):
    sources, cands, blocks, widths, begin, has_sum = plan
    arrays, refs = refs[:sources], refs[sources:]
    weights, refs = refs[: blocks * len(widths)], refs[blocks * len(widths) :]
    before, refs = (refs[0], refs[1:]) if has_sum else (None, refs)
    out, tile_buf, weight_buf, sum_buf, tile_sem, weight_sem, sum_sem = refs
    slots, tile_rows, depth = tile_buf.shape
    columns = sum_buf.shape[2]
    steps = cands * blocks

    def load(item):
        block, tile = item // cands, item % cands
        off, column = where_ref[2 * block], where_ref[2 * block + 1]
        column = pl.multiple_of(column, depth)
        slot = lax.rem(item, slots)
        for i in range(sources):

            @pl.when(off == i)
            def _():
                pltpu.make_async_copy(
                    arrays[i].at[tile, :, pl.ds(column, depth)], tile_buf.at[slot], tile_sem.at[slot]
                ).start()

    copies = []
    for block in range(blocks):
        at = 0
        for j, width in enumerate(widths):
            number = block * len(widths) + j
            copies.append(
                pltpu.make_async_copy(
                    weights[number].at[0:depth, :],
                    weight_buf.at[block, :, at : at + width],
                    weight_sem.at[number],
                )
            )
            at += width
    first = len(widths)
    for copy in copies[:first]:
        copy.start()
    for item in range(min(slots - 1, steps)):
        load(item)
    if has_sum:
        columns_of = before.at[:, :, begin : begin + columns]
        copies.append(pltpu.make_async_copy(columns_of, sum_buf, sum_sem))
    for copy in copies[first:]:
        copy.start()
    for copy in copies:
        copy.wait()

    def step(item, _):
        @pl.when(item + slots - 1 < steps)
        def _():
            load(item + slots - 1)

        slot = lax.rem(item, slots)
        block, tile = item // cands, item % cands
        pltpu.make_async_copy(
            arrays[0].at[0, :, pl.ds(0, depth)], tile_buf.at[slot], tile_sem.at[slot]
        ).wait()
        term = jnp.dot(tile_buf[slot], weight_buf[block], preferred_element_type=f32)
        if has_sum:
            term = term + sum_buf[tile]
        else:
            term = jnp.where(block > 0, term + sum_buf[tile], term)
        if blocks > 1:
            sum_buf[tile] = term

        @pl.when(block == blocks - 1)
        def _():
            out[tile] = term.astype(out.dtype)

        return 0

    lax.fori_loop(0, steps, step, 0)


def project(pieces, numbers, depth, weights, before, begin, final):
    here = lax.axis_index("tensor")
    cands, tile_rows, width = pieces[0].shape
    blocks = len(weights)
    widths = [w.shape[1] for w in weights[0]]
    columns = sum(widths)
    per_piece = width // depth
    where = []
    for number in numbers:
        where += [(number // per_piece) ^ here, number % per_piece * depth]
    where = jnp.stack(where).astype(jnp.int32)
    flat = [w for block in weights for w in block]
    operands = list(pieces) + flat + ([] if before is None else [before])
    plan = (len(pieces), cands, blocks, widths, begin, before is not None)
    slots = 3
    return pl.pallas_call(
        functools.partial(project_kernel, plan),
        in_specs=[pl.BlockSpec(memory_space=pltpu.SMEM)]
        + [pl.BlockSpec(memory_space=pl.ANY)] * len(operands),
        out_specs=pl.BlockSpec(memory_space=pltpu.VMEM),
        out_shape=jax.ShapeDtypeStruct((cands, tile_rows, columns), bf16 if final else f32),
        scratch_shapes=[
            pltpu.VMEM((slots, tile_rows, depth), bf16),
            pltpu.VMEM((blocks, depth, columns), bf16),
            pltpu.VMEM((cands, tile_rows, columns), f32),
            pltpu.SemaphoreType.DMA((slots,)),
            pltpu.SemaphoreType.DMA((len(flat),)),
            pltpu.SemaphoreType.DMA,
        ],
        compiler_params=pltpu.CompilerParams(vmem_limit_bytes=60 * 1024 * 1024),
        cost_estimate=pl.CostEstimate(
            flops=2 * cands * tile_rows * depth * blocks * columns,
            bytes_accessed=2 * cands * tile_rows * depth * blocks,
            transcendentals=0,
        ),
        name="project",
    )(where, *operands)


def reward_kernel(kg_ref, q_ref, old_key_ref, old_value_ref, key_ref, value_ref, grade_ref, so_far_ref, out_ref):
    span = q_ref.shape[0]
    context = old_key_ref.shape[1]
    rate = HD**-0.5 * math.log2(math.e)
    queries = q_ref[...]
    grade = grade_ref[0]
    block = math.gcd(HD, context)
    peak = jnp.full((8, span), -jnp.inf, f32)
    total = jnp.zeros((8, span), f32)
    graded = jnp.zeros((8, span), f32)
    places = [(old_key_ref.at[0], old_value_ref.at[0], i) for i in range(0, context, block)]
    places += [(key_ref, value_ref, i) for i in range(0, span, block)]

    def products(keys, values, start):
        scores = lax.dot_general(
            keys[start : start + block, :],
            queries,
            (((1,), (1,)), ((), ())),
            preferred_element_type=f32,
        )
        worth = jnp.dot(values[start : start + block, :], grade, preferred_element_type=f32)
        worth = worth[:, :HD] + worth[:, HD:]
        if keys is key_ref:
            shape = (block, span)
            visible = start + lax.broadcasted_iota(jnp.int32, shape, 0) <= (
                lax.broadcasted_iota(jnp.int32, shape, 1)
            )
            scores = jnp.where(visible, scores, masked_value)
        return scores.reshape(block // 8, 8, span), worth.reshape(block // 8, 8, HD)

    coming = products(*places[0])
    for number in range(len(places)):
        scores, worth = coming
        if number + 1 < len(places):
            coming = products(*places[number + 1])
        new_peak = jnp.maximum(peak, jnp.max(scores, axis=0))
        fade = jnp.exp2((peak - new_peak) * rate)
        weights = jnp.exp2((scores - new_peak[None]) * rate)
        total = total * fade + jnp.sum(weights, axis=0)
        worth = jnp.concatenate([worth] * (span // HD), axis=2)
        graded = graded * fade + jnp.sum(weights * worth, axis=0)
        peak = new_peak
    top = jnp.max(peak, axis=0, keepdims=True)
    fade = jnp.exp2((peak - top) * rate)
    total = jnp.sum(total * fade, axis=0, keepdims=True)
    graded = jnp.sum(graded * fade, axis=0, keepdims=True)
    result = jnp.broadcast_to(graded / total, (8, span))

    @pl.when(pl.program_id(1) == 0)
    def _():
        out_ref[0] = so_far_ref[0] + result

    @pl.when(pl.program_id(1) != 0)
    def _():
        out_ref[0] += result


def grading_columns(grading):
    high = lax.reduce_precision(grading, 8, 7)
    parts = []
    for part in (high, grading - high):
        part = part.astype(bf16).reshape(-1, HD)
        parts.append(jnp.broadcast_to(part[:, :, None], (part.shape[0], HD, HD)))
    return jnp.concatenate(parts, axis=2)


def reward_share(queries, first_block, numbers, stored, per_group, fresh, fresh_block, grades, so_far):
    cands, context, _ = stored.shape
    span = queries.shape[0] // cands
    heads = len(numbers)
    scalars = []
    for number in numbers:
        pair = number // per_group
        scalars += [number, 2 * pair, fresh_block(2 * pair), fresh_block(2 * pair + 1)]
    scalars = jnp.stack(scalars).astype(jnp.int32)
    spec = pltpu.PrefetchScalarGridSpec(
        num_scalar_prefetch=1,
        grid=(cands, heads),
        in_specs=[
            pl.BlockSpec((span, HD), lambda c, h, n: (c, first_block + h)),
            pl.BlockSpec((1, context, HD), lambda c, h, n: (c, 0, n[4 * h + 1])),
            pl.BlockSpec((1, context, HD), lambda c, h, n: (c, 0, n[4 * h + 1] + 1)),
            pl.BlockSpec((span, HD), lambda c, h, n: (c, n[4 * h + 2])),
            pl.BlockSpec((span, HD), lambda c, h, n: (c, n[4 * h + 3])),
            pl.BlockSpec((1, HD, 2 * HD), lambda c, h, n: (n[4 * h], 0, 0)),
            pl.BlockSpec((1, 8, span), lambda c, h, n: (c, 0, 0)),
        ],
        out_specs=pl.BlockSpec((1, 8, span), lambda c, h, n: (c, 0, 0)),
    )
    cells = cands * heads * span * (context + span)
    return pl.pallas_call(
        reward_kernel,
        grid_spec=spec,
        out_shape=jax.ShapeDtypeStruct((cands, 8, span), f32),
        compiler_params=pltpu.CompilerParams(vmem_limit_bytes=60 * 1024 * 1024),
        cost_estimate=pl.CostEstimate(
            flops=6 * HD * cells, bytes_accessed=4 * stored.size, transcendentals=cells
        ),
        name="reward_share",
    )(scalars, queries, stored, stored, fresh, fresh, grades, so_far)


def send_slots(placed, slots_here):
    devices = lax.axis_size("cand")
    here = lax.axis_index("cand")
    bit = devices // 2
    while bit:
        half = bit * slots_here
        low = (here & bit) == 0
        first, second = placed[:half], placed[half:]
        new = partner(jnp.where(low, second, first), "cand", bit)
        placed = jnp.where(low, first, second) + new
        bit //= 2
    return placed


def policy_rows(stored, extents, kept, everyone):
    cand_here = stored.shape[0]
    device_here = lax.axis_index("cand")
    key_scale = HD ** (-0.5)
    lane_number = kept.shape[0]
    new_count = everyone.shape[1]
    kv_here = stored.shape[2]
    policy_heads = everyone.shape[2] // HD - 2 * kv_here
    policy_group = policy_heads // kv_here
    cache_len = stored.shape[1]
    causal_new = lax.broadcasted_iota(jnp.int32, (new_count, new_count), 0) >= lax.broadcasted_iota(
        jnp.int32, (new_count, new_count), 1
    )
    ids_here = device_here * cand_here + lax.broadcasted_iota(jnp.int32, (cand_here,), 0)
    matched = kept[None, :] == ids_here[:, None]
    slot_index = jnp.sum(
        jnp.where(matched, lax.broadcasted_iota(jnp.int32, (cand_here, lane_number), 1), 0), axis=1
    )
    chosen = jnp.take(everyone, slot_index, axis=0)
    own_queries = chosen[:, :, : policy_heads * HD].reshape(
        cand_here, new_count, kv_here, policy_group, HD
    )
    own_fresh = chosen[:, :, policy_heads * HD :].reshape(cand_here, new_count, kv_here, 2 * HD)
    living = lax.broadcasted_iota(jnp.int32, (cand_here, cache_len), 1)
    living = living < jnp.take(extents, ids_here)[:, None]
    living = living[:, None, None, None, :]
    scores = (
        jnp.einsum("cikgd,ctkd->ckgit", own_queries, stored[..., :HD], preferred_element_type=f32)
        * key_scale
    )
    scores = jnp.where(living, scores, masked_value)
    fresh_scores = (
        jnp.einsum("cikgd,cjkd->ckgij", own_queries, own_fresh[..., :HD], preferred_element_type=f32)
        * key_scale
    )
    fresh_scores = jnp.where(causal_new, fresh_scores, masked_value)
    peak_score = jnp.maximum(jnp.max(scores, axis=-1), jnp.max(fresh_scores, axis=-1))
    old_weights = jnp.where(living, jnp.exp(scores - peak_score[..., None]), 0.0)
    fresh_weights = jnp.where(causal_new, jnp.exp(fresh_scores - peak_score[..., None]), 0.0)
    denominator = jnp.sum(old_weights, axis=-1) + jnp.sum(fresh_weights, axis=-1)
    numerator = jnp.einsum(
        "ckgit,ctkd->ckgid", old_weights, stored[..., HD:], preferred_element_type=f32
    )
    numerator = numerator + jnp.einsum(
        "ckgij,cjkd->ckgid", fresh_weights, own_fresh[..., HD:], preferred_element_type=f32
    )
    result = numerator / denominator[..., None]
    flattened = jnp.transpose(result, (0, 3, 1, 2, 4)).reshape(
        cand_here, new_count * policy_heads * HD
    )
    placed = jnp.einsum(
        "cs,cx->sx", matched.astype(f32), flattened, precision=lax.Precision.HIGHEST
    )
    return placed.reshape(lane_number, new_count, policy_heads * HD).astype(bf16)


def local(
    response_latest_embeddings,
    critic_probe_projector,
    critic_pair_projector,
    critic_stored_pairs,
    critic_grading_vector,
    actor_stored_pairs,
    filled_extents,
    kept_responses,
    actor_latest_probes,
    actor_latest_pairs,
):
    cand_here, span_len, _ = response_latest_embeddings.shape
    rows = cand_here * span_len
    devices = lax.axis_size("cand")
    group = lax.axis_index("groups")
    place = lax.axis_index("cand")
    depth, query_cols = critic_probe_projector.shape
    keyval_cols = critic_pair_projector.shape[1]
    heads_here = query_cols // HD
    per_group = heads_here // (keyval_cols // (2 * HD))
    query_half, keyval_half = query_cols // 2, keyval_cols // 2

    heads_half = heads_here // 2
    last = devices - 1
    tensor = lax.axis_size("tensor")

    def half_of(owner):
        pair = lax.dynamic_slice(critic_pair_projector, (0, owner * keyval_half), (depth, keyval_half))
        probe = lax.dynamic_slice(
            critic_probe_projector, (0, owner * query_half), (depth, query_half)
        )
        both = [pair[:, i : i + HD] for i in range(0, keyval_half, HD)]
        return both + [probe[:, i : i + HD] for i in range(0, query_half, HD)]

    mine, theirs = half_of(group), half_of(1 - group)
    count = len(mine)
    pairs = count - heads_half
    slots = jnp.concatenate([actor_latest_probes, actor_latest_pairs], axis=2)
    extra = slots.size // HD
    padding = -extra % 16
    mine[0] = jnp.concatenate([mine[0], slots.reshape(extra, HD), jnp.zeros((padding, HD), bf16)])
    value = {("w", 0, i): w for i, w in enumerate(mine)}
    value.update({("v", 0, i): w for i, w in enumerate(theirs)})

    value["token"] = jnp.zeros((8, HD), f32)

    def gate(*names):
        names = ["token"] + list(names)
        for name, array in zip(names, touch([value[n] for n in names])):
            value[name] = array

    value["own", 0] = response_latest_embeddings
    bits = [1 << b for b in range(int(math.log2(tensor)) - 1, -1, -1)]
    held = [0]
    for bit in bits[:-1]:
        for off in list(held):
            value["own", off ^ bit] = partner(value["own", off], "tensor", bit)
            held.append(off ^ bit)
    value["own", 1] = partner(value["own", 0], "tensor", 1)

    wide = 2
    groups = [range(low, min(pairs, low + wide)) for low in range(0, pairs, wide)]
    groups += [range(low, min(count, low + wide)) for low in range(pairs, count, wide)]
    hops = [(step, i) for chosen in groups for step in range(last) for i in chosen]
    total = len(hops)
    extras = {}

    def at(number, *names):
        extras.setdefault(min(number, total + wide - 1), []).extend(names)

    def arrived(number):
        step, i = hops[number]
        return step + 1, i

    numbers = [(place - step) % devices for step in range(devices)]

    def multiply(begin, end, names, before, column, final):
        weights = [[value[side, step, i] for side, i in names] for step in range(begin, end)]
        pieces = [value["own", off] for off in range(tensor)]
        done = project(pieces, numbers[begin:end], depth, weights, before, column, final)
        return done.reshape(rows, -1) if final else done

    grades = grading_columns(critic_grading_vector)
    value["share"] = jnp.zeros((cand_here, 8, span_len), f32)
    near = [off for off in held if off]
    def cross():
        for off in near:
            value["own", off ^ 1] = partner(value["own", off], "tensor", 1)
        at(now + 1, *[("own", off ^ 1) for off in near])

    def policy_now():
        everyone = jnp.zeros((devices * slots.shape[0],) + slots.shape[1:], bf16)
        for step in range(devices):
            part = value["w", step, 0][depth : depth + extra].reshape(slots.shape)
            start = (place - step) % devices * slots.shape[0]
            everyone = lax.dynamic_update_slice(everyone, part, (start, 0, 0))
        value["policy"] = policy_rows(
            actor_stored_pairs, filled_extents, kept_responses, everyone
        )
        at(now + 3, "policy")

    def fresh_block(chunk):
        return jnp.where(chunk // pairs == group, 0, pairs) + chunk % pairs

    def score(queries, first_block, heads):
        owners = {"w": group, "v": 1 - group}
        numbers = [owners[side] * heads_half + i - pairs for side, i in heads]
        value["share"] = reward_share(
            queries,
            first_block,
            numbers,
            critic_stored_pairs,
            per_group,
            value["initial"],
            fresh_block,
            grades,
            value["share"],
        )

    def keyval_now():
        names = [(side, i) for side in "wv" for i in range(pairs)]
        value["initial"] = multiply(0, devices, names, None, 0, True)
        at(now + 2, "initial")

    def both(chosen):
        return [(side, i) for i in chosen for side in "wv"]

    def some_now(chosen, first, end):
        before = value.get(("sums", chosen))
        value["sums", chosen] = multiply(first, end, both(chosen), before, 0, False)
        at(now + 2, ("sums", chosen))

    def scores_now(chosen, part):
        column = 2 * HD * chosen.index(part[0])
        heads = both(part)
        value["queries"] = multiply(last, devices, heads, value["sums", chosen], column, True)
        score(value["queries"], 0, heads)
        at(now + 3, "share")

    lag = 2

    def seen_at(step, i):
        return hops.index((step, i)) + wide + lag

    acts = [(seen_at(last - 1, 0) - lag, policy_now)]
    acts.append((seen_at(last - 1, pairs - 1), keyval_now))
    for chosen in groups:
        if chosen[0] < pairs:
            continue
        end = chosen[-1]
        if chosen is groups[-1]:
            acts.append((seen_at(0, end), functools.partial(some_now, chosen, 0, 2)))
            if last > 2:
                acts.append((seen_at(last - 2, end), functools.partial(some_now, chosen, 2, last)))
        else:
            acts.append((seen_at(last - 2, end), functools.partial(some_now, chosen, 0, last)))
            acts.append((seen_at(last - 1, end), functools.partial(scores_now, chosen, chosen)))
    acts.append((min(8, total // 2), cross))
    at(total + wide - 1, "policy")
    at(wide, ("own", 1))
    at(min(8, total // 2), *[("own", off) for off in near])
    for now in range(total + wide + lag):
        names = []
        if 0 <= now - wide < total:
            names.append(("w",) + arrived(now - wide))
        if 0 <= now - wide - lag < total:
            names.append(("v",) + arrived(now - wide - lag))
        if now < total and hops[now][0] == 0 and now >= wide:
            names.append(("w",) + hops[now])
        names += extras.pop(now, [])
        if now >= wide:
            gate(*names)
        if now < total:
            step, i = hops[now]
            value["w", step + 1, i] = shifted(value["w", step, i], "cand", 1)
        if 0 <= now - wide < total:
            step, i = arrived(now - wide)
            value["v", step, i] = partner(value["w", step, i], "groups", 1)
        for when, act in acts:
            if when == now:
                act()

    chosen = groups[-1]
    for i in chosen:
        if i != chosen[0]:
            gate(("w", last, i), ("v", last, i), "share")
        scores_now(chosen, [i])
    slot_rows = send_slots(value["policy"], slots.shape[0])
    share = value["share"]
    share = share[:, 0, :]
    terms = [share] + [partner(share, "tensor", bits) for bits in range(1, tensor)]
    while len(terms) > 1:
        terms = [a + b for a, b in zip(terms[::2], terms[1::2])]
    return terms[0], slot_rows


def solution(mesh):
    placed = (
        P(("groups", "cand"), None, "tensor"),
        P("cand", "tensor"),
        P("cand", "tensor"),
        P(("groups", "cand"), None, "tensor"),
        P("tensor"),
        P(("groups", "cand"), None, "tensor", None),
        P("groups"),
        P("groups"),
        P(("groups", "cand"), None, "tensor"),
        P(("groups", "cand"), None, "tensor"),
    )
    return jax.shard_map(
        local,
        mesh=mesh,
        in_specs=placed,
        out_specs=(P(("groups", "cand"), None), P(("groups", "cand"), None, "tensor")),
        check_vma=False,
    )
```

time: 287 us -> 281 us (0.979)
  waiting for transfers between devices: 119 us -> 96.3 us
  Pallas kernels: 81.1 us -> 88.9 us
  starting transfers between devices: 34 us -> 41.5 us
  local copies, waits for them, and re-layouts: 38 us -> 41.7 us
    ppermute x17 -> x26, waiting for transfers between devices: 24.7 us -> 2.88 us  [partner(): return lax.ppermute(value, axis, [(i, i ^ bits) for i in range(size)])]
    ppermute x17 -> x26, starting transfers between devices: 12.8 us -> 30 us  [partner(): return lax.ppermute(value, axis, [(i, i ^ bits) for i in range(size)])]
    ppermute x21 -> x18, starting transfers between devices: 21.2 us -> 11.5 us  [shifted(): lax.ppermute(value, axis, [(i, (i + step) % size) for i in range(size)])]
    unnamed x79 -> x72, local copies, waits for them, and re-layouts: 8.88 us -> 18.4 us
    pallas_call x7 -> x28, Pallas kernels: 54.1 us -> 58.7 us  [the longest x7 58.7 us: project(): pl.pallas_call(functools.partial(project_kernel, plan), in_specs=[pl.Bloc...]
    dynamic_update_slice x4, local copies, waits for them, and re-layouts: 4.53 us -> 0.06 us  [policy_now(): everyone = lax.dynamic_update_slice(everyone, part, (start, 0, 0))]
    pallas_call x8 -> x3, Pallas kernels: 27 us -> 30.2 us  [reward_share(): pl.pallas_call(reward_kernel, grid_spec=spec, out_shape=jax.ShapeDtypeStr...]
    another operation x0 -> x5, local copies, waits for them, and re-layouts: none -> 3.01 us  [the longest x3 1.82 us: reward_share(): scalars = jnp.stack(scalars).astype(jnp.int32)]
  transfers between devices with their start and end apart: 38 -> 44, of which waited for: 15 -> 16; matrix products, arithmetic and copies ran while one was open for 15% -> 12% of each run, Pallas kernels for 28% -> 32%
where the time goes in v1:
time: 281 us; the launch traced here: 280 us
  waiting for transfers between devices  96.3 us (34%)
  Pallas kernels  88.9 us (32%)
  local copies, waits for them, and re-layouts  41.7 us (15%)
  starting transfers between devices  41.5 us (15%)
  other arithmetic  6.49 us (2%)
  matrix products  3.78 us (1%)
    ppermute x18, waiting for transfers between devices, shifted(): lax.ppermute(value, axis, [(i, (i + step) % size) for i in range(size)])  93.4 us
    pallas_call x7, Pallas kernels, project(): pl.pallas_call(functools.partial(project_kernel, plan), in_specs=[pl.Bloc...  58.7 us
    pallas_call x3, Pallas kernels, reward_share(): pl.pallas_call(reward_kernel, grid_spec=spec, out_shape=jax.ShapeDtypeStr...  30.2 us
    ppermute x26, starting transfers between devices, partner(): return lax.ppermute(value, axis, [(i, i ^ bits) for i in range(size)])  30 us
    unnamed x72, local copies, waits for them, and re-layouts  18.4 us
    ppermute x18, starting transfers between devices, shifted(): lax.ppermute(value, axis, [(i, (i + step) % size) for i in range(size)])  11.5 us
    slice x1, local copies, waits for them, and re-layouts, policy_rows(): stored[..., :HD]  6.04 us
  transfers between devices with their start and end apart: 44, of which 16 were waited for; matrix products, arithmetic and copies ran while one was open for 12% of the time, Pallas kernels for 32%

profile of v1, /device:TPU:0, one launch (start us, length us, event | category | flops | bytes accessed | tf_op | source)
XLA Modules:
  0.0 279.9 jit_solution(11688746496246494328)
XLA Ops:
  1.2 2.6 collective-permute-start.13
  5.2 2.8 constant_dynamic-slice_fusion.9
  8.8 1.6 collective-permute-start
  10.4 1.6 collective-permute-start.2
  12.8 13.1 %collective-permute-done.refs_1_ = bf16[2096,128]{1,0:T(8,128)(2,1)} collective-permute-done((bf16[2096,128]{1,0:T(8,128)(2,1)}, bf16[2096,128]{1,0:T(8,128)(2,1)}, u32[]{:S(2)}, u32[]{:S(2)}) %collective-permute-start) | collective-permute-done | bytes 536608 | tf_op jit(solution)/shard_map/ppermute | solution.py:32
  27.7 1.5 collective-permute-start.4
  29.2 4.3 %constant_dynamic-slice_fusion.8 = (bf16[2048,128]{1,0:T(8,128)(2,1)}, bf16[2048,128]{1,0:T(8,128)(2,1)}, bf16[2048,128]{1,0:T(8,128)(2,1)}, bf16[2048,128]{1,0:...) fusion(bf16[2048,1024]{1,0:T(8,128)(2,1)} %param.11, ...), kind=kLoop, calls=%fused_computation.53 | loop fusion | bytes 8388640 | tf_op jit(solution)/shard_map/slice | solution.py:360
  33.5 3.7 %collective-permute-done.2.refs_1_ = bf16[2048,128]{1,0:T(8,128)(2,1)} collective-permute-done((bf16[2048,128]{1,0:T(8,128)(2,1)}, bf16[2048,128]{1,0:T(8,128)(2,1)}, u32[]{:S(2)}, u32[]{:S(2)}) %collective-permute-start.2) | collective-permute-done | bytes 524320 | tf_op jit(solution)/shard_map/ppermute | solution.py:32
  37.2 1.5 collective-permute-start.6
  38.7 9.9 %collective-permute-done.3.refs_1_ = bf16[2096,128]{1,0:T(8,128)(2,1)S(1)} collective-permute-done((bf16[2096,128]{1,0:T(8,128)(2,1)}, bf16[2096,128]{1,0:T(8,128)(2,1)S(1)}, u32[]{:S(2)}, u32[]{:S(2)}) %collective-permute-start.3) | collective-permute-done | bytes 536608 | tf_op jit(solution)/shard_map/ppermute | solution.py:32
  49.6 1.5 collective-permute-start.8
  51.1 6.0 %fusion.28 = (bf16[2,2048,2,128]{3,2,1,0:T(2,128)(2,1)}, bf16[2,2048,2,128]{3,2,1,0:T(2,128)(2,1)}) fusion(bf16[2,2048,2,256]{3,2,1,0:T(2,128)(2,1)} %param.15), kind=kLoop, calls=%fused_computation.86 | loop fusion | bytes 8388608 | tf_op jit(solution)/shard_map/slice | solution.py:298
  57.1 2.7 collective-permute-done.5.refs_1_
  60.8 1.5 collective-permute-start.10
  62.3 9.1 %collective-permute-done.7.refs_1_ = bf16[2096,128]{1,0:T(8,128)(2,1)} collective-permute-done((bf16[2096,128]{1,0:T(8,128)(2,1)}, bf16[2096,128]{1,0:T(8,128)(2,1)}, u32[]{:S(2)}, u32[]{:S(2)}) %collective-permute-start.7) | collective-permute-done | bytes 536608 | tf_op jit(solution)/shard_map/ppermute | solution.py:32
  72.2 1.5 collective-permute-start.12
  73.9 1.7 collective-permute-done.10.refs_2_
  75.6 7.0 %collective-permute-done.9.refs_1_ = bf16[2048,128]{1,0:T(8,128)(2,1)S(1)} collective-permute-done((bf16[2048,128]{1,0:T(8,128)(2,1)}, bf16[2048,128]{1,0:T(8,128)(2,1)S(1)}, u32[]{:S(2)}, u32[]{:S(2)}) %collective-permute-start.9) | collective-permute-done | bytes 524320 | tf_op jit(solution)/shard_map/ppermute | solution.py:32
  83.4 9.8 %collective-permute-done.11.refs_1_ = bf16[2048,128]{1,0:T(8,128)(2,1)} collective-permute-done((bf16[2048,128]{1,0:T(8,128)(2,1)}, bf16[2048,128]{1,0:T(8,128)(2,1)}, u32[]{:S(2)}, u32[]{:S(2)}) %collective-permute-start.11) | collective-permute-done | bytes 524320 | tf_op jit(solution)/shard_map/ppermute | solution.py:32
  97.8 1.6 collective-permute-start.15
  99.7 2.3 fusion.29
  106.2 8.5 %collective-permute-done.14.refs_1_ = bf16[2048,128]{1,0:T(8,128)(2,1)} collective-permute-done((bf16[2048,128]{1,0:T(8,128)(2,1)}, bf16[2048,128]{1,0:T(8,128)(2,1)}, u32[]{:S(2)}, u32[]{:S(2)}) %collective-permute-start.14) | collective-permute-done | bytes 524320 | tf_op jit(solution)/shard_map/ppermute | solution.py:32
  114.7 1.7 copy-done.1
  116.3 1.5 collective-permute-start.20
  117.9 8.0 %collective-permute-done.17.refs_1_ = bf16[2048,128]{1,0:T(8,128)(2,1)} collective-permute-done((bf16[2048,128]{1,0:T(8,128)(2,1)}, bf16[2048,128]{1,0:T(8,128)(2,1)}, u32[]{:S(2)}, u32[]{:S(2)}) %collective-permute-start.17) | collective-permute-done | bytes 524320 | tf_op jit(solution)/shard_map/ppermute | solution.py:32
  125.9 1.6 collective-permute-start.22
  127.5 14.1 %project.7 = bf16[2,384,512]{2,1,0:T(8,128)(2,1)} custom-call(s32[8]{0:T(128)} %stack.170.where_ref, bf16[2,384,2048]{2,1,0:T(8,128)(2,1)} %refs_0_.13, bf16[2,384,2048]{2,1,0:T(8,128)(2,1)} %get-tuple-element.74.refs_1_, bf16[2,384,2048]{2,1,0:T(8,128)(2,1)} %get-tuple-element.87.refs_2_, bf16[2,384,2048]{2,1,0:T(8,128)(2,1)} %get-tuple-element.91.refs_3_, ...), custom_call_target="tpu_custom_call" | custom-call | flops 6442450944 | bytes 12582912 | tf_op jit(solution)/shard_map/project/pallas_call | solution.py:131
  144.1 4.1 %collective-permute-done.21.refs_1_ = bf16[2048,128]{1,0:T(8,128)(2,1)S(1)} collective-permute-done((bf16[2048,128]{1,0:T(8,128)(2,1)}, bf16[2048,128]{1,0:T(8,128)(2,1)S(1)}, u32[]{:S(2)}, u32[]{:S(2)}) %collective-permute-start.21) | collective-permute-done | bytes 524320 | tf_op jit(solution)/shard_map/ppermute | solution.py:32
  149.2 1.5 collective-permute-start.26
  152.6 6.8 %collective-permute-done.23.refs_1_ = bf16[2048,128]{1,0:T(8,128)(2,1)S(1)} collective-permute-done((bf16[2048,128]{1,0:T(8,128)(2,1)}, bf16[2048,128]{1,0:T(8,128)(2,1)S(1)}, u32[]{:S(2)}, u32[]{:S(2)}) %collective-permute-start.23) | collective-permute-done | bytes 524320 | tf_op jit(solution)/shard_map/ppermute | solution.py:32
  162.7 8.0 %collective-permute-done.25.refs_1_ = bf16[2048,128]{1,0:T(8,128)(2,1)S(1)} collective-permute-done((bf16[2048,128]{1,0:T(8,128)(2,1)}, bf16[2048,128]{1,0:T(8,128)(2,1)S(1)}, u32[]{:S(2)}, u32[]{:S(2)}) %collective-permute-start.25) | collective-permute-done | bytes 524320 | tf_op jit(solution)/shard_map/ppermute | solution.py:32
  173.3 11.7 %project.8.refs_3_ = f32[2,384,512]{2,1,0:T(8,128)} custom-call(s32[6]{0:T(128)} %stack.171.where_ref, bf16[2,384,2048]{2,1,0:T(8,128)(2,1)} %refs_0_.13, bf16[2,384,2048]{2,1,0:T(8,128)(2,1)} %get-tuple-element.74.refs_1_, bf16[2,384,2048]{2,1,0:T(8,128)(2,1)} %get-tuple-element.87.refs_2_, bf16[2,384,2048]{2,1,0:T(8,128)(2,1)} %get-tuple-element.91.refs_3_, ...), custom_call_target="tpu_custom_call" | custom-call | flops 4831838208 | bytes 9437184 | tf_op jit(solution)/shard_map/project/pallas_call | solution.py:131
  186.0 1.8 collective-permute-start.31
  187.8 1.5 collective-permute-start.32
  195.8 6.7 %project.9 = bf16[2,384,512]{2,1,0:T(8,128)(2,1)} custom-call(s32[2]{0:T(128)} %pad_add_fusion.1.where_ref, bf16[2,384,2048]{2,1,0:T(8,128)(2,1)} %refs_0_.13, bf16[2,384,2048]{2,1,0:T(8,128)(2,1)} %get-tuple-element.74.refs_1_, bf16[2,384,2048]{2,1,0:T(8,128)(2,1)} %get-tuple-element.87.refs_2_, bf16[2,384,2048]{2,1,0:T(8,128)(2,1)} %get-tuple-element.91.refs_3_, ...), custom_call_target="tpu_custom_call" | custom-call | flops 1610612736 | bytes 3145728 | tf_op jit(solution)/shard_map/project/pallas_call | solution.py:131
  202.5 1.9 collective-permute-done.31.refs_1_
  207.6 13.8 %reward_share.3.refs_3_ = f32[2,8,384]{2,1,0:T(8,128)} custom-call(s32[16]{0:T(128)} %stack.188.kg_ref, bf16[768,512]{1,0:T(8,128)(2,1)} %bitcast.102, bf16[2,2048,512]{2,1,0:T(8,128)(2,1)} %old_value_ref.5, bf16[2,2048,512]{2,1,0:T(8,128)(2,1)} %old_value_ref.5, bf16[768,512]{1,0:T(8,128)(2,1)} %get-tuple-element.125.key_ref.value_ref, ...), custom_call_target="tpu_custom_call" | custom-call | flops 5737807872 | bytes 8388608 | tf_op jit(solution)/shard_map/reward_share/pallas_call | solution.py:245
  222.5 1.4 collective-permute-start.37
  223.9 9.1 %project.10.refs_4_ = f32[2,384,512]{2,1,0:T(8,128)} custom-call(s32[4]{0:T(128)} %pad_add_fusion.2.where_ref, bf16[2,384,2048]{2,1,0:T(8,128)(2,1)} %refs_0_.13, bf16[2,384,2048]{2,1,0:T(8,128)(2,1)} %get-tuple-element.74.refs_1_, bf16[2,384,2048]{2,1,0:T(8,128)(2,1)} %get-tuple-element.87.refs_2_, bf16[2,384,2048]{2,1,0:T(8,128)(2,1)} %get-tuple-element.91.refs_3_, ...), custom_call_target="tpu_custom_call" | custom-call | flops 3221225472 | bytes 6291456 | tf_op jit(solution)/shard_map/project/pallas_call | solution.py:131
  234.8 1.5 collective-permute-start.42
  236.3 1.5 collective-permute-start.38
  237.8 6.9 %project.11.refs_6_ = f32[2,384,512]{2,1,0:T(8,128)} custom-call(s32[2]{0:T(128)} %pad_add_fusion.where_ref, bf16[2,384,2048]{2,1,0:T(8,128)(2,1)} %refs_0_.13, bf16[2,384,2048]{2,1,0:T(8,128)(2,1)} %get-tuple-element.74.refs_1_, bf16[2,384,2048]{2,1,0:T(8,128)(2,1)} %get-tuple-element.87.refs_2_, bf16[2,384,2048]{2,1,0:T(8,128)(2,1)} %get-tuple-element.91.refs_3_, ...), custom_call_target="tpu_custom_call" | custom-call | flops 1610612736 | bytes 3145728 | tf_op jit(solution)/shard_map/project/pallas_call | solution.py:131
  245.6 5.1 %project.12 = bf16[2,384,256]{2,1,0:T(8,128)(2,1)} custom-call(s32[2]{0:T(128)} %pad_add_fusion.1.where_ref, bf16[2,384,2048]{2,1,0:T(8,128)(2,1)} %refs_0_.13, bf16[2,384,2048]{2,1,0:T(8,128)(2,1)} %get-tuple-element.74.refs_1_, bf16[2,384,2048]{2,1,0:T(8,128)(2,1)} %get-tuple-element.87.refs_2_, bf16[2,384,2048]{2,1,0:T(8,128)(2,1)} %get-tuple-element.91.refs_3_, ...), custom_call_target="tpu_custom_call" | custom-call | flops 805306368 | bytes 3145728 | tf_op jit(solution)/shard_map/project/pallas_call | solution.py:131
  250.7 8.2 %reward_share.4.refs_3_ = f32[2,8,384]{2,1,0:T(8,128)} custom-call(s32[8]{0:T(128)} %stack.198.kg_ref, bf16[768,256]{1,0:T(8,128)(2,1)} %bitcast.101, bf16[2,2048,512]{2,1,0:T(8,128)(2,1)} %old_value_ref.5, bf16[2,2048,512]{2,1,0:T(8,128)(2,1)} %old_value_ref.5, bf16[768,512]{1,0:T(8,128)(2,1)} %get-tuple-element.125.key_ref.value_ref, ...), custom_call_target="tpu_custom_call" | custom-call | flops 2868903936 | bytes 8388608 | tf_op jit(solution)/shard_map/reward_share/pallas_call | solution.py:245
  258.9 2.0 collective-permute-start.43
  261.7 5.1 %project.13 = bf16[2,384,256]{2,1,0:T(8,128)(2,1)} custom-call(s32[2]{0:T(128)} %pad_add_fusion.1.where_ref, bf16[2,384,2048]{2,1,0:T(8,128)(2,1)} %refs_0_.13, bf16[2,384,2048]{2,1,0:T(8,128)(2,1)} %get-tuple-element.74.refs_1_, bf16[2,384,2048]{2,1,0:T(8,128)(2,1)} %get-tuple-element.87.refs_2_, bf16[2,384,2048]{2,1,0:T(8,128)(2,1)} %get-tuple-element.91.refs_3_, ...), custom_call_target="tpu_custom_call" | custom-call | flops 805306368 | bytes 3145728 | tf_op jit(solution)/shard_map/project/pallas_call | solution.py:131
  266.8 8.2 %reward_share.5 = f32[2,8,384]{2,1,0:T(8,128)} custom-call(s32[8]{0:T(128)} %stack.164.kg_ref, bf16[768,256]{1,0:T(8,128)(2,1)} %bitcast.100, bf16[2,2048,512]{2,1,0:T(8,128)(2,1)} %old_value_ref.5, bf16[2,2048,512]{2,1,0:T(8,128)(2,1)} %old_value_ref.5, bf16[768,512]{1,0:T(8,128)(2,1)} %get-tuple-element.125.key_ref.value_ref, ...), custom_call_target="tpu_custom_call" | custom-call | flops 2868903936 | bytes 8388608 | tf_op jit(solution)/shard_map/reward_share/pallas_call | solution.py:245
  276.3 1.3 collective-permute-start.41
  (207 shorter events, 47.8 us)
Async XLA Ops:
  0.6 11.6 %copy-start = (s32[8]{0:T(128)S(1)}, s32[8]{0:T(128)}, u32[]{:S(2)}) copy-start(s32[8]{0:T(128)} %param.16) | copy-start | bytes 100
  0.6 25.3 %collective-permute-start.1 = (bf16[2,384,2048]{2,1,0:T(8,128)(2,1)}, bf16[2,384,2048]{2,1,0:T(8,128)(2,1)S(1)}, u32[]{:S(2)}, u32[]{:S(2)}) collective-permute-start(bf16[2,384,2048]{2,1,0:T(8,128)(2,1)} %refs_0_.13), channel_id=1, source_target_pairs={{0,1},{1,0},{2,3},{3,2},{4,5},{5,4},{6,7},{7,6},{8,9},{9,8},{10,11... | collective-permute-start | bytes 9437192 | tf_op jit(solution)/shard_map/ppermute | solution.py:37
  1.2 82.2 %collective-permute-start.13 = (bf16[2,384,2048]{2,1,0:T(8,128)(2,1)}, bf16[2,384,2048]{2,1,0:T(8,128)(2,1)}, u32[]{:S(2)}, u32[]{:S(2)}) collective-permute-start(bf16[2,384,2048]{2,1,0:T(8,128)(2,1)} %refs_0_.13), channel_id=1, source_target_pairs={{0,2},{1,3},{2,0},{3,1},{4,6},{5,7},{6,4},{7,5},{8,10},{9,11},{10,... | collective-permute-start | bytes 9437192 | tf_op jit(solution)/shard_map/ppermute | solution.py:37
  5.1 6.8 %copy-start.34 = (s32[4]{0:T(128)S(1)}, s32[4]{0:T(128)}, u32[]{:S(2)}) copy-start(s32[4]{0:T(128)} %param.17) | copy-start | bytes 52
  8.8 17.1 %collective-permute-start = (bf16[2096,128]{1,0:T(8,128)(2,1)}, bf16[2096,128]{1,0:T(8,128)(2,1)}, u32[]{:S(2)}, u32[]{:S(2)}) collective-permute-start(bf16[2096,128]{1,0:T(8,128)(2,1)} %pad_maximum_fusion.refs_4_), channel_id=1, source_target_pairs={{0,4},{4,8},{8,12},{12,0},{1,5},{5,9},{9,13},{13,1},{2,6},{6,10},{... | collective-permute-start | bytes 1609736 | tf_op jit(solution)/shard_map/ppermute | solution.py:32
  10.4 26.8 %collective-permute-start.2 = (bf16[2048,128]{1,0:T(8,128)(2,1)}, bf16[2048,128]{1,0:T(8,128)(2,1)}, u32[]{:S(2)}, u32[]{:S(2)}) collective-permute-start(bf16[2048,128]{1,0:T(8,128)(2,1)} %get-tuple-element.159.refs_5_), channel_id=1, source_target_pairs={{0,4},{4,8},{8,12},{12,0},{1,5},{5,9},{9,13},{13,1},{2,6},{6,10},{... | collective-permute-start | bytes 1572872 | tf_op jit(solution)/shard_map/ppermute | solution.py:32
  27.7 20.9 %collective-permute-start.3 = (bf16[2096,128]{1,0:T(8,128)(2,1)}, bf16[2096,128]{1,0:T(8,128)(2,1)S(1)}, u32[]{:S(2)}, u32[]{:S(2)}) collective-permute-start(bf16[2096,128]{1,0:T(8,128)(2,1)} %get-tuple-element.77.refs_8_), channel_id=1, source_target_pairs={{0,4},{4,8},{8,12},{12,0},{1,5},{5,9},{9,13},{13,1},{2,6},{6,10},{... | collective-permute-start | bytes 1609736 | tf_op jit(solution)/shard_map/ppermute | solution.py:32
  27.7 20.9 %collective-permute-start.4 = (bf16[2096,128]{1,0:T(8,128)(2,1)}, bf16[2096,128]{1,0:T(8,128)(2,1)S(1)}, u32[]{:S(2)}, u32[]{:S(2)}) collective-permute-start(bf16[2096,128]{1,0:T(8,128)(2,1)} %get-tuple-element.77.refs_8_), channel_id=1, source_target_pairs={{0,16},{16,0},{1,17},{17,1},{2,18},{18,2},{3,19},{19,3},{4,20},{20... | collective-permute-start | bytes 1609736 | tf_op jit(solution)/shard_map/ppermute | solution.py:37
  37.2 22.6 %collective-permute-start.5 = (bf16[2048,128]{1,0:T(8,128)(2,1)}, bf16[2048,128]{1,0:T(8,128)(2,1)S(1)}, u32[]{:S(2)}, u32[]{:S(2)}) collective-permute-start(bf16[2048,128]{1,0:T(8,128)(2,1)} %get-tuple-element.79.refs_9_), channel_id=1, source_target_pairs={{0,4},{4,8},{8,12},{12,0},{1,5},{5,9},{9,13},{13,1},{2,6},{6,10},{... | collective-permute-start | bytes 1572872 | tf_op jit(solution)/shard_map/ppermute | solution.py:32
  37.2 22.6 %collective-permute-start.6 = (bf16[2048,128]{1,0:T(8,128)(2,1)}, bf16[2048,128]{1,0:T(8,128)(2,1)S(1)}, u32[]{:S(2)}, u32[]{:S(2)}) collective-permute-start(bf16[2048,128]{1,0:T(8,128)(2,1)} %get-tuple-element.79.refs_9_), channel_id=1, source_target_pairs={{0,16},{16,0},{1,17},{17,1},{2,18},{18,2},{3,19},{19,3},{4,20},{20... | collective-permute-start | bytes 1572872 | tf_op jit(solution)/shard_map/ppermute | solution.py:37
  49.6 21.8 %collective-permute-start.7 = (bf16[2096,128]{1,0:T(8,128)(2,1)}, bf16[2096,128]{1,0:T(8,128)(2,1)}, u32[]{:S(2)}, u32[]{:S(2)}) collective-permute-start(bf16[2096,128]{1,0:T(8,128)(2,1)} %get-tuple-element.81.refs_12_), channel_id=1, source_target_pairs={{0,4},{4,8},{8,12},{12,0},{1,5},{5,9},{9,13},{13,1},{2,6},{6,10},{... | collective-permute-start | bytes 1609736 | tf_op jit(solution)/shard_map/ppermute | solution.py:32
  49.6 21.8 %collective-permute-start.8 = (bf16[2096,128]{1,0:T(8,128)(2,1)}, bf16[2096,128]{1,0:T(8,128)(2,1)S(1)}, u32[]{:S(2)}, u32[]{:S(2)}) collective-permute-start(bf16[2096,128]{1,0:T(8,128)(2,1)} %get-tuple-element.81.refs_12_), channel_id=1, source_target_pairs={{0,16},{16,0},{1,17},{17,1},{2,18},{18,2},{3,19},{19,3},{4,20},{20... | collective-permute-start | bytes 1609736 | tf_op jit(solution)/shard_map/ppermute | solution.py:37
  60.8 14.8 %collective-permute-start.10 = (bf16[2048,128]{1,0:T(8,128)(2,1)}, bf16[2048,128]{1,0:T(8,128)(2,1)S(1)}, u32[]{:S(2)}, u32[]{:S(2)}) collective-permute-start(bf16[2048,128]{1,0:T(8,128)(2,1)} %get-tuple-element.83.refs_13_), channel_id=1, source_target_pairs={{0,16},{16,0},{1,17},{17,1},{2,18},{18,2},{3,19},{19,3},{4,20},{20... | collective-permute-start | bytes 1572872 | tf_op jit(solution)/shard_map/ppermute | solution.py:37
  62.3 20.2 %collective-permute-start.9 = (bf16[2048,128]{1,0:T(8,128)(2,1)}, bf16[2048,128]{1,0:T(8,128)(2,1)S(1)}, u32[]{:S(2)}, u32[]{:S(2)}) collective-permute-start(bf16[2048,128]{1,0:T(8,128)(2,1)} %get-tuple-element.83.refs_13_), channel_id=1, source_target_pairs={{0,4},{4,8},{8,12},{12,0},{1,5},{5,9},{9,13},{13,1},{2,6},{6,10},{... | collective-permute-start | bytes 1572872 | tf_op jit(solution)/shard_map/ppermute | solution.py:32
  72.2 21.0 %collective-permute-start.12 = (bf16[2096,128]{1,0:T(8,128)(2,1)}, bf16[2096,128]{1,0:T(8,128)(2,1)S(1)}, u32[]{:S(2)}, u32[]{:S(2)}) collective-permute-start(bf16[2096,128]{1,0:T(8,128)(2,1)} %get-tuple-element.86.refs_16_), channel_id=1, source_target_pairs={{0,16},{16,0},{1,17},{17,1},{2,18},{18,2},{3,19},{19,3},{4,20},{20... | collective-permute-start | bytes 1609736 | tf_op jit(solution)/shard_map/ppermute | solution.py:37
  73.8 19.4 %collective-permute-start.11 = (bf16[2048,128]{1,0:T(8,128)(2,1)}, bf16[2048,128]{1,0:T(8,128)(2,1)}, u32[]{:S(2)}, u32[]{:S(2)}) collective-permute-start(bf16[2048,128]{1,0:T(8,128)(2,1)} %get-tuple-element.85.refs_4_), channel_id=1, source_target_pairs={{0,4},{4,8},{8,12},{12,0},{1,5},{5,9},{9,13},{13,1},{2,6},{6,10},{... | collective-permute-start | bytes 1572872 | tf_op jit(solution)/shard_map/ppermute | solution.py:32
  75.6 7.0 %copy-start.29 = (bf16[2048,128]{1,0:T(8,128)(2,1)}, bf16[2048,128]{1,0:T(8,128)(2,1)S(1)}, u32[]{:S(2)}) copy-start(bf16[2048,128]{1,0:T(8,128)(2,1)S(1)} %collective-permute-done.10.refs_2_) | copy-start | bytes 1572868
  94.0 20.6 %collective-permute-start.16 = (bf16[2,384,2048]{2,1,0:T(8,128)(2,1)}, bf16[2,384,2048]{2,1,0:T(8,128)(2,1)S(1)}, u32[]{:S(2)}, u32[]{:S(2)}) collective-permute-start(bf16[2,384,2048]{2,1,0:T(8,128)(2,1)} %get-tuple-element.87.refs_2_), channel_id=1, source_target_pairs={{0,1},{1,0},{2,3},{3,2},{4,5},{5,4},{6,7},{7,6},{8,9},{9,8},{10,11... | collective-permute-start | bytes 9437192 | tf_op jit(solution)/shard_map/ppermute | solution.py:37
  97.7 16.9 %collective-permute-start.14 = (bf16[2048,128]{1,0:T(8,128)(2,1)}, bf16[2048,128]{1,0:T(8,128)(2,1)}, u32[]{:S(2)}, u32[]{:S(2)}) collective-permute-start(bf16[2048,128]{1,0:T(8,128)(2,1)} %get-tuple-element.89.refs_6_), channel_id=1, source_target_pairs={{0,4},{4,8},{8,12},{12,0},{1,5},{5,9},{9,13},{13,1},{2,6},{6,10},{... | collective-permute-start | bytes 1572872 | tf_op jit(solution)/shard_map/ppermute | solution.py:32
  97.8 16.8 %collective-permute-start.15 = (bf16[2048,128]{1,0:T(8,128)(2,1)}, bf16[2048,128]{1,0:T(8,128)(2,1)}, u32[]{:S(2)}, u32[]{:S(2)}) collective-permute-start(bf16[2048,128]{1,0:T(8,128)(2,1)} %get-tuple-element.90.refs_17_), channel_id=1, source_target_pairs={{0,16},{16,0},{1,17},{17,1},{2,18},{18,2},{3,19},{19,3},{4,20},{20... | collective-permute-start | bytes 1572872 | tf_op jit(solution)/shard_map/ppermute | solution.py:37
  103.1 22.8 %collective-permute-start.17 = (bf16[2048,128]{1,0:T(8,128)(2,1)}, bf16[2048,128]{1,0:T(8,128)(2,1)}, u32[]{:S(2)}, u32[]{:S(2)}) collective-permute-start(bf16[2048,128]{1,0:T(8,128)(2,1)} %get-tuple-element.93.refs_8_), channel_id=1, source_target_pairs={{0,4},{4,8},{8,12},{12,0},{1,5},{5,9},{9,13},{13,1},{2,6},{6,10},{... | collective-permute-start | bytes 1572872 | tf_op jit(solution)/shard_map/ppermute | solution.py:32
  104.4 21.5 %collective-permute-start.18 = (bf16[2048,128]{1,0:T(8,128)(2,1)}, bf16[2048,128]{1,0:T(8,128)(2,1)}, u32[]{:S(2)}, u32[]{:S(2)}) collective-permute-start(bf16[2048,128]{1,0:T(8,128)(2,1)} %get-tuple-element.93.refs_8_), channel_id=1, source_target_pairs={{0,16},{16,0},{1,17},{17,1},{2,18},{18,2},{3,19},{19,3},{4,20},{20... | collective-permute-start | bytes 1572872 | tf_op jit(solution)/shard_map/ppermute | solution.py:37
  116.3 25.2 %collective-permute-start.19 = (bf16[2048,128]{1,0:T(8,128)(2,1)}, bf16[2048,128]{1,0:T(8,128)(2,1)S(1)}, u32[]{:S(2)}, u32[]{:S(2)}) collective-permute-start(bf16[2048,128]{1,0:T(8,128)(2,1)} %get-tuple-element.95.refs_10_), channel_id=1, source_target_pairs={{0,4},{4,8},{8,12},{12,0},{1,5},{5,9},{9,13},{13,1},{2,6},{6,10},{... | collective-permute-start | bytes 1572872 | tf_op jit(solution)/shard_map/ppermute | solution.py:32
  116.3 25.2 %collective-permute-start.20 = (bf16[2048,128]{1,0:T(8,128)(2,1)}, bf16[2048,128]{1,0:T(8,128)(2,1)S(1)}, u32[]{:S(2)}, u32[]{:S(2)}) collective-permute-start(bf16[2048,128]{1,0:T(8,128)(2,1)} %get-tuple-element.95.refs_10_), channel_id=1, source_target_pairs={{0,16},{16,0},{1,17},{17,1},{2,18},{18,2},{3,19},{19,3},{4,20},{20... | collective-permute-start | bytes 1572872 | tf_op jit(solution)/shard_map/ppermute | solution.py:37
  125.9 22.4 %collective-permute-start.21 = (bf16[2048,128]{1,0:T(8,128)(2,1)}, bf16[2048,128]{1,0:T(8,128)(2,1)S(1)}, u32[]{:S(2)}, u32[]{:S(2)}) collective-permute-start(bf16[2048,128]{1,0:T(8,128)(2,1)} %get-tuple-element.103.refs_12_), channel_id=1, source_target_pairs={{0,4},{4,8},{8,12},{12,0},{1,5},{5,9},{9,13},{13,1},{2,6},{6,10},{... | collective-permute-start | bytes 1572872 | tf_op jit(solution)/shard_map/ppermute | solution.py:32
  125.9 22.4 %collective-permute-start.22 = (bf16[2048,128]{1,0:T(8,128)(2,1)}, bf16[2048,128]{1,0:T(8,128)(2,1)S(1)}, u32[]{:S(2)}, u32[]{:S(2)}) collective-permute-start(bf16[2048,128]{1,0:T(8,128)(2,1)} %get-tuple-element.103.refs_12_), channel_id=1, source_target_pairs={{0,16},{16,0},{1,17},{17,1},{2,18},{18,2},{3,19},{19,3},{4,20},{20... | collective-permute-start | bytes 1572872 | tf_op jit(solution)/shard_map/ppermute | solution.py:37
  142.6 16.9 %collective-permute-start.23 = (bf16[2048,128]{1,0:T(8,128)(2,1)}, bf16[2048,128]{1,0:T(8,128)(2,1)S(1)}, u32[]{:S(2)}, u32[]{:S(2)}) collective-permute-start(bf16[2048,128]{1,0:T(8,128)(2,1)} %get-tuple-element.105.refs_14_), channel_id=1, source_target_pairs={{0,4},{4,8},{8,12},{12,0},{1,5},{5,9},{9,13},{13,1},{2,6},{6,10},{... | collective-permute-start | bytes 1572872 | tf_op jit(solution)/shard_map/ppermute | solution.py:32
  143.6 15.9 %collective-permute-start.24 = (bf16[2048,128]{1,0:T(8,128)(2,1)}, bf16[2048,128]{1,0:T(8,128)(2,1)S(1)}, u32[]{:S(2)}, u32[]{:S(2)}) collective-permute-start(bf16[2048,128]{1,0:T(8,128)(2,1)} %get-tuple-element.105.refs_14_), channel_id=1, source_target_pairs={{0,16},{16,0},{1,17},{17,1},{2,18},{18,2},{3,19},{19,3},{4,20},{20... | collective-permute-start | bytes 1572872 | tf_op jit(solution)/shard_map/ppermute | solution.py:37
  149.2 21.5 %collective-permute-start.25 = (bf16[2048,128]{1,0:T(8,128)(2,1)}, bf16[2048,128]{1,0:T(8,128)(2,1)S(1)}, u32[]{:S(2)}, u32[]{:S(2)}) collective-permute-start(bf16[2048,128]{1,0:T(8,128)(2,1)} %get-tuple-element.107.refs_4_), channel_id=1, source_target_pairs={{0,4},{4,8},{8,12},{12,0},{1,5},{5,9},{9,13},{13,1},{2,6},{6,10},{... | collective-permute-start | bytes 1572872 | tf_op jit(solution)/shard_map/ppermute | solution.py:32
  149.2 21.5 %collective-permute-start.26 = (bf16[2048,128]{1,0:T(8,128)(2,1)}, bf16[2048,128]{1,0:T(8,128)(2,1)S(1)}, u32[]{:S(2)}, u32[]{:S(2)}) collective-permute-start(bf16[2048,128]{1,0:T(8,128)(2,1)} %get-tuple-element.108.refs_4_), channel_id=1, source_target_pairs={{0,16},{16,0},{1,17},{17,1},{2,18},{18,2},{3,19},{19,3},{4,20},{20... | collective-permute-start | bytes 1572872 | tf_op jit(solution)/shard_map/ppermute | solution.py:37
  160.5 24.6 %collective-permute-start.27 = (bf16[2048,128]{1,0:T(8,128)(2,1)}, bf16[2048,128]{1,0:T(8,128)(2,1)S(1)}, u32[]{:S(2)}, u32[]{:S(2)}) collective-permute-start(bf16[2048,128]{1,0:T(8,128)(2,1)} %get-tuple-element.110.refs_6_), channel_id=1, source_target_pairs={{0,4},{4,8},{8,12},{12,0},{1,5},{5,9},{9,13},{13,1},{2,6},{6,10},{... | collective-permute-start | bytes 1572872 | tf_op jit(solution)/shard_map/ppermute | solution.py:32
  161.6 23.5 %collective-permute-start.28 = (bf16[2048,128]{1,0:T(8,128)(2,1)}, bf16[2048,128]{1,0:T(8,128)(2,1)S(1)}, u32[]{:S(2)}, u32[]{:S(2)}) collective-permute-start(bf16[2048,128]{1,0:T(8,128)(2,1)} %get-tuple-element.111.refs_6_), channel_id=1, source_target_pairs={{0,16},{16,0},{1,17},{17,1},{2,18},{18,2},{3,19},{19,3},{4,20},{20... | collective-permute-start | bytes 1572872 | tf_op jit(solution)/shard_map/ppermute | solution.py:37
  171.7 21.5 %collective-permute-start.29 = (bf16[2048,128]{1,0:T(8,128)(2,1)}, bf16[2048,128]{1,0:T(8,128)(2,1)S(1)}, u32[]{:S(2)}, u32[]{:S(2)}) collective-permute-start(bf16[2048,128]{1,0:T(8,128)(2,1)} %get-tuple-element.117.refs_8_), channel_id=1, source_target_pairs={{0,4},{4,8},{8,12},{12,0},{1,5},{5,9},{9,13},{13,1},{2,6},{6,10},{... | collective-permute-start | bytes 1572872 | tf_op jit(solution)/shard_map/ppermute | solution.py:32
  172.8 20.4 %collective-permute-start.30 = (bf16[2048,128]{1,0:T(8,128)(2,1)}, bf16[2048,128]{1,0:T(8,128)(2,1)S(1)}, u32[]{:S(2)}, u32[]{:S(2)}) collective-permute-start(bf16[2048,128]{1,0:T(8,128)(2,1)} %get-tuple-element.117.refs_8_), channel_id=1, source_target_pairs={{0,16},{16,0},{1,17},{17,1},{2,18},{18,2},{3,19},{19,3},{4,20},{20... | collective-permute-start | bytes 1572872 | tf_op jit(solution)/shard_map/ppermute | solution.py:37
  186.0 18.4 %collective-permute-start.31 = (bf16[2048,128]{1,0:T(8,128)(2,1)}, bf16[2048,128]{1,0:T(8,128)(2,1)S(1)}, u32[]{:S(2)}, u32[]{:S(2)}) collective-permute-start(bf16[2048,128]{1,0:T(8,128)(2,1)} %get-tuple-element.119.refs_10_), channel_id=1, source_target_pairs={{0,4},{4,8},{8,12},{12,0},{1,5},{5,9},{9,13},{13,1},{2,6},{6,10},{... | collective-permute-start | bytes 1572872 | tf_op jit(solution)/shard_map/ppermute | solution.py:32
  187.8 16.6 %collective-permute-start.32 = (bf16[2048,128]{1,0:T(8,128)(2,1)}, bf16[2048,128]{1,0:T(8,128)(2,1)S(1)}, u32[]{:S(2)}, u32[]{:S(2)}) collective-permute-start(bf16[2048,128]{1,0:T(8,128)(2,1)} %get-tuple-element.119.refs_10_), channel_id=1, source_target_pairs={{0,16},{16,0},{1,17},{17,1},{2,18},{18,2},{3,19},{19,3},{4,20},{20... | collective-permute-start | bytes 1572872 | tf_op jit(solution)/shard_map/ppermute | solution.py:37
  194.2 27.3 %collective-permute-start.33 = (bf16[2048,128]{1,0:T(8,128)(2,1)}, bf16[2048,128]{1,0:T(8,128)(2,1)S(1)}, u32[]{:S(2)}, u32[]{:S(2)}) collective-permute-start(bf16[2048,128]{1,0:T(8,128)(2,1)} %get-tuple-element.121.refs_4_), channel_id=1, source_target_pairs={{0,4},{4,8},{8,12},{12,0},{1,5},{5,9},{9,13},{13,1},{2,6},{6,10},{... | collective-permute-start | bytes 1572872 | tf_op jit(solution)/shard_map/ppermute | solution.py:32
  195.1 26.4 %collective-permute-start.34 = (bf16[2048,128]{1,0:T(8,128)(2,1)}, bf16[2048,128]{1,0:T(8,128)(2,1)S(1)}, u32[]{:S(2)}, u32[]{:S(2)}) collective-permute-start(bf16[2048,128]{1,0:T(8,128)(2,1)} %get-tuple-element.121.refs_4_), channel_id=1, source_target_pairs={{0,16},{16,0},{1,17},{17,1},{2,18},{18,2},{3,19},{19,3},{4,20},{20... | collective-permute-start | bytes 1572872 | tf_op jit(solution)/shard_map/ppermute | solution.py:37
  205.4 27.6 %collective-permute-start.35 = (bf16[2048,128]{1,0:T(8,128)(2,1)}, bf16[2048,128]{1,0:T(8,128)(2,1)S(1)}, u32[]{:S(2)}, u32[]{:S(2)}) collective-permute-start(bf16[2048,128]{1,0:T(8,128)(2,1)} %get-tuple-element.127.refs_6_), channel_id=1, source_target_pairs={{0,4},{4,8},{8,12},{12,0},{1,5},{5,9},{9,13},{13,1},{2,6},{6,10},{... | collective-permute-start | bytes 1572872 | tf_op jit(solution)/shard_map/ppermute | solution.py:32
  206.4 26.6 %collective-permute-start.36 = (bf16[2048,128]{1,0:T(8,128)(2,1)}, bf16[2048,128]{1,0:T(8,128)(2,1)S(1)}, u32[]{:S(2)}, u32[]{:S(2)}) collective-permute-start(bf16[2048,128]{1,0:T(8,128)(2,1)} %get-tuple-element.127.refs_6_), channel_id=1, source_target_pairs={{0,16},{16,0},{1,17},{17,1},{2,18},{18,2},{3,19},{19,3},{4,20},{20... | collective-permute-start | bytes 1572872 | tf_op jit(solution)/shard_map/ppermute | solution.py:37
  222.5 22.3 %collective-permute-start.37 = (bf16[2048,128]{1,0:T(8,128)(2,1)}, bf16[2048,128]{1,0:T(8,128)(2,1)S(1)}, u32[]{:S(2)}, u32[]{:S(2)}) collective-permute-start(bf16[2048,128]{1,0:T(8,128)(2,1)} %get-tuple-element.132.refs_4_), channel_id=1, source_target_pairs={{0,16},{16,0},{1,17},{17,1},{2,18},{18,2},{3,19},{19,3},{4,20},{20... | collective-permute-start | bytes 1572872 | tf_op jit(solution)/shard_map/ppermute | solution.py:37
  234.8 24.1 %collective-permute-start.42 = (bf16[2,4,1024]{2,1,0:T(4,128)(2,1)S(1)}, bf16[2,4,1024]{2,1,0:T(4,128)(2,1)S(1)}, u32[]{:S(2)}, u32[]{:S(2)}) collective-permute-start(bf16[2,4,1024]{2,1,0:T(4,128)(2,1)S(1)} %broadcast_select_fusion.1), channel_id=1, source_target_pairs={{0,8},{4,12},{8,0},{12,4},{1,9},{5,13},{9,1},{13,5},{2,10},{6,14},... | collective-permute-start | bytes 49160 | tf_op jit(solution)/shard_map/ppermute | solution.py:37
  236.3 24.6 %collective-permute-start.38 = (bf16[2048,128]{1,0:T(8,128)(2,1)}, bf16[2048,128]{1,0:T(8,128)(2,1)S(1)}, u32[]{:S(2)}, u32[]{:S(2)}) collective-permute-start(bf16[2048,128]{1,0:T(8,128)(2,1)} %get-tuple-element.134.refs_1_), channel_id=1, source_target_pairs={{0,16},{16,0},{1,17},{17,1},{2,18},{18,2},{3,19},{19,3},{4,20},{20... | collective-permute-start | bytes 1572872 | tf_op jit(solution)/shard_map/ppermute | solution.py:37
  250.6 8.2 %copy-start.24 = (bf16[4,4,1024]{2,1,0:T(4,128)(2,1)S(1)}, bf16[4,4,1024]{2,1,0:T(4,128)(2,1)}, u32[]{:S(2)}) copy-start(bf16[4,4,1024]{2,1,0:T(4,128)(2,1)} %get-tuple-element.145) | copy-start | bytes 98308
  258.9 18.7 %collective-permute-start.43 = (bf16[1,4,1024]{2,1,0:T(4,128)(2,1)S(1)}, bf16[1,4,1024]{2,1,0:T(4,128)(2,1)S(1)}, u32[]{:S(2)}, u32[]{:S(2)}) collective-permute-start(bf16[1,4,1024]{2,1,0:T(4,128)(2,1)S(1)} %broadcast_select_fusion.2), channel_id=1, source_target_pairs={{0,4},{4,0},{8,12},{12,8},{1,5},{5,1},{9,13},{13,9},{2,6},{6,2},{1... | collective-permute-start | bytes 24584 | tf_op jit(solution)/shard_map/ppermute | solution.py:37
  275.7 2.5 collective-permute-start.39
  275.7 3.6 %collective-permute-start.40 = (f32[2,384]{1,0:T(2,128)S(1)}, f32[2,384]{1,0:T(2,128)S(1)}, u32[]{:S(2)}, u32[]{:S(2)}) collective-permute-start(f32[2,384]{1,0:T(2,128)S(1)} %bitcast.107), channel_id=1, source_target_pairs={{0,2},{1,3},{2,0},{3,1},{4,6},{5,7},{6,4},{7,5},{8,10},{9,11},{10,... | collective-permute-start | bytes 9224 | tf_op jit(solution)/shard_map/ppermute | solution.py:37
  276.3 3.1 %collective-permute-start.41 = (f32[2,384]{1,0:T(2,128)S(1)}, f32[2,384]{1,0:T(2,128)S(1)}, u32[]{:S(2)}, u32[]{:S(2)}) collective-permute-start(f32[2,384]{1,0:T(2,128)S(1)} %bitcast.108), channel_id=1, source_target_pairs={{0,3},{1,2},{2,1},{3,0},{4,7},{5,6},{6,5},{7,4},{8,11},{9,10},{10,... | collective-permute-start | bytes 9224 | tf_op jit(solution)/shard_map/ppermute | solution.py:37
  (31 other events, 38.0 us)

commit v2 on v1

--- a/solution.py
+++ b/solution.py
@@ -38,8 +38,9 @@
 
 
 def project_kernel(plan, where_ref, *refs):
-    sources, cands, blocks, widths, begin, has_sum = plan
+    sources, tile_of, blocks, widths, begin, has_sum = plan
     arrays, refs = refs[:sources], refs[sources:]
+    cands = len(tile_of[0])
     weights, refs = refs[: blocks * len(widths)], refs[blocks * len(widths) :]
     before, refs = (refs[0], refs[1:]) if has_sum else (None, refs)
     out, tile_buf, weight_buf, sum_buf, tile_sem, weight_sem, sum_sem = refs
@@ -52,20 +53,23 @@
         off, column = where_ref[2 * block], where_ref[2 * block + 1]
         column = pl.multiple_of(column, depth)
         slot = lax.rem(item, slots)
-        for i in range(sources):
-
-            @pl.when(off == i)
-            def _():
-                pltpu.make_async_copy(
-                    arrays[i].at[tile, :, pl.ds(column, depth)], tile_buf.at[slot], tile_sem.at[slot]
-                ).start()
+        for i, row in enumerate(tile_of):
+            for j, (number, place) in enumerate(row):
+
+                @pl.when((off == i) & (tile == j))
+                def _():
+                    whole = arrays[number] if place is None else arrays[number].at[place]
+                    pltpu.make_async_copy(
+                        whole.at[:, pl.ds(column, depth)], tile_buf.at[slot], tile_sem.at[slot]
+                    ).start()
 
     copies = []
     for block in range(blocks):
         at = 0
+        copies.append([])
         for j, width in enumerate(widths):
             number = block * len(widths) + j
-            copies.append(
+            copies[-1].append(
                 pltpu.make_async_copy(
                     weights[number].at[0:depth, :],
                     weight_buf.at[block, :, at : at + width],
@@ -73,18 +77,17 @@
                 )
             )
             at += width
-    first = len(widths)
-    for copy in copies[:first]:
+    for copy in copies[0]:
         copy.start()
     for item in range(min(slots - 1, steps)):
         load(item)
     if has_sum:
         columns_of = before.at[:, :, begin : begin + columns]
-        copies.append(pltpu.make_async_copy(columns_of, sum_buf, sum_sem))
-    for copy in copies[first:]:
-        copy.start()
-    for copy in copies:
-        copy.wait()
+        sum_copy = pltpu.make_async_copy(columns_of, sum_buf, sum_sem)
+        sum_copy.start()
+    for block in copies[1:]:
+        for copy in block:
+            copy.start()
 
     def step(item, _):
         @pl.when(item + slots - 1 < steps)
@@ -93,8 +96,23 @@
 
         slot = lax.rem(item, slots)
         block, tile = item // cands, item % cands
+        for i in range(blocks):
+
+            @pl.when(item == i * cands)
+            def _():
+                for copy in copies[i]:
+                    copy.wait()
+
+        if has_sum:
+
+            @pl.when(item == 0)
+            def _():
+                sum_copy.wait()
+
         pltpu.make_async_copy(
-            arrays[0].at[0, :, pl.ds(0, depth)], tile_buf.at[slot], tile_sem.at[slot]
+            arrays[0].at[0, :, pl.ds(0, depth)] if tile_of[0][0][1] is not None else arrays[0].at[:, pl.ds(0, depth)],
+            tile_buf.at[slot],
+            tile_sem.at[slot],
         ).wait()
         term = jnp.dot(tile_buf[slot], weight_buf[block], preferred_element_type=f32)
         if has_sum:
@@ -116,6 +134,14 @@
 def project(pieces, numbers, depth, weights, before, begin, final):
     here = lax.axis_index("tensor")
     cands, tile_rows, width = pieces[0].shape
+    arrays, tile_of = [], []
+    for piece in pieces:
+        if isinstance(piece, list):
+            tile_of.append([(len(arrays) + c, None) for c in range(cands)])
+            arrays += piece
+        else:
+            tile_of.append([(len(arrays), c) for c in range(cands)])
+            arrays.append(piece)
     blocks = len(weights)
     widths = [w.shape[1] for w in weights[0]]
     columns = sum(widths)
@@ -125,8 +151,8 @@
         where += [(number // per_piece) ^ here, number % per_piece * depth]
     where = jnp.stack(where).astype(jnp.int32)
     flat = [w for block in weights for w in block]
-    operands = list(pieces) + flat + ([] if before is None else [before])
-    plan = (len(pieces), cands, blocks, widths, begin, before is not None)
+    operands = arrays + flat + ([] if before is None else [before])
+    plan = (len(arrays), tile_of, blocks, widths, begin, before is not None)
     slots = 3
     return pl.pallas_call(
         functools.partial(project_kernel, plan),
@@ -254,21 +280,14 @@
     )(scalars, queries, stored, stored, fresh, fresh, grades, so_far)
 
 
-def send_slots(placed, slots_here):
-    devices = lax.axis_size("cand")
-    here = lax.axis_index("cand")
-    bit = devices // 2
-    while bit:
-        half = bit * slots_here
-        low = (here & bit) == 0
-        first, second = placed[:half], placed[half:]
-        new = partner(jnp.where(low, second, first), "cand", bit)
-        placed = jnp.where(low, first, second) + new
-        bit //= 2
-    return placed
-
-
-def policy_rows(stored, extents, kept, everyone):
+def send_half(placed, slots_here, bit):
+    low = (lax.axis_index("cand") & bit) == 0
+    first, second = placed[: bit * slots_here], placed[bit * slots_here :]
+    new = partner(jnp.where(low, second, first), "cand", bit)
+    return jnp.where(low, first, second) + new
+
+
+def policy_rows(stored, stored_values, extents, kept, everyone):
     cand_here = stored.shape[0]
     device_here = lax.axis_index("cand")
     key_scale = HD ** (-0.5)
@@ -295,7 +314,7 @@
     living = living < jnp.take(extents, ids_here)[:, None]
     living = living[:, None, None, None, :]
     scores = (
-        jnp.einsum("cikgd,ctkd->ckgit", own_queries, stored[..., :HD], preferred_element_type=f32)
+        jnp.einsum("cikgd,ctkd->ckgit", own_queries, stored, preferred_element_type=f32)
         * key_scale
     )
     scores = jnp.where(living, scores, masked_value)
@@ -309,7 +328,7 @@
     fresh_weights = jnp.where(causal_new, jnp.exp(fresh_scores - peak_score[..., None]), 0.0)
     denominator = jnp.sum(old_weights, axis=-1) + jnp.sum(fresh_weights, axis=-1)
     numerator = jnp.einsum(
-        "ckgit,ctkd->ckgid", old_weights, stored[..., HD:], preferred_element_type=f32
+        "ckgit,ctkd->ckgid", old_weights, stored_values, preferred_element_type=f32
     )
     numerator = numerator + jnp.einsum(
         "ckgij,cjkd->ckgid", fresh_weights, own_fresh[..., HD:], preferred_element_type=f32
@@ -376,14 +395,17 @@
         for name, array in zip(names, touch([value[n] for n in names])):
             value[name] = array
 
-    value["own", 0] = response_latest_embeddings
+    each = range(cand_here)
+    for c in each:
+        value["own", 0, c] = response_latest_embeddings[c]
     bits = [1 << b for b in range(int(math.log2(tensor)) - 1, -1, -1)]
     held = [0]
     for bit in bits[:-1]:
         for off in list(held):
-            value["own", off ^ bit] = partner(value["own", off], "tensor", bit)
+            for c in each:
+                value["own", off ^ bit, c] = partner(value["own", off, c], "tensor", bit)
             held.append(off ^ bit)
-    value["own", 1] = partner(value["own", 0], "tensor", 1)
+    value["own", 1] = partner(response_latest_embeddings, "tensor", 1)
 
     wide = 2
     groups = [range(low, min(pairs, low + wide)) for low in range(0, pairs, wide)]
@@ -403,17 +425,18 @@
 
     def multiply(begin, end, names, before, column, final):
         weights = [[value[side, step, i] for side, i in names] for step in range(begin, end)]
-        pieces = [value["own", off] for off in range(tensor)]
+        pieces = [response_latest_embeddings, value["own", 1]]
+        pieces += [[value["own", off, c] for c in each] for off in range(2, tensor)]
         done = project(pieces, numbers[begin:end], depth, weights, before, column, final)
         return done.reshape(rows, -1) if final else done
 
     grades = grading_columns(critic_grading_vector)
     value["share"] = jnp.zeros((cand_here, 8, span_len), f32)
     near = [off for off in held if off]
-    def cross():
+    def cross(c, until):
         for off in near:
-            value["own", off ^ 1] = partner(value["own", off], "tensor", 1)
-        at(now + 1, *[("own", off ^ 1) for off in near])
+            value["own", off ^ 1, c] = partner(value["own", off, c], "tensor", 1)
+        at(until, *[("own", off ^ 1, c) for off in near])
 
     def policy_now():
         everyone = jnp.zeros((devices * slots.shape[0],) + slots.shape[1:], bf16)
@@ -422,7 +445,7 @@
             start = (place - step) % devices * slots.shape[0]
             everyone = lax.dynamic_update_slice(everyone, part, (start, 0, 0))
         value["policy"] = policy_rows(
-            actor_stored_pairs, filled_extents, kept_responses, everyone
+            value["actor", 0], value["actor", 1], filled_extents, kept_responses, everyone
         )
         at(now + 3, "policy")
 
@@ -447,7 +470,7 @@
     def keyval_now():
         names = [(side, i) for side in "wv" for i in range(pairs)]
         value["initial"] = multiply(0, devices, names, None, 0, True)
-        at(now + 2, "initial")
+        at(now + 1, "initial")
 
     def both(chosen):
         return [(side, i) for i in chosen for side in "wv"]
@@ -455,15 +478,25 @@
     def some_now(chosen, first, end):
         before = value.get(("sums", chosen))
         value["sums", chosen] = multiply(first, end, both(chosen), before, 0, False)
-        at(now + 2, ("sums", chosen))
-
-    def scores_now(chosen, part):
-        column = 2 * HD * chosen.index(part[0])
-        heads = both(part)
-        value["queries"] = multiply(last, devices, heads, value["sums", chosen], column, True)
-        score(value["queries"], 0, heads)
-        at(now + 3, "share")
-
+        at(min(now + 1, total + wide + lag - 1), ("sums", chosen))
+
+    def queries_now(chosen, i):
+        column = 2 * HD * chosen.index(i)
+        before = value["sums", chosen]
+        first = last if chosen is groups[-1] else min(2, last)
+        value["queries", i] = multiply(first, devices, both([i]), before, column, True)
+        at(now + 1, ("queries", i))
+
+    def score_now(i):
+        score(value["queries", i], 0, both([i]))
+        at(now + 1, "share")
+
+    def cache_now():
+        value["actor", 0] = actor_stored_pairs[..., :HD]
+        value["actor", 1] = actor_stored_pairs[..., HD:]
+        at(now + 2, ("actor", 0), ("actor", 1))
+
+    at(total + wide - 1, "policy")
     lag = 2
 
     def seen_at(step, i):
@@ -475,17 +508,22 @@
         if chosen[0] < pairs:
             continue
         end = chosen[-1]
-        if chosen is groups[-1]:
-            acts.append((seen_at(0, end), functools.partial(some_now, chosen, 0, 2)))
-            if last > 2:
-                acts.append((seen_at(last - 2, end), functools.partial(some_now, chosen, 2, last)))
-        else:
-            acts.append((seen_at(last - 2, end), functools.partial(some_now, chosen, 0, last)))
-            acts.append((seen_at(last - 1, end), functools.partial(scores_now, chosen, chosen)))
-    acts.append((min(8, total // 2), cross))
-    at(total + wide - 1, "policy")
+        ends = chosen is groups[-1]
+        acts.append((seen_at(0, end) + ends, functools.partial(some_now, chosen, 0, 2)))
+        if ends and last > 2:
+            when = max(seen_at(0, end) + 2, seen_at(last - 2, end))
+            acts.append((when, functools.partial(some_now, chosen, 2, last)))
+        if chosen is not groups[-1]:
+            for order, i in enumerate(chosen):
+                when = seen_at(last - 1, i) + order
+                acts.append((when, functools.partial(queries_now, chosen, i)))
+                acts.append((when + 1, functools.partial(score_now, i)))
+    acts.append((wide + 1, cache_now))
+    for c in each:
+        when = 7
+        at(when, *[("own", off, c) for off in near])
+        acts.append((when, functools.partial(cross, c, when + 2)))
     at(wide, ("own", 1))
-    at(min(8, total // 2), *[("own", off) for off in near])
     for now in range(total + wide + lag):
         names = []
         if 0 <= now - wide < total:
@@ -511,8 +549,13 @@
     for i in chosen:
         if i != chosen[0]:
             gate(("w", last, i), ("v", last, i), "share")
-        scores_now(chosen, [i])
-    slot_rows = send_slots(value["policy"], slots.shape[0])
+        queries_now(chosen, i)
+        score_now(i)
+    bit = devices // 2
+    slot_rows = value["policy"]
+    while bit:
+        slot_rows = send_half(slot_rows, slots.shape[0], bit)
+        bit //= 2
     share = value["share"]
     share = share[:, 0, :]
     terms = [share] + [partner(share, "tensor", bits) for bits in range(1, tensor)]

time: 281 us -> 272 us (0.968)
  waiting for transfers between devices: 96.3 us -> 88.4 us
  starting transfers between devices: 41.5 us -> 36.9 us
  Pallas kernels: 88.9 us -> 92.3 us
    ppermute x18, waiting for transfers between devices: 93.4 us -> 59.4 us  [shifted(): lax.ppermute(value, axis, [(i, (i + step) % size) for i in range(size)])]
    ppermute x26 -> x28, waiting for transfers between devices: 2.88 us -> 29 us  [partner(): return lax.ppermute(value, axis, [(i, i ^ bits) for i in range(size)])]
    ppermute x18, starting transfers between devices: 11.5 us -> 5.91 us  [shifted(): lax.ppermute(value, axis, [(i, (i + step) % size) for i in range(size)])]
    unnamed x72 -> x80, local copies, waits for them, and re-layouts: 18.4 us -> 15.5 us
    pallas_call x3 -> x4, Pallas kernels: 30.2 us -> 32.7 us  [reward_share(): pl.pallas_call(reward_kernel, grid_spec=spec, out_shape=jax.ShapeDtypeStr...]
    ppermute x26 -> x28, starting transfers between devices: 30 us -> 31 us  [partner(): return lax.ppermute(value, axis, [(i, i ^ bits) for i in range(size)])]
    pallas_call x7 -> x8, Pallas kernels: 58.7 us -> 59.6 us  [project(): pl.pallas_call(functools.partial(project_kernel, plan), in_specs=[pl.Bloc...]
  transfers between devices with their start and end apart: 44 -> 46, of which waited for: 16 -> 26; matrix products, arithmetic and copies ran while one was open for 12% -> 14% of each run, Pallas kernels for 32% -> 34%
where the time goes in v2:
time: 272 us
  Pallas kernels  92.3 us (34%)
  waiting for transfers between devices  88.4 us (32%)
  local copies, waits for them, and re-layouts  41.3 us (15%)
  starting transfers between devices  36.9 us (14%)
  other arithmetic  7.22 us (3%)
  matrix products  4.11 us (2%)
    pallas_call x8, Pallas kernels, project(): pl.pallas_call(functools.partial(project_kernel, plan), in_specs=[pl.Bloc...  59.6 us
    ppermute x18, waiting for transfers between devices, shifted(): lax.ppermute(value, axis, [(i, (i + step) % size) for i in range(size)])  59.4 us
    pallas_call x4, Pallas kernels, reward_share(): pl.pallas_call(reward_kernel, grid_spec=spec, out_shape=jax.ShapeDtypeStr...  32.7 us
    ppermute x28, starting transfers between devices, partner(): return lax.ppermute(value, axis, [(i, i ^ bits) for i in range(size)])  31 us
    ppermute x28, waiting for transfers between devices, partner(): return lax.ppermute(value, axis, [(i, i ^ bits) for i in range(size)])  29 us
    unnamed x80, local copies, waits for them, and re-layouts  15.5 us
    slice x1, local copies, waits for them, and re-layouts, cache_now(): value['actor', 1] = actor_stored_pairs[..., HD:]  6.08 us
    ppermute x18, starting transfers between devices, shifted(): lax.ppermute(value, axis, [(i, (i + step) % size) for i in range(size)])  5.91 us
  transfers between devices with their start and end apart: 46, of which 26 were waited for; matrix products, arithmetic and copies ran while one was open for 14% of the time, Pallas kernels for 34%

profile of v2, /device:TPU:0, one launch (start us, length us, event | category | flops | bytes accessed | tf_op | source)
XLA Modules:
  0.0 271.5 jit_solution(667803438145649274)
XLA Ops:
  2.6 3.0 %constant_dynamic-slice_fusion.9 = (bf16[2048,128]{1,0:T(8,128)(2,1)}, bf16[2048,128]{1,0:T(8,128)(2,1)}, bf16[2048,128]{1,0:T(8,128)(2,1)S(1)}, bf16[2048,128]{1,0:T(8,128)(2,1)}) fusion(bf16[2048,512]{1,0:T(8,128)(2,1)} %param.12, s32[]{:T(128)S(6)} %add.409, s32[]{:T(128)S(6)} %select_n.409, s32[]{:T(128)S(6)} %select_n.388, s32[]{:T(128)S(6)} %add.407), kind=kLoop, calls=%fused_computation.57 | loop fusion | bytes 4194320 | tf_op jit(solution)/shard_map/slice | solution.py:378
  6.4 2.6 collective-permute-start
  9.0 1.6 collective-permute-start.2
  10.6 2.0 slice_bitcast_fusion
  15.5 6.1 %fusion.40 = (bf16[2,2048,2,128]{3,2,1,0:T(2,128)(2,1)}, bf16[2,2048,2,128]{3,2,1,0:T(2,128)(2,1)}) fusion(bf16[2,2048,2,256]{3,2,1,0:T(2,128)(2,1)} %param.15), kind=kLoop, calls=%fused_computation.94 | loop fusion | bytes 8388608 | tf_op jit(solution)/shard_map/slice | solution.py:496
  22.4 1.9 collective-permute-done.refs_1_
  26.0 4.3 %constant_dynamic-slice_fusion.8 = (bf16[2048,128]{1,0:T(8,128)(2,1)}, bf16[2048,128]{1,0:T(8,128)(2,1)}, bf16[2048,128]{1,0:T(8,128)(2,1)}, bf16[2048,128]{1,0:...) fusion(bf16[2048,1024]{1,0:T(8,128)(2,1)} %param.11, ...), kind=kLoop, calls=%fused_computation.56 | loop fusion | bytes 8388640 | tf_op jit(solution)/shard_map/slice | solution.py:379
  30.4 1.7 collective-permute-start.4
  32.0 3.6 %collective-permute-done.2.refs_1_ = bf16[2048,128]{1,0:T(8,128)(2,1)} collective-permute-done((bf16[2048,128]{1,0:T(8,128)(2,1)}, bf16[2048,128]{1,0:T(8,128)(2,1)}, u32[]{:S(2)}, u32[]{:S(2)}) %collective-permute-start.2) | collective-permute-done | bytes 524320 | tf_op jit(solution)/shard_map/ppermute | solution.py:32
  35.7 11.3 %collective-permute-done.3.refs_1_ = bf16[2096,128]{1,0:T(8,128)(2,1)S(1)} collective-permute-done((bf16[2096,128]{1,0:T(8,128)(2,1)}, bf16[2096,128]{1,0:T(8,128)(2,1)S(1)}, u32[]{:S(2)}, u32[]{:S(2)}) %collective-permute-start.3) | collective-permute-done | bytes 536608 | tf_op jit(solution)/shard_map/ppermute | solution.py:32
  47.0 1.7 collective-permute-start.6
  49.5 8.8 %collective-permute-done.5.refs_1_ = bf16[2048,128]{1,0:T(8,128)(2,1)S(1)} collective-permute-done((bf16[2048,128]{1,0:T(8,128)(2,1)}, bf16[2048,128]{1,0:T(8,128)(2,1)S(1)}, u32[]{:S(2)}, u32[]{:S(2)}) %collective-permute-start.5) | collective-permute-done | bytes 524320 | tf_op jit(solution)/shard_map/ppermute | solution.py:32
  58.2 1.7 collective-permute-start.8
  63.0 6.6 %collective-permute-done.7.refs_1_ = bf16[2096,128]{1,0:T(8,128)(2,1)S(1)} collective-permute-done((bf16[2096,128]{1,0:T(8,128)(2,1)}, bf16[2096,128]{1,0:T(8,128)(2,1)S(1)}, u32[]{:S(2)}, u32[]{:S(2)}) %collective-permute-start.7) | collective-permute-done | bytes 536608 | tf_op jit(solution)/shard_map/ppermute | solution.py:32
  69.5 4.0 %collective-permute-done.8.refs_2_ = bf16[2096,128]{1,0:T(8,128)(2,1)S(1)} collective-permute-done((bf16[2096,128]{1,0:T(8,128)(2,1)}, bf16[2096,128]{1,0:T(8,128)(2,1)S(1)}, u32[]{:S(2)}, u32[]{:S(2)}) %collective-permute-start.8) | collective-permute-done | bytes 536608 | tf_op jit(solution)/shard_map/ppermute | solution.py:37
  75.0 1.7 collective-permute-start.14
  77.5 5.3 %collective-permute-done.12.refs_5_ = bf16[384,2048]{1,0:T(8,128)(2,1)} collective-permute-done((bf16[384,2048]{1,0:T(8,128)(2,1)}, bf16[384,2048]{1,0:T(8,128)(2,1)}, u32[]{:S(2)}, u32[]{:S(2)}) %collective-permute-start.12) | collective-permute-done | bytes 1572896 | tf_op jit(solution)/shard_map/ppermute | solution.py:37
  82.9 1.9 collective-permute-done.10.refs_2_
  84.8 1.7 collective-permute-done.9.refs_1_
  87.0 2.6 fusion.41
  90.7 6.9 %collective-permute-done.13.refs_1_ = bf16[2048,128]{1,0:T(8,128)(2,1)S(1)} collective-permute-done((bf16[2048,128]{1,0:T(8,128)(2,1)}, bf16[2048,128]{1,0:T(8,128)(2,1)S(1)}, u32[]{:S(2)}, u32[]{:S(2)}) %collective-permute-start.13) | collective-permute-done | bytes 524320 | tf_op jit(solution)/shard_map/ppermute | solution.py:32
  97.6 1.5 collective-permute-start.16
  100.8 8.2 %collective-permute-done.15.refs_1_ = bf16[2048,128]{1,0:T(8,128)(2,1)} collective-permute-done((bf16[2048,128]{1,0:T(8,128)(2,1)}, bf16[2048,128]{1,0:T(8,128)(2,1)}, u32[]{:S(2)}, u32[]{:S(2)}) %collective-permute-start.15) | collective-permute-done | bytes 524320 | tf_op jit(solution)/shard_map/ppermute | solution.py:32
  108.9 1.5 collective-permute-start.20
  112.6 13.1 %project.8 = bf16[2,384,512]{2,1,0:T(8,128)(2,1)} custom-call(s32[8]{0:T(128)} %stack.178.where_ref, bf16[2,384,2048]{2,1,0:T(8,128)(2,1)} %refs_0_.15, bf16[2,384,2048]{2,1,0:T(8,128)(2,1)} %get-tuple-element.81.refs_1_, bf16[384,2048]{1,0:T(8,128)(2,1)} %get-tuple-element.91.refs_2_, bf16[384,2048]{1,0:T(8,128)(2,1)} %get-tuple-element.92.refs_3_, ...), custom_call_target="tpu_custom_call" | custom-call | flops 6442450944 | bytes 12582912 | tf_op jit(solution)/shard_map/project/pallas_call | solution.py:157
  128.8 2.5 collective-permute-done.21.refs_1_
  131.3 3.9 %collective-permute-done.22.refs_2_ = bf16[2048,128]{1,0:T(8,128)(2,1)S(1)} collective-permute-done((bf16[2048,128]{1,0:T(8,128)(2,1)}, bf16[2048,128]{1,0:T(8,128)(2,1)S(1)}, u32[]{:S(2)}, u32[]{:S(2)}) %collective-permute-start.22) | collective-permute-done | bytes 524320 | tf_op jit(solution)/shard_map/ppermute | solution.py:37
  136.0 1.5 collective-permute-start.26
  137.6 8.1 %project.9.refs_4_ = f32[2,384,512]{2,1,0:T(8,128)} custom-call(s32[4]{0:T(128)} %pad_add_fusion.3.where_ref, bf16[2,384,2048]{2,1,0:T(8,128)(2,1)} %refs_0_.15, bf16[2,384,2048]{2,1,0:T(8,128)(2,1)} %get-tuple-element.81.refs_1_, bf16[384,2048]{1,0:T(8,128)(2,1)} %get-tuple-element.91.refs_2_, bf16[384,2048]{1,0:T(8,128)(2,1)} %get-tuple-element.92.refs_3_, ...), custom_call_target="tpu_custom_call" | custom-call | flops 3221225472 | bytes 6291456 | tf_op jit(solution)/shard_map/project/pallas_call | solution.py:157
  148.8 6.2 %collective-permute-done.25.refs_1_ = bf16[2048,128]{1,0:T(8,128)(2,1)S(1)} collective-permute-done((bf16[2048,128]{1,0:T(8,128)(2,1)}, bf16[2048,128]{1,0:T(8,128)(2,1)S(1)}, u32[]{:S(2)}, u32[]{:S(2)}) %collective-permute-start.25) | collective-permute-done | bytes 524320 | tf_op jit(solution)/shard_map/ppermute | solution.py:32
  155.0 2.7 collective-permute-done.26.refs_2_
  164.4 1.8 collective-permute-done.27.refs_1_
  166.2 2.7 collective-permute-done.28.refs_2_
  169.7 1.5 collective-permute-start.32
  171.9 6.7 %project.10 = bf16[2,384,256]{2,1,0:T(8,128)(2,1)} custom-call(s32[4]{0:T(128)} %pad_add_fusion.2.where_ref, bf16[2,384,2048]{2,1,0:T(8,128)(2,1)} %refs_0_.15, bf16[2,384,2048]{2,1,0:T(8,128)(2,1)} %get-tuple-element.81.refs_1_, bf16[384,2048]{1,0:T(8,128)(2,1)} %get-tuple-element.91.refs_2_, bf16[384,2048]{1,0:T(8,128)(2,1)} %get-tuple-element.92.refs_3_, ...), custom_call_target="tpu_custom_call" | custom-call | flops 1610612736 | bytes 6291456 | tf_op jit(solution)/shard_map/project/pallas_call | solution.py:157
  178.6 1.5 collective-permute-done.30.refs_2_
  181.0 1.5 collective-permute-start.34
  183.1 8.2 %reward_share.4.refs_3_ = f32[2,8,384]{2,1,0:T(8,128)} custom-call(s32[8]{0:T(128)} %stack.189.kg_ref, bf16[768,256]{1,0:T(8,128)(2,1)} %get-tuple-element.130.q_ref, bf16[2,2048,512]{2,1,0:T(8,128)(2,1)} %old_value_ref.7, bf16[2,2048,512]{2,1,0:T(8,128)(2,1)} %old_value_ref.7, bf16[768,512]{1,0:T(8,128)(2,1)} %get-tuple-element.131.key_ref.value_ref, ...), custom_call_target="tpu_custom_call" | custom-call | flops 2868903936 | bytes 8388608 | tf_op jit(solution)/shard_map/reward_share/pallas_call | solution.py:271
  194.4 6.7 %project.11 = bf16[2,384,256]{2,1,0:T(8,128)(2,1)} custom-call(s32[4]{0:T(128)} %pad_add_fusion.2.where_ref, bf16[2,384,2048]{2,1,0:T(8,128)(2,1)} %refs_0_.15, bf16[2,384,2048]{2,1,0:T(8,128)(2,1)} %get-tuple-element.81.refs_1_, bf16[384,2048]{1,0:T(8,128)(2,1)} %get-tuple-element.91.refs_2_, bf16[384,2048]{1,0:T(8,128)(2,1)} %get-tuple-element.92.refs_3_, ...), custom_call_target="tpu_custom_call" | custom-call | flops 1610612736 | bytes 6291456 | tf_op jit(solution)/shard_map/project/pallas_call | solution.py:157
  201.1 1.6 collective-permute-done.34.refs_2_
  205.1 8.2 %reward_share.5.refs_3_ = f32[2,8,384]{2,1,0:T(8,128)} custom-call(s32[8]{0:T(128)} %stack.198.kg_ref, bf16[768,256]{1,0:T(8,128)(2,1)} %get-tuple-element.138.q_ref, bf16[2,2048,512]{2,1,0:T(8,128)(2,1)} %old_value_ref.7, bf16[2,2048,512]{2,1,0:T(8,128)(2,1)} %old_value_ref.7, bf16[768,512]{1,0:T(8,128)(2,1)} %get-tuple-element.131.key_ref.value_ref, ...), custom_call_target="tpu_custom_call" | custom-call | flops 2868903936 | bytes 8388608 | tf_op jit(solution)/shard_map/reward_share/pallas_call | solution.py:271
  214.7 1.5 collective-permute-start.39
  216.2 8.0 %project.12.refs_4_ = f32[2,384,512]{2,1,0:T(8,128)} custom-call(s32[4]{0:T(128)} %pad_add_fusion.3.where_ref, bf16[2,384,2048]{2,1,0:T(8,128)(2,1)} %refs_0_.15, bf16[2,384,2048]{2,1,0:T(8,128)(2,1)} %get-tuple-element.81.refs_1_, bf16[384,2048]{1,0:T(8,128)(2,1)} %get-tuple-element.91.refs_2_, bf16[384,2048]{1,0:T(8,128)(2,1)} %get-tuple-element.92.refs_3_, ...), custom_call_target="tpu_custom_call" | custom-call | flops 3221225472 | bytes 6291456 | tf_op jit(solution)/shard_map/project/pallas_call | solution.py:157
  228.4 6.9 %project.13.refs_8_ = f32[2,384,512]{2,1,0:T(8,128)} custom-call(s32[2]{0:T(128)} %pad_add_fusion.where_ref, bf16[2,384,2048]{2,1,0:T(8,128)(2,1)} %refs_0_.15, bf16[2,384,2048]{2,1,0:T(8,128)(2,1)} %get-tuple-element.81.refs_1_, bf16[384,2048]{1,0:T(8,128)(2,1)} %get-tuple-element.91.refs_2_, bf16[384,2048]{1,0:T(8,128)(2,1)} %get-tuple-element.92.refs_3_, ...), custom_call_target="tpu_custom_call" | custom-call | flops 1610612736 | bytes 3145728 | tf_op jit(solution)/shard_map/project/pallas_call | solution.py:157
  237.1 5.1 %project.14 = bf16[2,384,256]{2,1,0:T(8,128)(2,1)} custom-call(s32[2]{0:T(128)} %pad_add_fusion.1.where_ref, bf16[2,384,2048]{2,1,0:T(8,128)(2,1)} %refs_0_.15, bf16[2,384,2048]{2,1,0:T(8,128)(2,1)} %get-tuple-element.81.refs_1_, bf16[384,2048]{1,0:T(8,128)(2,1)} %get-tuple-element.91.refs_2_, bf16[384,2048]{1,0:T(8,128)(2,1)} %get-tuple-element.92.refs_3_, ...), custom_call_target="tpu_custom_call" | custom-call | flops 805306368 | bytes 3145728 | tf_op jit(solution)/shard_map/project/pallas_call | solution.py:157
  242.2 8.2 %reward_share.6.refs_3_ = f32[2,8,384]{2,1,0:T(8,128)} custom-call(s32[8]{0:T(128)} %stack.207.kg_ref, bf16[768,256]{1,0:T(8,128)(2,1)} %bitcast.100, bf16[2,2048,512]{2,1,0:T(8,128)(2,1)} %old_value_ref.7, bf16[2,2048,512]{2,1,0:T(8,128)(2,1)} %old_value_ref.7, bf16[768,512]{1,0:T(8,128)(2,1)} %get-tuple-element.131.key_ref.value_ref, ...), custom_call_target="tpu_custom_call" | custom-call | flops 2868903936 | bytes 8388608 | tf_op jit(solution)/shard_map/reward_share/pallas_call | solution.py:271
  252.5 5.1 %project.15 = bf16[2,384,256]{2,1,0:T(8,128)(2,1)} custom-call(s32[2]{0:T(128)} %pad_add_fusion.1.where_ref, bf16[2,384,2048]{2,1,0:T(8,128)(2,1)} %refs_0_.15, bf16[2,384,2048]{2,1,0:T(8,128)(2,1)} %get-tuple-element.81.refs_1_, bf16[384,2048]{1,0:T(8,128)(2,1)} %get-tuple-element.91.refs_2_, bf16[384,2048]{1,0:T(8,128)(2,1)} %get-tuple-element.92.refs_3_, ...), custom_call_target="tpu_custom_call" | custom-call | flops 805306368 | bytes 3145728 | tf_op jit(solution)/shard_map/project/pallas_call | solution.py:157
  257.6 8.2 %reward_share.7 = f32[2,8,384]{2,1,0:T(8,128)} custom-call(s32[8]{0:T(128)} %stack.172.kg_ref, bf16[768,256]{1,0:T(8,128)(2,1)} %bitcast.99, bf16[2,2048,512]{2,1,0:T(8,128)(2,1)} %old_value_ref.7, bf16[2,2048,512]{2,1,0:T(8,128)(2,1)} %old_value_ref.7, bf16[768,512]{1,0:T(8,128)(2,1)} %get-tuple-element.131.key_ref.value_ref, ...), custom_call_target="tpu_custom_call" | custom-call | flops 2868903936 | bytes 8388608 | tf_op jit(solution)/shard_map/reward_share/pallas_call | solution.py:271
  (223 shorter events, 56.8 us)
Async XLA Ops:
  0.6 14.2 %copy-start = (s32[8]{0:T(128)S(1)}, s32[8]{0:T(128)}, u32[]{:S(2)}) copy-start(s32[8]{0:T(128)} %param.16) | copy-start | bytes 100
  0.6 23.7 %collective-permute-start.1 = (bf16[2,384,2048]{2,1,0:T(8,128)(2,1)}, bf16[2,384,2048]{2,1,0:T(8,128)(2,1)S(1)}, u32[]{:S(2)}, u32[]{:S(2)}) collective-permute-start(bf16[2,384,2048]{2,1,0:T(8,128)(2,1)} %refs_0_.15), channel_id=1, source_target_pairs={{0,1},{1,0},{2,3},{3,2},{4,5},{5,4},{6,7},{7,6},{8,9},{9,8},{10,11... | collective-permute-start | bytes 9437192 | tf_op jit(solution)/shard_map/ppermute | solution.py:37
  6.4 18.0 %collective-permute-start = (bf16[2096,128]{1,0:T(8,128)(2,1)}, bf16[2096,128]{1,0:T(8,128)(2,1)}, u32[]{:S(2)}, u32[]{:S(2)}) collective-permute-start(bf16[2096,128]{1,0:T(8,128)(2,1)} %pad_maximum_fusion.refs_6_), channel_id=1, source_target_pairs={{0,4},{4,8},{8,12},{12,0},{1,5},{5,9},{9,13},{13,1},{2,6},{6,10},{... | collective-permute-start | bytes 1609736 | tf_op jit(solution)/shard_map/ppermute | solution.py:32
  9.0 26.6 %collective-permute-start.2 = (bf16[2048,128]{1,0:T(8,128)(2,1)}, bf16[2048,128]{1,0:T(8,128)(2,1)}, u32[]{:S(2)}, u32[]{:S(2)}) collective-permute-start(bf16[2048,128]{1,0:T(8,128)(2,1)} %get-tuple-element.175.refs_7_), channel_id=1, source_target_pairs={{0,4},{4,8},{8,12},{12,0},{1,5},{5,9},{9,13},{13,1},{2,6},{6,10},{... | collective-permute-start | bytes 1572872 | tf_op jit(solution)/shard_map/ppermute | solution.py:32
  12.6 64.8 %collective-permute-start.11 = (bf16[384,2048]{1,0:T(8,128)(2,1)}, bf16[384,2048]{1,0:T(8,128)(2,1)}, u32[]{:S(2)}, u32[]{:S(2)}) collective-permute-start(bf16[384,2048]{1,0:T(8,128)(2,1)} %get-tuple-element.171), channel_id=1, source_target_pairs={{0,2},{1,3},{2,0},{3,1},{4,6},{5,7},{6,4},{7,5},{8,10},{9,11},{10,... | collective-permute-start | bytes 4718600 | tf_op jit(solution)/shard_map/ppermute | solution.py:37
  14.1 68.8 %collective-permute-start.12 = (bf16[384,2048]{1,0:T(8,128)(2,1)}, bf16[384,2048]{1,0:T(8,128)(2,1)}, u32[]{:S(2)}, u32[]{:S(2)}) collective-permute-start(bf16[384,2048]{1,0:T(8,128)(2,1)} %get-tuple-element.170), channel_id=1, source_target_pairs={{0,2},{1,3},{2,0},{3,1},{4,6},{5,7},{6,4},{7,5},{8,10},{9,11},{10,... | collective-permute-start | bytes 4718600 | tf_op jit(solution)/shard_map/ppermute | solution.py:37
  26.0 21.0 %collective-permute-start.3 = (bf16[2096,128]{1,0:T(8,128)(2,1)}, bf16[2096,128]{1,0:T(8,128)(2,1)S(1)}, u32[]{:S(2)}, u32[]{:S(2)}) collective-permute-start(bf16[2096,128]{1,0:T(8,128)(2,1)} %get-tuple-element.84.refs_10_), channel_id=1, source_target_pairs={{0,4},{4,8},{8,12},{12,0},{1,5},{5,9},{9,13},{13,1},{2,6},{6,10},{... | collective-permute-start | bytes 1609736 | tf_op jit(solution)/shard_map/ppermute | solution.py:32
  30.4 18.3 %collective-permute-start.4 = (bf16[2096,128]{1,0:T(8,128)(2,1)}, bf16[2096,128]{1,0:T(8,128)(2,1)S(1)}, u32[]{:S(2)}, u32[]{:S(2)}) collective-permute-start(bf16[2096,128]{1,0:T(8,128)(2,1)} %get-tuple-element.84.refs_10_), channel_id=1, source_target_pairs={{0,16},{16,0},{1,17},{17,1},{2,18},{18,2},{3,19},{19,3},{4,20},{20... | collective-permute-start | bytes 1609736 | tf_op jit(solution)/shard_map/ppermute | solution.py:37
  35.6 22.6 %collective-permute-start.5 = (bf16[2048,128]{1,0:T(8,128)(2,1)}, bf16[2048,128]{1,0:T(8,128)(2,1)S(1)}, u32[]{:S(2)}, u32[]{:S(2)}) collective-permute-start(bf16[2048,128]{1,0:T(8,128)(2,1)} %get-tuple-element.86.refs_11_), channel_id=1, source_target_pairs={{0,4},{4,8},{8,12},{12,0},{1,5},{5,9},{9,13},{13,1},{2,6},{6,10},{... | collective-permute-start | bytes 1572872 | tf_op jit(solution)/shard_map/ppermute | solution.py:32
  47.0 14.4 %collective-permute-start.6 = (bf16[2048,128]{1,0:T(8,128)(2,1)}, bf16[2048,128]{1,0:T(8,128)(2,1)S(1)}, u32[]{:S(2)}, u32[]{:S(2)}) collective-permute-start(bf16[2048,128]{1,0:T(8,128)(2,1)} %get-tuple-element.86.refs_11_), channel_id=1, source_target_pairs={{0,16},{16,0},{1,17},{17,1},{2,18},{18,2},{3,19},{19,3},{4,20},{20... | collective-permute-start | bytes 1572872 | tf_op jit(solution)/shard_map/ppermute | solution.py:37
  49.5 20.1 %collective-permute-start.7 = (bf16[2096,128]{1,0:T(8,128)(2,1)}, bf16[2096,128]{1,0:T(8,128)(2,1)S(1)}, u32[]{:S(2)}, u32[]{:S(2)}) collective-permute-start(bf16[2096,128]{1,0:T(8,128)(2,1)} %get-tuple-element.88.refs_14_), channel_id=1, source_target_pairs={{0,4},{4,8},{8,12},{12,0},{1,5},{5,9},{9,13},{13,1},{2,6},{6,10},{... | collective-permute-start | bytes 1609736 | tf_op jit(solution)/shard_map/ppermute | solution.py:32
  58.2 15.3 %collective-permute-start.8 = (bf16[2096,128]{1,0:T(8,128)(2,1)}, bf16[2096,128]{1,0:T(8,128)(2,1)S(1)}, u32[]{:S(2)}, u32[]{:S(2)}) collective-permute-start(bf16[2096,128]{1,0:T(8,128)(2,1)} %get-tuple-element.88.refs_14_), channel_id=1, source_target_pairs={{0,16},{16,0},{1,17},{17,1},{2,18},{18,2},{3,19},{19,3},{4,20},{20... | collective-permute-start | bytes 1609736 | tf_op jit(solution)/shard_map/ppermute | solution.py:37
  62.2 22.6 %collective-permute-start.10 = (bf16[2048,128]{1,0:T(8,128)(2,1)}, bf16[2048,128]{1,0:T(8,128)(2,1)S(1)}, u32[]{:S(2)}, u32[]{:S(2)}) collective-permute-start(bf16[2048,128]{1,0:T(8,128)(2,1)} %get-tuple-element.90.refs_15_), channel_id=1, source_target_pairs={{0,16},{16,0},{1,17},{17,1},{2,18},{18,2},{3,19},{19,3},{4,20},{20... | collective-permute-start | bytes 1572872 | tf_op jit(solution)/shard_map/ppermute | solution.py:37
  69.5 16.9 %collective-permute-start.9 = (bf16[2048,128]{1,0:T(8,128)(2,1)}, bf16[2048,128]{1,0:T(8,128)(2,1)}, u32[]{:S(2)}, u32[]{:S(2)}) collective-permute-start(bf16[2048,128]{1,0:T(8,128)(2,1)} %get-tuple-element.90.refs_15_), channel_id=1, source_target_pairs={{0,4},{4,8},{8,12},{12,0},{1,5},{5,9},{9,13},{13,1},{2,6},{6,10},{... | collective-permute-start | bytes 1572872 | tf_op jit(solution)/shard_map/ppermute | solution.py:32
  75.0 25.7 %collective-permute-start.14 = (bf16[2096,128]{1,0:T(8,128)(2,1)}, bf16[2096,128]{1,0:T(8,128)(2,1)}, u32[]{:S(2)}, u32[]{:S(2)}) collective-permute-start(bf16[2096,128]{1,0:T(8,128)(2,1)} %get-tuple-element.95.refs_18_), channel_id=1, source_target_pairs={{0,16},{16,0},{1,17},{17,1},{2,18},{18,2},{3,19},{19,3},{4,20},{20... | collective-permute-start | bytes 1609736 | tf_op jit(solution)/shard_map/ppermute | solution.py:37
  77.5 20.1 %collective-permute-start.13 = (bf16[2048,128]{1,0:T(8,128)(2,1)}, bf16[2048,128]{1,0:T(8,128)(2,1)S(1)}, u32[]{:S(2)}, u32[]{:S(2)}) collective-permute-start(bf16[2048,128]{1,0:T(8,128)(2,1)} %get-tuple-element.94.refs_6_), channel_id=1, source_target_pairs={{0,4},{4,8},{8,12},{12,0},{1,5},{5,9},{9,13},{13,1},{2,6},{6,10},{... | collective-permute-start | bytes 1572872 | tf_op jit(solution)/shard_map/ppermute | solution.py:32
  86.5 24.0 %collective-permute-start.17 = (bf16[384,2048]{1,0:T(8,128)(2,1)}, bf16[384,2048]{1,0:T(8,128)(2,1)S(1)}, u32[]{:S(2)}, u32[]{:S(2)}) collective-permute-start(bf16[384,2048]{1,0:T(8,128)(2,1)} %get-tuple-element.91.refs_2_), channel_id=1, source_target_pairs={{0,1},{1,0},{2,3},{3,2},{4,5},{5,4},{6,7},{7,6},{8,9},{9,8},{10,11... | collective-permute-start | bytes 4718600 | tf_op jit(solution)/shard_map/ppermute | solution.py:37
  86.5 24.0 %collective-permute-start.18 = (bf16[384,2048]{1,0:T(8,128)(2,1)}, bf16[384,2048]{1,0:T(8,128)(2,1)S(1)}, u32[]{:S(2)}, u32[]{:S(2)}) collective-permute-start(bf16[384,2048]{1,0:T(8,128)(2,1)} %get-tuple-element.92.refs_3_), channel_id=1, source_target_pairs={{0,1},{1,0},{2,3},{3,2},{4,5},{5,4},{6,7},{7,6},{8,9},{9,8},{10,11... | collective-permute-start | bytes 4718600 | tf_op jit(solution)/shard_map/ppermute | solution.py:37
  87.0 22.0 %collective-permute-start.15 = (bf16[2048,128]{1,0:T(8,128)(2,1)}, bf16[2048,128]{1,0:T(8,128)(2,1)}, u32[]{:S(2)}, u32[]{:S(2)}) collective-permute-start(bf16[2048,128]{1,0:T(8,128)(2,1)} %get-tuple-element.97.refs_8_), channel_id=1, source_target_pairs={{0,4},{4,8},{8,12},{12,0},{1,5},{5,9},{9,13},{13,1},{2,6},{6,10},{... | collective-permute-start | bytes 1572872 | tf_op jit(solution)/shard_map/ppermute | solution.py:32
  97.6 12.9 %collective-permute-start.16 = (bf16[2048,128]{1,0:T(8,128)(2,1)}, bf16[2048,128]{1,0:T(8,128)(2,1)}, u32[]{:S(2)}, u32[]{:S(2)}) collective-permute-start(bf16[2048,128]{1,0:T(8,128)(2,1)} %get-tuple-element.98.refs_19_), channel_id=1, source_target_pairs={{0,16},{16,0},{1,17},{17,1},{2,18},{18,2},{3,19},{19,3},{4,20},{20... | collective-permute-start | bytes 1572872 | tf_op jit(solution)/shard_map/ppermute | solution.py:37
  100.8 25.0 %collective-permute-start.19 = (bf16[2048,128]{1,0:T(8,128)(2,1)}, bf16[2048,128]{1,0:T(8,128)(2,1)S(1)}, u32[]{:S(2)}, u32[]{:S(2)}) collective-permute-start(bf16[2048,128]{1,0:T(8,128)(2,1)} %get-tuple-element.104.refs_10_), channel_id=1, source_target_pairs={{0,4},{4,8},{8,12},{12,0},{1,5},{5,9},{9,13},{13,1},{2,6},{6,10},{... | collective-permute-start | bytes 1572872 | tf_op jit(solution)/shard_map/ppermute | solution.py:32
  108.9 16.8 %collective-permute-start.20 = (bf16[2048,128]{1,0:T(8,128)(2,1)}, bf16[2048,128]{1,0:T(8,128)(2,1)}, u32[]{:S(2)}, u32[]{:S(2)}) collective-permute-start(bf16[2048,128]{1,0:T(8,128)(2,1)} %get-tuple-element.104.refs_10_), channel_id=1, source_target_pairs={{0,16},{16,0},{1,17},{17,1},{2,18},{18,2},{3,19},{19,3},{4,20},{20... | collective-permute-start | bytes 1572872 | tf_op jit(solution)/shard_map/ppermute | solution.py:37
  112.1 19.1 %collective-permute-start.21 = (bf16[2048,128]{1,0:T(8,128)(2,1)}, bf16[2048,128]{1,0:T(8,128)(2,1)S(1)}, u32[]{:S(2)}, u32[]{:S(2)}) collective-permute-start(bf16[2048,128]{1,0:T(8,128)(2,1)} %get-tuple-element.112.refs_12_), channel_id=1, source_target_pairs={{0,4},{4,8},{8,12},{12,0},{1,5},{5,9},{9,13},{13,1},{2,6},{6,10},{... | collective-permute-start | bytes 1572872 | tf_op jit(solution)/shard_map/ppermute | solution.py:32
  112.2 23.1 %collective-permute-start.22 = (bf16[2048,128]{1,0:T(8,128)(2,1)}, bf16[2048,128]{1,0:T(8,128)(2,1)S(1)}, u32[]{:S(2)}, u32[]{:S(2)}) collective-permute-start(bf16[2048,128]{1,0:T(8,128)(2,1)} %get-tuple-element.112.refs_12_), channel_id=1, source_target_pairs={{0,16},{16,0},{1,17},{17,1},{2,18},{18,2},{3,19},{19,3},{4,20},{20... | collective-permute-start | bytes 1572872 | tf_op jit(solution)/shard_map/ppermute | solution.py:37
  126.6 19.1 %collective-permute-start.23 = (bf16[2048,128]{1,0:T(8,128)(2,1)}, bf16[2048,128]{1,0:T(8,128)(2,1)S(1)}, u32[]{:S(2)}, u32[]{:S(2)}) collective-permute-start(bf16[2048,128]{1,0:T(8,128)(2,1)} %get-tuple-element.114.refs_6_), channel_id=1, source_target_pairs={{0,4},{4,8},{8,12},{12,0},{1,5},{5,9},{9,13},{13,1},{2,6},{6,10},{... | collective-permute-start | bytes 1572872 | tf_op jit(solution)/shard_map/ppermute | solution.py:32
  126.6 19.9 %collective-permute-start.24 = (bf16[2048,128]{1,0:T(8,128)(2,1)}, bf16[2048,128]{1,0:T(8,128)(2,1)S(1)}, u32[]{:S(2)}, u32[]{:S(2)}) collective-permute-start(bf16[2048,128]{1,0:T(8,128)(2,1)} %get-tuple-element.114.refs_6_), channel_id=1, source_target_pairs={{0,16},{16,0},{1,17},{17,1},{2,18},{18,2},{3,19},{19,3},{4,20},{20... | collective-permute-start | bytes 1572872 | tf_op jit(solution)/shard_map/ppermute | solution.py:37
  136.0 19.0 %collective-permute-start.25 = (bf16[2048,128]{1,0:T(8,128)(2,1)}, bf16[2048,128]{1,0:T(8,128)(2,1)S(1)}, u32[]{:S(2)}, u32[]{:S(2)}) collective-permute-start(bf16[2048,128]{1,0:T(8,128)(2,1)} %get-tuple-element.118.refs_6_), channel_id=1, source_target_pairs={{0,4},{4,8},{8,12},{12,0},{1,5},{5,9},{9,13},{13,1},{2,6},{6,10},{... | collective-permute-start | bytes 1572872 | tf_op jit(solution)/shard_map/ppermute | solution.py:32
  136.0 21.7 %collective-permute-start.26 = (bf16[2048,128]{1,0:T(8,128)(2,1)}, bf16[2048,128]{1,0:T(8,128)(2,1)S(1)}, u32[]{:S(2)}, u32[]{:S(2)}) collective-permute-start(bf16[2048,128]{1,0:T(8,128)(2,1)} %get-tuple-element.118.refs_6_), channel_id=1, source_target_pairs={{0,16},{16,0},{1,17},{17,1},{2,18},{18,2},{3,19},{19,3},{4,20},{20... | collective-permute-start | bytes 1572872 | tf_op jit(solution)/shard_map/ppermute | solution.py:37
  147.3 19.0 %collective-permute-start.27 = (bf16[2048,128]{1,0:T(8,128)(2,1)}, bf16[2048,128]{1,0:T(8,128)(2,1)S(1)}, u32[]{:S(2)}, u32[]{:S(2)}) collective-permute-start(bf16[2048,128]{1,0:T(8,128)(2,1)} %get-tuple-element.120.refs_6_), channel_id=1, source_target_pairs={{0,4},{4,8},{8,12},{12,0},{1,5},{5,9},{9,13},{13,1},{2,6},{6,10},{... | collective-permute-start | bytes 1572872 | tf_op jit(solution)/shard_map/ppermute | solution.py:32
  147.3 21.7 %collective-permute-start.28 = (bf16[2048,128]{1,0:T(8,128)(2,1)}, bf16[2048,128]{1,0:T(8,128)(2,1)S(1)}, u32[]{:S(2)}, u32[]{:S(2)}) collective-permute-start(bf16[2048,128]{1,0:T(8,128)(2,1)} %get-tuple-element.121.refs_8_), channel_id=1, source_target_pairs={{0,16},{16,0},{1,17},{17,1},{2,18},{18,2},{3,19},{19,3},{4,20},{20... | collective-permute-start | bytes 1572872 | tf_op jit(solution)/shard_map/ppermute | solution.py:37
  158.5 20.1 %collective-permute-start.29 = (bf16[2048,128]{1,0:T(8,128)(2,1)}, bf16[2048,128]{1,0:T(8,128)(2,1)S(1)}, u32[]{:S(2)}, u32[]{:S(2)}) collective-permute-start(bf16[2048,128]{1,0:T(8,128)(2,1)} %get-tuple-element.123.refs_8_), channel_id=1, source_target_pairs={{0,4},{4,8},{8,12},{12,0},{1,5},{5,9},{9,13},{13,1},{2,6},{6,10},{... | collective-permute-start | bytes 1572872 | tf_op jit(solution)/shard_map/ppermute | solution.py:32
  158.5 21.7 %collective-permute-start.30 = (bf16[2048,128]{1,0:T(8,128)(2,1)}, bf16[2048,128]{1,0:T(8,128)(2,1)S(1)}, u32[]{:S(2)}, u32[]{:S(2)}) collective-permute-start(bf16[2048,128]{1,0:T(8,128)(2,1)} %get-tuple-element.124.refs_8_), channel_id=1, source_target_pairs={{0,16},{16,0},{1,17},{17,1},{2,18},{18,2},{3,19},{19,3},{4,20},{20... | collective-permute-start | bytes 1572872 | tf_op jit(solution)/shard_map/ppermute | solution.py:37
  169.7 21.6 %collective-permute-start.31 = (bf16[2048,128]{1,0:T(8,128)(2,1)}, bf16[2048,128]{1,0:T(8,128)(2,1)S(1)}, u32[]{:S(2)}, u32[]{:S(2)}) collective-permute-start(bf16[2048,128]{1,0:T(8,128)(2,1)} %get-tuple-element.129.refs_10_), channel_id=1, source_target_pairs={{0,4},{4,8},{8,12},{12,0},{1,5},{5,9},{9,13},{13,1},{2,6},{6,10},{... | collective-permute-start | bytes 1572872 | tf_op jit(solution)/shard_map/ppermute | solution.py:32
  169.7 21.7 %collective-permute-start.32 = (bf16[2048,128]{1,0:T(8,128)(2,1)}, bf16[2048,128]{1,0:T(8,128)(2,1)S(1)}, u32[]{:S(2)}, u32[]{:S(2)}) collective-permute-start(bf16[2048,128]{1,0:T(8,128)(2,1)} %get-tuple-element.129.refs_10_), channel_id=1, source_target_pairs={{0,16},{16,0},{1,17},{17,1},{2,18},{18,2},{3,19},{19,3},{4,20},{20... | collective-permute-start | bytes 1572872 | tf_op jit(solution)/shard_map/ppermute | solution.py:37
  181.0 20.1 %collective-permute-start.33 = (bf16[2048,128]{1,0:T(8,128)(2,1)}, bf16[2048,128]{1,0:T(8,128)(2,1)S(1)}, u32[]{:S(2)}, u32[]{:S(2)}) collective-permute-start(bf16[2048,128]{1,0:T(8,128)(2,1)} %get-tuple-element.133.refs_12_), channel_id=1, source_target_pairs={{0,4},{4,8},{8,12},{12,0},{1,5},{5,9},{9,13},{13,1},{2,6},{6,10},{... | collective-permute-start | bytes 1572872 | tf_op jit(solution)/shard_map/ppermute | solution.py:32
  181.0 21.7 %collective-permute-start.34 = (bf16[2048,128]{1,0:T(8,128)(2,1)}, bf16[2048,128]{1,0:T(8,128)(2,1)S(1)}, u32[]{:S(2)}, u32[]{:S(2)}) collective-permute-start(bf16[2048,128]{1,0:T(8,128)(2,1)} %get-tuple-element.133.refs_12_), channel_id=1, source_target_pairs={{0,16},{16,0},{1,17},{17,1},{2,18},{18,2},{3,19},{19,3},{4,20},{20... | collective-permute-start | bytes 1572872 | tf_op jit(solution)/shard_map/ppermute | solution.py:37
  192.3 21.0 %collective-permute-start.35 = (bf16[2048,128]{1,0:T(8,128)(2,1)}, bf16[2048,128]{1,0:T(8,128)(2,1)S(1)}, u32[]{:S(2)}, u32[]{:S(2)}) collective-permute-start(bf16[2048,128]{1,0:T(8,128)(2,1)} %get-tuple-element.137.refs_6_), channel_id=1, source_target_pairs={{0,4},{4,8},{8,12},{12,0},{1,5},{5,9},{9,13},{13,1},{2,6},{6,10},{... | collective-permute-start | bytes 1572872 | tf_op jit(solution)/shard_map/ppermute | solution.py:32
  192.7 21.1 %collective-permute-start.36 = (bf16[2048,128]{1,0:T(8,128)(2,1)}, bf16[2048,128]{1,0:T(8,128)(2,1)S(1)}, u32[]{:S(2)}, u32[]{:S(2)}) collective-permute-start(bf16[2048,128]{1,0:T(8,128)(2,1)} %get-tuple-element.137.refs_6_), channel_id=1, source_target_pairs={{0,16},{16,0},{1,17},{17,1},{2,18},{18,2},{3,19},{19,3},{4,20},{20... | collective-permute-start | bytes 1572872 | tf_op jit(solution)/shard_map/ppermute | solution.py:37
  203.4 20.8 %collective-permute-start.37 = (bf16[2048,128]{1,0:T(8,128)(2,1)}, bf16[2048,128]{1,0:T(8,128)(2,1)S(1)}, u32[]{:S(2)}, u32[]{:S(2)}) collective-permute-start(bf16[2048,128]{1,0:T(8,128)(2,1)} %get-tuple-element.141.refs_8_), channel_id=1, source_target_pairs={{0,4},{4,8},{8,12},{12,0},{1,5},{5,9},{9,13},{13,1},{2,6},{6,10},{... | collective-permute-start | bytes 1572872 | tf_op jit(solution)/shard_map/ppermute | solution.py:32
  204.6 20.5 %collective-permute-start.38 = (bf16[2048,128]{1,0:T(8,128)(2,1)}, bf16[2048,128]{1,0:T(8,128)(2,1)S(1)}, u32[]{:S(2)}, u32[]{:S(2)}) collective-permute-start(bf16[2048,128]{1,0:T(8,128)(2,1)} %get-tuple-element.141.refs_8_), channel_id=1, source_target_pairs={{0,16},{16,0},{1,17},{17,1},{2,18},{18,2},{3,19},{19,3},{4,20},{20... | collective-permute-start | bytes 1572872 | tf_op jit(solution)/shard_map/ppermute | solution.py:37
  214.7 21.7 %collective-permute-start.39 = (bf16[2048,128]{1,0:T(8,128)(2,1)}, bf16[2048,128]{1,0:T(8,128)(2,1)S(1)}, u32[]{:S(2)}, u32[]{:S(2)}) collective-permute-start(bf16[2048,128]{1,0:T(8,128)(2,1)} %get-tuple-element.146.refs_6_), channel_id=1, source_target_pairs={{0,16},{16,0},{1,17},{17,1},{2,18},{18,2},{3,19},{19,3},{4,20},{20... | collective-permute-start | bytes 1572872 | tf_op jit(solution)/shard_map/ppermute | solution.py:37
  226.7 23.8 %collective-permute-start.44 = (bf16[2,4,1024]{2,1,0:T(4,128)(2,1)S(1)}, bf16[2,4,1024]{2,1,0:T(4,128)(2,1)S(1)}, u32[]{:S(2)}, u32[]{:S(2)}) collective-permute-start(bf16[2,4,1024]{2,1,0:T(4,128)(2,1)S(1)} %broadcast_select_fusion.1), channel_id=1, source_target_pairs={{0,8},{4,12},{8,0},{12,4},{1,9},{5,13},{9,1},{13,5},{2,10},{6,14},... | collective-permute-start | bytes 49160 | tf_op jit(solution)/shard_map/ppermute | solution.py:37
  227.5 24.2 %collective-permute-start.40 = (bf16[2048,128]{1,0:T(8,128)(2,1)}, bf16[2048,128]{1,0:T(8,128)(2,1)S(1)}, u32[]{:S(2)}, u32[]{:S(2)}) collective-permute-start(bf16[2048,128]{1,0:T(8,128)(2,1)} %get-tuple-element.148.refs_1_), channel_id=1, source_target_pairs={{0,16},{16,0},{1,17},{17,1},{2,18},{18,2},{3,19},{19,3},{4,20},{20... | collective-permute-start | bytes 1572872 | tf_op jit(solution)/shard_map/ppermute | solution.py:37
  250.5 17.9 %collective-permute-start.45 = (bf16[1,4,1024]{2,1,0:T(4,128)(2,1)S(1)}, bf16[1,4,1024]{2,1,0:T(4,128)(2,1)S(1)}, u32[]{:S(2)}, u32[]{:S(2)}) collective-permute-start(bf16[1,4,1024]{2,1,0:T(4,128)(2,1)S(1)} %broadcast_select_fusion.2), channel_id=1, source_target_pairs={{0,4},{4,0},{8,12},{12,8},{1,5},{5,1},{9,13},{13,9},{2,6},{6,2},{1... | collective-permute-start | bytes 24584 | tf_op jit(solution)/shard_map/ppermute | solution.py:37
  257.5 14.0 %copy-start.1 = (s32[8]{0:T(128)S(1)}, s32[8]{0:T(128)}, u32[]{:S(2)}) copy-start(s32[8]{0:T(128)} %param.16) | copy-start | bytes 100
  266.5 2.5 collective-permute-start.41
  266.5 3.6 %collective-permute-start.42 = (f32[2,384]{1,0:T(2,128)S(1)}, f32[2,384]{1,0:T(2,128)S(1)}, u32[]{:S(2)}, u32[]{:S(2)}) collective-permute-start(f32[2,384]{1,0:T(2,128)S(1)} %bitcast.105), channel_id=1, source_target_pairs={{0,2},{1,3},{2,0},{3,1},{4,6},{5,7},{6,4},{7,5},{8,10},{9,11},{10,... | collective-permute-start | bytes 9224 | tf_op jit(solution)/shard_map/ppermute | solution.py:37
  267.9 3.0 %collective-permute-start.43 = (f32[2,384]{1,0:T(2,128)S(1)}, f32[2,384]{1,0:T(2,128)S(1)}, u32[]{:S(2)}, u32[]{:S(2)}) collective-permute-start(f32[2,384]{1,0:T(2,128)S(1)} %bitcast.106), channel_id=1, source_target_pairs={{0,3},{1,2},{2,1},{3,0},{4,7},{5,6},{6,5},{7,4},{8,11},{9,10},{10,... | collective-permute-start | bytes 9224 | tf_op jit(solution)/shard_map/ppermute | solution.py:37
  (37 other events, 82.3 us)

commit v3 on v2

--- a/solution.py
+++ b/solution.py
@@ -520,9 +520,9 @@
                 acts.append((when + 1, functools.partial(score_now, i)))
     acts.append((wide + 1, cache_now))
     for c in each:
-        when = 7
+        when = 6 + c
         at(when, *[("own", off, c) for off in near])
-        acts.append((when, functools.partial(cross, c, when + 2)))
+        acts.append((when, functools.partial(cross, c, 9)))
     at(wide, ("own", 1))
     for now in range(total + wide + lag):
         names = []

time: 272 us -> 268 us (0.985)
  waiting for transfers between devices: 88.4 us -> 82.1 us
    ppermute x28, waiting for transfers between devices: 29 us -> 25 us  [partner(): return lax.ppermute(value, axis, [(i, i ^ bits) for i in range(size)])]
  transfers between devices with their start and end apart: 46 -> 46, of which waited for: 26 -> 27; matrix products, arithmetic and copies ran while one was open for 14% -> 14% of each run, Pallas kernels for 34% -> 35%
where the time goes in v3:
time: 268 us; the launch traced here: 267 us
  Pallas kernels  92.3 us (34%)
  waiting for transfers between devices  82.1 us (31%)
  local copies, waits for them, and re-layouts  42 us (16%)
  starting transfers between devices  38.1 us (14%)
  other arithmetic  7.14 us (3%)
  matrix products  4.1 us (2%)
    pallas_call x8, Pallas kernels, project(): pl.pallas_call(functools.partial(project_kernel, plan), in_specs=[pl.Bloc...  59.6 us
    ppermute x18, waiting for transfers between devices, shifted(): lax.ppermute(value, axis, [(i, (i + step) % size) for i in range(size)])  57.1 us
    pallas_call x4, Pallas kernels, reward_share(): pl.pallas_call(reward_kernel, grid_spec=spec, out_shape=jax.ShapeDtypeStr...  32.7 us
    ppermute x28, starting transfers between devices, partner(): return lax.ppermute(value, axis, [(i, i ^ bits) for i in range(size)])  30.2 us
    ppermute x28, waiting for transfers between devices, partner(): return lax.ppermute(value, axis, [(i, i ^ bits) for i in range(size)])  25 us
    unnamed x80, local copies, waits for them, and re-layouts  16.3 us
    ppermute x18, starting transfers between devices, shifted(): lax.ppermute(value, axis, [(i, (i + step) % size) for i in range(size)])  7.96 us
    slice x1, local copies, waits for them, and re-layouts, cache_now(): value['actor', 1] = actor_stored_pairs[..., HD:]  6.02 us
  transfers between devices with their start and end apart: 46, of which 27 were waited for; matrix products, arithmetic and copies ran while one was open for 14% of the time, Pallas kernels for 35%

profile of v3, /device:TPU:0, one launch (start us, length us, event | category | flops | bytes accessed | tf_op | source)
XLA Modules:
  0.0 267.0 jit_solution(367693091522140346)
XLA Ops:
  2.6 2.9 %constant_dynamic-slice_fusion.9 = (bf16[2048,128]{1,0:T(8,128)(2,1)}, bf16[2048,128]{1,0:T(8,128)(2,1)}, bf16[2048,128]{1,0:T(8,128)(2,1)S(1)}, bf16[2048,128]{1,0:T(8,128)(2,1)}) fusion(bf16[2048,512]{1,0:T(8,128)(2,1)} %param.12, s32[]{:T(128)S(6)} %add.409, s32[]{:T(128)S(6)} %select_n.409, s32[]{:T(128)S(6)} %select_n.388, s32[]{:T(128)S(6)} %add.407), kind=kLoop, calls=%fused_computation.57 | loop fusion | bytes 4194320 | tf_op jit(solution)/shard_map/slice | solution.py:378
  6.4 2.6 collective-permute-start
  9.0 1.6 collective-permute-start.2
  10.5 2.1 slice_bitcast_fusion
  12.6 1.5 collective-permute-start.9
  15.5 6.0 %fusion.40 = (bf16[2,2048,2,128]{3,2,1,0:T(2,128)(2,1)}, bf16[2,2048,2,128]{3,2,1,0:T(2,128)(2,1)}) fusion(bf16[2,2048,2,256]{3,2,1,0:T(2,128)(2,1)} %param.15), kind=kLoop, calls=%fused_computation.94 | loop fusion | bytes 8388608 | tf_op jit(solution)/shard_map/slice | solution.py:496
  22.4 1.9 collective-permute-done.refs_1_
  26.0 4.3 %constant_dynamic-slice_fusion.8 = (bf16[2048,128]{1,0:T(8,128)(2,1)}, bf16[2048,128]{1,0:T(8,128)(2,1)}, bf16[2048,128]{1,0:T(8,128)(2,1)}, bf16[2048,128]{1,0:...) fusion(bf16[2048,1024]{1,0:T(8,128)(2,1)} %param.11, ...), kind=kLoop, calls=%fused_computation.56 | loop fusion | bytes 8388640 | tf_op jit(solution)/shard_map/slice | solution.py:379
  30.3 1.7 collective-permute-start.4
  32.0 3.6 %collective-permute-done.2.refs_1_ = bf16[2048,128]{1,0:T(8,128)(2,1)} collective-permute-done((bf16[2048,128]{1,0:T(8,128)(2,1)}, bf16[2048,128]{1,0:T(8,128)(2,1)}, u32[]{:S(2)}, u32[]{:S(2)}) %collective-permute-start.2) | collective-permute-done | bytes 524320 | tf_op jit(solution)/shard_map/ppermute | solution.py:32
  35.6 11.3 %collective-permute-done.3.refs_1_ = bf16[2096,128]{1,0:T(8,128)(2,1)S(1)} collective-permute-done((bf16[2096,128]{1,0:T(8,128)(2,1)}, bf16[2096,128]{1,0:T(8,128)(2,1)S(1)}, u32[]{:S(2)}, u32[]{:S(2)}) %collective-permute-start.3) | collective-permute-done | bytes 536608 | tf_op jit(solution)/shard_map/ppermute | solution.py:32
  47.0 1.7 collective-permute-start.6
  49.4 8.8 %collective-permute-done.5.refs_1_ = bf16[2048,128]{1,0:T(8,128)(2,1)S(1)} collective-permute-done((bf16[2048,128]{1,0:T(8,128)(2,1)}, bf16[2048,128]{1,0:T(8,128)(2,1)S(1)}, u32[]{:S(2)}, u32[]{:S(2)}) %collective-permute-start.5) | collective-permute-done | bytes 524320 | tf_op jit(solution)/shard_map/ppermute | solution.py:32
  58.2 1.7 collective-permute-start.8
  63.0 6.7 %collective-permute-done.7.refs_1_ = bf16[2096,128]{1,0:T(8,128)(2,1)S(1)} collective-permute-done((bf16[2096,128]{1,0:T(8,128)(2,1)}, bf16[2096,128]{1,0:T(8,128)(2,1)S(1)}, u32[]{:S(2)}, u32[]{:S(2)}) %collective-permute-start.7) | collective-permute-done | bytes 536608 | tf_op jit(solution)/shard_map/ppermute | solution.py:32
  69.7 3.8 %collective-permute-done.8.refs_2_ = bf16[2096,128]{1,0:T(8,128)(2,1)S(1)} collective-permute-done((bf16[2096,128]{1,0:T(8,128)(2,1)}, bf16[2096,128]{1,0:T(8,128)(2,1)S(1)}, u32[]{:S(2)}, u32[]{:S(2)}) %collective-permute-start.8) | collective-permute-done | bytes 536608 | tf_op jit(solution)/shard_map/ppermute | solution.py:37
  75.1 1.7 collective-permute-start.14
  77.6 5.3 %collective-permute-done.12.refs_4_ = bf16[384,2048]{1,0:T(8,128)(2,1)} collective-permute-done((bf16[384,2048]{1,0:T(8,128)(2,1)}, bf16[384,2048]{1,0:T(8,128)(2,1)}, u32[]{:S(2)}, u32[]{:S(2)}) %collective-permute-start.12) | collective-permute-done | bytes 1572896 | tf_op jit(solution)/shard_map/ppermute | solution.py:37
  82.9 1.8 collective-permute-done.11.refs_2_
  86.0 2.6 fusion.41
  89.7 3.5 %collective-permute-done.13.refs_1_ = bf16[2048,128]{1,0:T(8,128)(2,1)S(1)} collective-permute-done((bf16[2048,128]{1,0:T(8,128)(2,1)}, bf16[2048,128]{1,0:T(8,128)(2,1)S(1)}, u32[]{:S(2)}, u32[]{:S(2)}) %collective-permute-start.13) | collective-permute-done | bytes 524320 | tf_op jit(solution)/shard_map/ppermute | solution.py:32
  93.2 1.3 collective-permute-start.16
  96.4 8.2 %collective-permute-done.15.refs_1_ = bf16[2048,128]{1,0:T(8,128)(2,1)} collective-permute-done((bf16[2048,128]{1,0:T(8,128)(2,1)}, bf16[2048,128]{1,0:T(8,128)(2,1)}, u32[]{:S(2)}, u32[]{:S(2)}) %collective-permute-start.15) | collective-permute-done | bytes 524320 | tf_op jit(solution)/shard_map/ppermute | solution.py:32
  104.6 1.3 collective-permute-start.20
  105.9 1.5 collective-permute-done.16.refs_2_
  110.2 13.0 %project.8 = bf16[2,384,512]{2,1,0:T(8,128)(2,1)} custom-call(s32[8]{0:T(128)} %stack.178.where_ref, bf16[2,384,2048]{2,1,0:T(8,128)(2,1)} %refs_0_.15, bf16[2,384,2048]{2,1,0:T(8,128)(2,1)} %get-tuple-element.81.refs_1_, bf16[384,2048]{1,0:T(8,128)(2,1)} %get-tuple-element.89.refs_2_, bf16[384,2048]{1,0:T(8,128)(2,1)} %get-tuple-element.92.refs_3_, ...), custom_call_target="tpu_custom_call" | custom-call | flops 6442450944 | bytes 12582912 | tf_op jit(solution)/shard_map/project/pallas_call | solution.py:157
  126.1 4.8 %collective-permute-done.22.refs_2_ = bf16[2048,128]{1,0:T(8,128)(2,1)S(1)} collective-permute-done((bf16[2048,128]{1,0:T(8,128)(2,1)}, bf16[2048,128]{1,0:T(8,128)(2,1)S(1)}, u32[]{:S(2)}, u32[]{:S(2)}) %collective-permute-start.22) | collective-permute-done | bytes 524320 | tf_op jit(solution)/shard_map/ppermute | solution.py:37
  131.7 1.3 collective-permute-start.26
  133.0 8.1 %project.9.refs_4_ = f32[2,384,512]{2,1,0:T(8,128)} custom-call(s32[4]{0:T(128)} %pad_add_fusion.3.where_ref, bf16[2,384,2048]{2,1,0:T(8,128)(2,1)} %refs_0_.15, bf16[2,384,2048]{2,1,0:T(8,128)(2,1)} %get-tuple-element.81.refs_1_, bf16[384,2048]{1,0:T(8,128)(2,1)} %get-tuple-element.89.refs_2_, bf16[384,2048]{1,0:T(8,128)(2,1)} %get-tuple-element.92.refs_3_, ...), custom_call_target="tpu_custom_call" | custom-call | flops 3221225472 | bytes 6291456 | tf_op jit(solution)/shard_map/project/pallas_call | solution.py:157
  142.9 1.3 collective-permute-start.28
  144.3 8.2 %collective-permute-done.25.refs_1_ = bf16[2048,128]{1,0:T(8,128)(2,1)S(1)} collective-permute-done((bf16[2048,128]{1,0:T(8,128)(2,1)}, bf16[2048,128]{1,0:T(8,128)(2,1)S(1)}, u32[]{:S(2)}, u32[]{:S(2)}) %collective-permute-start.25) | collective-permute-done | bytes 524320 | tf_op jit(solution)/shard_map/ppermute | solution.py:32
  154.2 1.3 collective-permute-start.30
  159.9 3.8 %collective-permute-done.27.refs_1_ = bf16[2048,128]{1,0:T(8,128)(2,1)S(1)} collective-permute-done((bf16[2048,128]{1,0:T(8,128)(2,1)}, bf16[2048,128]{1,0:T(8,128)(2,1)S(1)}, u32[]{:S(2)}, u32[]{:S(2)}) %collective-permute-start.27) | collective-permute-done | bytes 524320 | tf_op jit(solution)/shard_map/ppermute | solution.py:32
  165.4 1.3 collective-permute-start.32
  167.4 6.7 %project.10 = bf16[2,384,256]{2,1,0:T(8,128)(2,1)} custom-call(s32[4]{0:T(128)} %pad_add_fusion.2.where_ref, bf16[2,384,2048]{2,1,0:T(8,128)(2,1)} %refs_0_.15, bf16[2,384,2048]{2,1,0:T(8,128)(2,1)} %get-tuple-element.81.refs_1_, bf16[384,2048]{1,0:T(8,128)(2,1)} %get-tuple-element.89.refs_2_, bf16[384,2048]{1,0:T(8,128)(2,1)} %get-tuple-element.92.refs_3_, ...), custom_call_target="tpu_custom_call" | custom-call | flops 1610612736 | bytes 6291456 | tf_op jit(solution)/shard_map/project/pallas_call | solution.py:157
  178.6 8.2 %reward_share.4.refs_3_ = f32[2,8,384]{2,1,0:T(8,128)} custom-call(s32[8]{0:T(128)} %stack.189.kg_ref, bf16[768,256]{1,0:T(8,128)(2,1)} %get-tuple-element.130.q_ref, bf16[2,2048,512]{2,1,0:T(8,128)(2,1)} %old_value_ref.7, bf16[2,2048,512]{2,1,0:T(8,128)(2,1)} %old_value_ref.7, bf16[768,512]{1,0:T(8,128)(2,1)} %get-tuple-element.131.key_ref.value_ref, ...), custom_call_target="tpu_custom_call" | custom-call | flops 2868903936 | bytes 8388608 | tf_op jit(solution)/shard_map/reward_share/pallas_call | solution.py:271
  187.8 1.8 collective-permute-start.35
  191.3 6.7 %project.11 = bf16[2,384,256]{2,1,0:T(8,128)(2,1)} custom-call(s32[4]{0:T(128)} %pad_add_fusion.2.where_ref, bf16[2,384,2048]{2,1,0:T(8,128)(2,1)} %refs_0_.15, bf16[2,384,2048]{2,1,0:T(8,128)(2,1)} %get-tuple-element.81.refs_1_, bf16[384,2048]{1,0:T(8,128)(2,1)} %get-tuple-element.89.refs_2_, bf16[384,2048]{1,0:T(8,128)(2,1)} %get-tuple-element.92.refs_3_, ...), custom_call_target="tpu_custom_call" | custom-call | flops 1610612736 | bytes 6291456 | tf_op jit(solution)/shard_map/project/pallas_call | solution.py:157
  200.8 8.2 %reward_share.5.refs_3_ = f32[2,8,384]{2,1,0:T(8,128)} custom-call(s32[8]{0:T(128)} %stack.198.kg_ref, bf16[768,256]{1,0:T(8,128)(2,1)} %get-tuple-element.138.q_ref, bf16[2,2048,512]{2,1,0:T(8,128)(2,1)} %old_value_ref.7, bf16[2,2048,512]{2,1,0:T(8,128)(2,1)} %old_value_ref.7, bf16[768,512]{1,0:T(8,128)(2,1)} %get-tuple-element.131.key_ref.value_ref, ...), custom_call_target="tpu_custom_call" | custom-call | flops 2868903936 | bytes 8388608 | tf_op jit(solution)/shard_map/reward_share/pallas_call | solution.py:271
  210.3 1.3 collective-permute-start.39
  211.7 8.1 %project.12.refs_4_ = f32[2,384,512]{2,1,0:T(8,128)} custom-call(s32[4]{0:T(128)} %pad_add_fusion.3.where_ref, bf16[2,384,2048]{2,1,0:T(8,128)(2,1)} %refs_0_.15, bf16[2,384,2048]{2,1,0:T(8,128)(2,1)} %get-tuple-element.81.refs_1_, bf16[384,2048]{1,0:T(8,128)(2,1)} %get-tuple-element.89.refs_2_, bf16[384,2048]{1,0:T(8,128)(2,1)} %get-tuple-element.92.refs_3_, ...), custom_call_target="tpu_custom_call" | custom-call | flops 3221225472 | bytes 6291456 | tf_op jit(solution)/shard_map/project/pallas_call | solution.py:157
  222.3 1.8 collective-permute-start.44
  225.0 7.0 %project.13.refs_8_ = f32[2,384,512]{2,1,0:T(8,128)} custom-call(s32[2]{0:T(128)} %pad_add_fusion.where_ref, bf16[2,384,2048]{2,1,0:T(8,128)(2,1)} %refs_0_.15, bf16[2,384,2048]{2,1,0:T(8,128)(2,1)} %get-tuple-element.81.refs_1_, bf16[384,2048]{1,0:T(8,128)(2,1)} %get-tuple-element.89.refs_2_, bf16[384,2048]{1,0:T(8,128)(2,1)} %get-tuple-element.92.refs_3_, ...), custom_call_target="tpu_custom_call" | custom-call | flops 1610612736 | bytes 3145728 | tf_op jit(solution)/shard_map/project/pallas_call | solution.py:157
  232.8 5.1 %project.14 = bf16[2,384,256]{2,1,0:T(8,128)(2,1)} custom-call(s32[2]{0:T(128)} %pad_add_fusion.1.where_ref, bf16[2,384,2048]{2,1,0:T(8,128)(2,1)} %refs_0_.15, bf16[2,384,2048]{2,1,0:T(8,128)(2,1)} %get-tuple-element.81.refs_1_, bf16[384,2048]{1,0:T(8,128)(2,1)} %get-tuple-element.89.refs_2_, bf16[384,2048]{1,0:T(8,128)(2,1)} %get-tuple-element.92.refs_3_, ...), custom_call_target="tpu_custom_call" | custom-call | flops 805306368 | bytes 3145728 | tf_op jit(solution)/shard_map/project/pallas_call | solution.py:157
  237.9 8.2 %reward_share.6.refs_3_ = f32[2,8,384]{2,1,0:T(8,128)} custom-call(s32[8]{0:T(128)} %stack.207.kg_ref, bf16[768,256]{1,0:T(8,128)(2,1)} %bitcast.100, bf16[2,2048,512]{2,1,0:T(8,128)(2,1)} %old_value_ref.7, bf16[2,2048,512]{2,1,0:T(8,128)(2,1)} %old_value_ref.7, bf16[768,512]{1,0:T(8,128)(2,1)} %get-tuple-element.131.key_ref.value_ref, ...), custom_call_target="tpu_custom_call" | custom-call | flops 2868903936 | bytes 8388608 | tf_op jit(solution)/shard_map/reward_share/pallas_call | solution.py:271
  247.9 5.1 %project.15 = bf16[2,384,256]{2,1,0:T(8,128)(2,1)} custom-call(s32[2]{0:T(128)} %pad_add_fusion.1.where_ref, bf16[2,384,2048]{2,1,0:T(8,128)(2,1)} %refs_0_.15, bf16[2,384,2048]{2,1,0:T(8,128)(2,1)} %get-tuple-element.81.refs_1_, bf16[384,2048]{1,0:T(8,128)(2,1)} %get-tuple-element.89.refs_2_, bf16[384,2048]{1,0:T(8,128)(2,1)} %get-tuple-element.92.refs_3_, ...), custom_call_target="tpu_custom_call" | custom-call | flops 805306368 | bytes 3145728 | tf_op jit(solution)/shard_map/project/pallas_call | solution.py:157
  253.0 8.2 %reward_share.7 = f32[2,8,384]{2,1,0:T(8,128)} custom-call(s32[8]{0:T(128)} %stack.172.kg_ref, bf16[768,256]{1,0:T(8,128)(2,1)} %bitcast.99, bf16[2,2048,512]{2,1,0:T(8,128)(2,1)} %old_value_ref.7, bf16[2,2048,512]{2,1,0:T(8,128)(2,1)} %old_value_ref.7, bf16[768,512]{1,0:T(8,128)(2,1)} %get-tuple-element.131.key_ref.value_ref, ...), custom_call_target="tpu_custom_call" | custom-call | flops 2868903936 | bytes 8388608 | tf_op jit(solution)/shard_map/reward_share/pallas_call | solution.py:271
  261.9 1.4 collective-permute-start.42
  (223 shorter events, 55.5 us)
Async XLA Ops:
  0.6 14.3 %copy-start = (s32[8]{0:T(128)S(1)}, s32[8]{0:T(128)}, u32[]{:S(2)}) copy-start(s32[8]{0:T(128)} %param.16) | copy-start | bytes 100
  0.6 23.7 %collective-permute-start.1 = (bf16[2,384,2048]{2,1,0:T(8,128)(2,1)}, bf16[2,384,2048]{2,1,0:T(8,128)(2,1)S(1)}, u32[]{:S(2)}, u32[]{:S(2)}) collective-permute-start(bf16[2,384,2048]{2,1,0:T(8,128)(2,1)} %refs_0_.15), channel_id=1, source_target_pairs={{0,1},{1,0},{2,3},{3,2},{4,5},{5,4},{6,7},{7,6},{8,9},{9,8},{10,11... | collective-permute-start | bytes 9437192 | tf_op jit(solution)/shard_map/ppermute | solution.py:37
  6.4 18.0 %collective-permute-start = (bf16[2096,128]{1,0:T(8,128)(2,1)}, bf16[2096,128]{1,0:T(8,128)(2,1)}, u32[]{:S(2)}, u32[]{:S(2)}) collective-permute-start(bf16[2096,128]{1,0:T(8,128)(2,1)} %pad_maximum_fusion.refs_6_), channel_id=1, source_target_pairs={{0,4},{4,8},{8,12},{12,0},{1,5},{5,9},{9,13},{13,1},{2,6},{6,10},{... | collective-permute-start | bytes 1609736 | tf_op jit(solution)/shard_map/ppermute | solution.py:32
  9.0 26.6 %collective-permute-start.2 = (bf16[2048,128]{1,0:T(8,128)(2,1)}, bf16[2048,128]{1,0:T(8,128)(2,1)}, u32[]{:S(2)}, u32[]{:S(2)}) collective-permute-start(bf16[2048,128]{1,0:T(8,128)(2,1)} %get-tuple-element.175.refs_7_), channel_id=1, source_target_pairs={{0,4},{4,8},{8,12},{12,0},{1,5},{5,9},{9,13},{13,1},{2,6},{6,10},{... | collective-permute-start | bytes 1572872 | tf_op jit(solution)/shard_map/ppermute | solution.py:32
  12.6 49.5 %collective-permute-start.9 = (bf16[384,2048]{1,0:T(8,128)(2,1)}, bf16[384,2048]{1,0:T(8,128)(2,1)}, u32[]{:S(2)}, u32[]{:S(2)}) collective-permute-start(bf16[384,2048]{1,0:T(8,128)(2,1)} %get-tuple-element.171), channel_id=1, source_target_pairs={{0,2},{1,3},{2,0},{3,1},{4,6},{5,7},{6,4},{7,5},{8,10},{9,11},{10,... | collective-permute-start | bytes 4718600 | tf_op jit(solution)/shard_map/ppermute | solution.py:37
  14.1 68.8 %collective-permute-start.12 = (bf16[384,2048]{1,0:T(8,128)(2,1)}, bf16[384,2048]{1,0:T(8,128)(2,1)}, u32[]{:S(2)}, u32[]{:S(2)}) collective-permute-start(bf16[384,2048]{1,0:T(8,128)(2,1)} %get-tuple-element.170), channel_id=1, source_target_pairs={{0,2},{1,3},{2,0},{3,1},{4,6},{5,7},{6,4},{7,5},{8,10},{9,11},{10,... | collective-permute-start | bytes 4718600 | tf_op jit(solution)/shard_map/ppermute | solution.py:37
  26.0 21.0 %collective-permute-start.3 = (bf16[2096,128]{1,0:T(8,128)(2,1)}, bf16[2096,128]{1,0:T(8,128)(2,1)S(1)}, u32[]{:S(2)}, u32[]{:S(2)}) collective-permute-start(bf16[2096,128]{1,0:T(8,128)(2,1)} %get-tuple-element.84.refs_10_), channel_id=1, source_target_pairs={{0,4},{4,8},{8,12},{12,0},{1,5},{5,9},{9,13},{13,1},{2,6},{6,10},{... | collective-permute-start | bytes 1609736 | tf_op jit(solution)/shard_map/ppermute | solution.py:32
  30.3 18.3 %collective-permute-start.4 = (bf16[2096,128]{1,0:T(8,128)(2,1)}, bf16[2096,128]{1,0:T(8,128)(2,1)S(1)}, u32[]{:S(2)}, u32[]{:S(2)}) collective-permute-start(bf16[2096,128]{1,0:T(8,128)(2,1)} %get-tuple-element.84.refs_10_), channel_id=1, source_target_pairs={{0,16},{16,0},{1,17},{17,1},{2,18},{18,2},{3,19},{19,3},{4,20},{20... | collective-permute-start | bytes 1609736 | tf_op jit(solution)/shard_map/ppermute | solution.py:37
  35.6 22.6 %collective-permute-start.5 = (bf16[2048,128]{1,0:T(8,128)(2,1)}, bf16[2048,128]{1,0:T(8,128)(2,1)S(1)}, u32[]{:S(2)}, u32[]{:S(2)}) collective-permute-start(bf16[2048,128]{1,0:T(8,128)(2,1)} %get-tuple-element.86.refs_11_), channel_id=1, source_target_pairs={{0,4},{4,8},{8,12},{12,0},{1,5},{5,9},{9,13},{13,1},{2,6},{6,10},{... | collective-permute-start | bytes 1572872 | tf_op jit(solution)/shard_map/ppermute | solution.py:32
  47.0 14.4 %collective-permute-start.6 = (bf16[2048,128]{1,0:T(8,128)(2,1)}, bf16[2048,128]{1,0:T(8,128)(2,1)S(1)}, u32[]{:S(2)}, u32[]{:S(2)}) collective-permute-start(bf16[2048,128]{1,0:T(8,128)(2,1)} %get-tuple-element.86.refs_11_), channel_id=1, source_target_pairs={{0,16},{16,0},{1,17},{17,1},{2,18},{18,2},{3,19},{19,3},{4,20},{20... | collective-permute-start | bytes 1572872 | tf_op jit(solution)/shard_map/ppermute | solution.py:37
  49.4 20.3 %collective-permute-start.7 = (bf16[2096,128]{1,0:T(8,128)(2,1)}, bf16[2096,128]{1,0:T(8,128)(2,1)S(1)}, u32[]{:S(2)}, u32[]{:S(2)}) collective-permute-start(bf16[2096,128]{1,0:T(8,128)(2,1)} %get-tuple-element.88.refs_14_), channel_id=1, source_target_pairs={{0,4},{4,8},{8,12},{12,0},{1,5},{5,9},{9,13},{13,1},{2,6},{6,10},{... | collective-permute-start | bytes 1609736 | tf_op jit(solution)/shard_map/ppermute | solution.py:32
  58.2 15.3 %collective-permute-start.8 = (bf16[2096,128]{1,0:T(8,128)(2,1)}, bf16[2096,128]{1,0:T(8,128)(2,1)S(1)}, u32[]{:S(2)}, u32[]{:S(2)}) collective-permute-start(bf16[2096,128]{1,0:T(8,128)(2,1)} %get-tuple-element.88.refs_14_), channel_id=1, source_target_pairs={{0,16},{16,0},{1,17},{17,1},{2,18},{18,2},{3,19},{19,3},{4,20},{20... | collective-permute-start | bytes 1609736 | tf_op jit(solution)/shard_map/ppermute | solution.py:37
  62.1 20.7 %collective-permute-start.10 = (bf16[2048,128]{1,0:T(8,128)(2,1)}, bf16[2048,128]{1,0:T(8,128)(2,1)}, u32[]{:S(2)}, u32[]{:S(2)}) collective-permute-start(bf16[2048,128]{1,0:T(8,128)(2,1)} %get-tuple-element.91.refs_15_), channel_id=1, source_target_pairs={{0,4},{4,8},{8,12},{12,0},{1,5},{5,9},{9,13},{13,1},{2,6},{6,10},{... | collective-permute-start | bytes 1572872 | tf_op jit(solution)/shard_map/ppermute | solution.py:32
  62.2 22.6 %collective-permute-start.11 = (bf16[2048,128]{1,0:T(8,128)(2,1)}, bf16[2048,128]{1,0:T(8,128)(2,1)S(1)}, u32[]{:S(2)}, u32[]{:S(2)}) collective-permute-start(bf16[2048,128]{1,0:T(8,128)(2,1)} %get-tuple-element.91.refs_15_), channel_id=1, source_target_pairs={{0,16},{16,0},{1,17},{17,1},{2,18},{18,2},{3,19},{19,3},{4,20},{20... | collective-permute-start | bytes 1572872 | tf_op jit(solution)/shard_map/ppermute | solution.py:37
  75.1 21.3 %collective-permute-start.14 = (bf16[2096,128]{1,0:T(8,128)(2,1)}, bf16[2096,128]{1,0:T(8,128)(2,1)}, u32[]{:S(2)}, u32[]{:S(2)}) collective-permute-start(bf16[2096,128]{1,0:T(8,128)(2,1)} %get-tuple-element.95.refs_18_), channel_id=1, source_target_pairs={{0,16},{16,0},{1,17},{17,1},{2,18},{18,2},{3,19},{19,3},{4,20},{20... | collective-permute-start | bytes 1609736 | tf_op jit(solution)/shard_map/ppermute | solution.py:37
  77.5 15.7 %collective-permute-start.13 = (bf16[2048,128]{1,0:T(8,128)(2,1)}, bf16[2048,128]{1,0:T(8,128)(2,1)S(1)}, u32[]{:S(2)}, u32[]{:S(2)}) collective-permute-start(bf16[2048,128]{1,0:T(8,128)(2,1)} %get-tuple-element.94.refs_6_), channel_id=1, source_target_pairs={{0,4},{4,8},{8,12},{12,0},{1,5},{5,9},{9,13},{13,1},{2,6},{6,10},{... | collective-permute-start | bytes 1572872 | tf_op jit(solution)/shard_map/ppermute | solution.py:32
  85.5 21.9 %collective-permute-start.18 = (bf16[384,2048]{1,0:T(8,128)(2,1)}, bf16[384,2048]{1,0:T(8,128)(2,1)S(1)}, u32[]{:S(2)}, u32[]{:S(2)}) collective-permute-start(bf16[384,2048]{1,0:T(8,128)(2,1)} %get-tuple-element.92.refs_3_), channel_id=1, source_target_pairs={{0,1},{1,0},{2,3},{3,2},{4,5},{5,4},{6,7},{7,6},{8,9},{9,8},{10,11... | collective-permute-start | bytes 4718600 | tf_op jit(solution)/shard_map/ppermute | solution.py:37
  85.5 19.0 %collective-permute-start.15 = (bf16[2048,128]{1,0:T(8,128)(2,1)}, bf16[2048,128]{1,0:T(8,128)(2,1)}, u32[]{:S(2)}, u32[]{:S(2)}) collective-permute-start(bf16[2048,128]{1,0:T(8,128)(2,1)} %get-tuple-element.97.refs_8_), channel_id=1, source_target_pairs={{0,4},{4,8},{8,12},{12,0},{1,5},{5,9},{9,13},{13,1},{2,6},{6,10},{... | collective-permute-start | bytes 1572872 | tf_op jit(solution)/shard_map/ppermute | solution.py:32
  85.5 21.9 %collective-permute-start.17 = (bf16[384,2048]{1,0:T(8,128)(2,1)}, bf16[384,2048]{1,0:T(8,128)(2,1)S(1)}, u32[]{:S(2)}, u32[]{:S(2)}) collective-permute-start(bf16[384,2048]{1,0:T(8,128)(2,1)} %get-tuple-element.89.refs_2_), channel_id=1, source_target_pairs={{0,1},{1,0},{2,3},{3,2},{4,5},{5,4},{6,7},{7,6},{8,9},{9,8},{10,11... | collective-permute-start | bytes 4718600 | tf_op jit(solution)/shard_map/ppermute | solution.py:37
  93.2 14.2 %collective-permute-start.16 = (bf16[2048,128]{1,0:T(8,128)(2,1)}, bf16[2048,128]{1,0:T(8,128)(2,1)}, u32[]{:S(2)}, u32[]{:S(2)}) collective-permute-start(bf16[2048,128]{1,0:T(8,128)(2,1)} %get-tuple-element.98.refs_19_), channel_id=1, source_target_pairs={{0,16},{16,0},{1,17},{17,1},{2,18},{18,2},{3,19},{19,3},{4,20},{20... | collective-permute-start | bytes 1572872 | tf_op jit(solution)/shard_map/ppermute | solution.py:37
  96.3 26.9 %collective-permute-start.19 = (bf16[2048,128]{1,0:T(8,128)(2,1)}, bf16[2048,128]{1,0:T(8,128)(2,1)S(1)}, u32[]{:S(2)}, u32[]{:S(2)}) collective-permute-start(bf16[2048,128]{1,0:T(8,128)(2,1)} %get-tuple-element.104.refs_10_), channel_id=1, source_target_pairs={{0,4},{4,8},{8,12},{12,0},{1,5},{5,9},{9,13},{13,1},{2,6},{6,10},{... | collective-permute-start | bytes 1572872 | tf_op jit(solution)/shard_map/ppermute | solution.py:32
  104.6 18.7 %collective-permute-start.20 = (bf16[2048,128]{1,0:T(8,128)(2,1)}, bf16[2048,128]{1,0:T(8,128)(2,1)}, u32[]{:S(2)}, u32[]{:S(2)}) collective-permute-start(bf16[2048,128]{1,0:T(8,128)(2,1)} %get-tuple-element.104.refs_10_), channel_id=1, source_target_pairs={{0,16},{16,0},{1,17},{17,1},{2,18},{18,2},{3,19},{19,3},{4,20},{20... | collective-permute-start | bytes 1572872 | tf_op jit(solution)/shard_map/ppermute | solution.py:37
  109.1 17.0 %collective-permute-start.21 = (bf16[2048,128]{1,0:T(8,128)(2,1)}, bf16[2048,128]{1,0:T(8,128)(2,1)S(1)}, u32[]{:S(2)}, u32[]{:S(2)}) collective-permute-start(bf16[2048,128]{1,0:T(8,128)(2,1)} %get-tuple-element.112.refs_12_), channel_id=1, source_target_pairs={{0,4},{4,8},{8,12},{12,0},{1,5},{5,9},{9,13},{13,1},{2,6},{6,10},{... | collective-permute-start | bytes 1572872 | tf_op jit(solution)/shard_map/ppermute | solution.py:32
  109.1 21.7 %collective-permute-start.22 = (bf16[2048,128]{1,0:T(8,128)(2,1)}, bf16[2048,128]{1,0:T(8,128)(2,1)S(1)}, u32[]{:S(2)}, u32[]{:S(2)}) collective-permute-start(bf16[2048,128]{1,0:T(8,128)(2,1)} %get-tuple-element.112.refs_12_), channel_id=1, source_target_pairs={{0,16},{16,0},{1,17},{17,1},{2,18},{18,2},{3,19},{19,3},{4,20},{20... | collective-permute-start | bytes 1572872 | tf_op jit(solution)/shard_map/ppermute | solution.py:37
  124.1 17.2 %collective-permute-start.23 = (bf16[2048,128]{1,0:T(8,128)(2,1)}, bf16[2048,128]{1,0:T(8,128)(2,1)S(1)}, u32[]{:S(2)}, u32[]{:S(2)}) collective-permute-start(bf16[2048,128]{1,0:T(8,128)(2,1)} %get-tuple-element.114.refs_6_), channel_id=1, source_target_pairs={{0,4},{4,8},{8,12},{12,0},{1,5},{5,9},{9,13},{13,1},{2,6},{6,10},{... | collective-permute-start | bytes 1572872 | tf_op jit(solution)/shard_map/ppermute | solution.py:32
  124.7 17.4 %collective-permute-start.24 = (bf16[2048,128]{1,0:T(8,128)(2,1)}, bf16[2048,128]{1,0:T(8,128)(2,1)S(1)}, u32[]{:S(2)}, u32[]{:S(2)}) collective-permute-start(bf16[2048,128]{1,0:T(8,128)(2,1)} %get-tuple-element.114.refs_6_), channel_id=1, source_target_pairs={{0,16},{16,0},{1,17},{17,1},{2,18},{18,2},{3,19},{19,3},{4,20},{20... | collective-permute-start | bytes 1572872 | tf_op jit(solution)/shard_map/ppermute | solution.py:37
  131.7 20.8 %collective-permute-start.25 = (bf16[2048,128]{1,0:T(8,128)(2,1)}, bf16[2048,128]{1,0:T(8,128)(2,1)S(1)}, u32[]{:S(2)}, u32[]{:S(2)}) collective-permute-start(bf16[2048,128]{1,0:T(8,128)(2,1)} %get-tuple-element.118.refs_6_), channel_id=1, source_target_pairs={{0,4},{4,8},{8,12},{12,0},{1,5},{5,9},{9,13},{13,1},{2,6},{6,10},{... | collective-permute-start | bytes 1572872 | tf_op jit(solution)/shard_map/ppermute | solution.py:32
  131.7 21.7 %collective-permute-start.26 = (bf16[2048,128]{1,0:T(8,128)(2,1)}, bf16[2048,128]{1,0:T(8,128)(2,1)S(1)}, u32[]{:S(2)}, u32[]{:S(2)}) collective-permute-start(bf16[2048,128]{1,0:T(8,128)(2,1)} %get-tuple-element.118.refs_6_), channel_id=1, source_target_pairs={{0,16},{16,0},{1,17},{17,1},{2,18},{18,2},{3,19},{19,3},{4,20},{20... | collective-permute-start | bytes 1572872 | tf_op jit(solution)/shard_map/ppermute | solution.py:37
  142.9 20.8 %collective-permute-start.27 = (bf16[2048,128]{1,0:T(8,128)(2,1)}, bf16[2048,128]{1,0:T(8,128)(2,1)S(1)}, u32[]{:S(2)}, u32[]{:S(2)}) collective-permute-start(bf16[2048,128]{1,0:T(8,128)(2,1)} %get-tuple-element.120.refs_6_), channel_id=1, source_target_pairs={{0,4},{4,8},{8,12},{12,0},{1,5},{5,9},{9,13},{13,1},{2,6},{6,10},{... | collective-permute-start | bytes 1572872 | tf_op jit(solution)/shard_map/ppermute | solution.py:32
  142.9 21.7 %collective-permute-start.28 = (bf16[2048,128]{1,0:T(8,128)(2,1)}, bf16[2048,128]{1,0:T(8,128)(2,1)S(1)}, u32[]{:S(2)}, u32[]{:S(2)}) collective-permute-start(bf16[2048,128]{1,0:T(8,128)(2,1)} %get-tuple-element.121.refs_8_), channel_id=1, source_target_pairs={{0,16},{16,0},{1,17},{17,1},{2,18},{18,2},{3,19},{19,3},{4,20},{20... | collective-permute-start | bytes 1572872 | tf_op jit(solution)/shard_map/ppermute | solution.py:37
  154.2 20.8 %collective-permute-start.29 = (bf16[2048,128]{1,0:T(8,128)(2,1)}, bf16[2048,128]{1,0:T(8,128)(2,1)S(1)}, u32[]{:S(2)}, u32[]{:S(2)}) collective-permute-start(bf16[2048,128]{1,0:T(8,128)(2,1)} %get-tuple-element.123.refs_8_), channel_id=1, source_target_pairs={{0,4},{4,8},{8,12},{12,0},{1,5},{5,9},{9,13},{13,1},{2,6},{6,10},{... | collective-permute-start | bytes 1572872 | tf_op jit(solution)/shard_map/ppermute | solution.py:32
  154.2 21.7 %collective-permute-start.30 = (bf16[2048,128]{1,0:T(8,128)(2,1)}, bf16[2048,128]{1,0:T(8,128)(2,1)S(1)}, u32[]{:S(2)}, u32[]{:S(2)}) collective-permute-start(bf16[2048,128]{1,0:T(8,128)(2,1)} %get-tuple-element.124.refs_8_), channel_id=1, source_target_pairs={{0,16},{16,0},{1,17},{17,1},{2,18},{18,2},{3,19},{19,3},{4,20},{20... | collective-permute-start | bytes 1572872 | tf_op jit(solution)/shard_map/ppermute | solution.py:37
  165.4 21.4 %collective-permute-start.31 = (bf16[2048,128]{1,0:T(8,128)(2,1)}, bf16[2048,128]{1,0:T(8,128)(2,1)S(1)}, u32[]{:S(2)}, u32[]{:S(2)}) collective-permute-start(bf16[2048,128]{1,0:T(8,128)(2,1)} %get-tuple-element.129.refs_10_), channel_id=1, source_target_pairs={{0,4},{4,8},{8,12},{12,0},{1,5},{5,9},{9,13},{13,1},{2,6},{6,10},{... | collective-permute-start | bytes 1572872 | tf_op jit(solution)/shard_map/ppermute | solution.py:32
  165.4 21.7 %collective-permute-start.32 = (bf16[2048,128]{1,0:T(8,128)(2,1)}, bf16[2048,128]{1,0:T(8,128)(2,1)S(1)}, u32[]{:S(2)}, u32[]{:S(2)}) collective-permute-start(bf16[2048,128]{1,0:T(8,128)(2,1)} %get-tuple-element.129.refs_10_), channel_id=1, source_target_pairs={{0,16},{16,0},{1,17},{17,1},{2,18},{18,2},{3,19},{19,3},{4,20},{20... | collective-permute-start | bytes 1572872 | tf_op jit(solution)/shard_map/ppermute | solution.py:37
  176.6 21.4 %collective-permute-start.33 = (bf16[2048,128]{1,0:T(8,128)(2,1)}, bf16[2048,128]{1,0:T(8,128)(2,1)S(1)}, u32[]{:S(2)}, u32[]{:S(2)}) collective-permute-start(bf16[2048,128]{1,0:T(8,128)(2,1)} %get-tuple-element.133.refs_12_), channel_id=1, source_target_pairs={{0,4},{4,8},{8,12},{12,0},{1,5},{5,9},{9,13},{13,1},{2,6},{6,10},{... | collective-permute-start | bytes 1572872 | tf_op jit(solution)/shard_map/ppermute | solution.py:32
  176.9 21.4 %collective-permute-start.34 = (bf16[2048,128]{1,0:T(8,128)(2,1)}, bf16[2048,128]{1,0:T(8,128)(2,1)S(1)}, u32[]{:S(2)}, u32[]{:S(2)}) collective-permute-start(bf16[2048,128]{1,0:T(8,128)(2,1)} %get-tuple-element.133.refs_12_), channel_id=1, source_target_pairs={{0,16},{16,0},{1,17},{17,1},{2,18},{18,2},{3,19},{19,3},{4,20},{20... | collective-permute-start | bytes 1572872 | tf_op jit(solution)/shard_map/ppermute | solution.py:37
  187.8 21.1 %collective-permute-start.35 = (bf16[2048,128]{1,0:T(8,128)(2,1)}, bf16[2048,128]{1,0:T(8,128)(2,1)S(1)}, u32[]{:S(2)}, u32[]{:S(2)}) collective-permute-start(bf16[2048,128]{1,0:T(8,128)(2,1)} %get-tuple-element.137.refs_6_), channel_id=1, source_target_pairs={{0,4},{4,8},{8,12},{12,0},{1,5},{5,9},{9,13},{13,1},{2,6},{6,10},{... | collective-permute-start | bytes 1572872 | tf_op jit(solution)/shard_map/ppermute | solution.py:32
  189.6 19.9 %collective-permute-start.36 = (bf16[2048,128]{1,0:T(8,128)(2,1)}, bf16[2048,128]{1,0:T(8,128)(2,1)S(1)}, u32[]{:S(2)}, u32[]{:S(2)}) collective-permute-start(bf16[2048,128]{1,0:T(8,128)(2,1)} %get-tuple-element.137.refs_6_), channel_id=1, source_target_pairs={{0,16},{16,0},{1,17},{17,1},{2,18},{18,2},{3,19},{19,3},{4,20},{20... | collective-permute-start | bytes 1572872 | tf_op jit(solution)/shard_map/ppermute | solution.py:37
  199.1 20.7 %collective-permute-start.37 = (bf16[2048,128]{1,0:T(8,128)(2,1)}, bf16[2048,128]{1,0:T(8,128)(2,1)S(1)}, u32[]{:S(2)}, u32[]{:S(2)}) collective-permute-start(bf16[2048,128]{1,0:T(8,128)(2,1)} %get-tuple-element.141.refs_8_), channel_id=1, source_target_pairs={{0,4},{4,8},{8,12},{12,0},{1,5},{5,9},{9,13},{13,1},{2,6},{6,10},{... | collective-permute-start | bytes 1572872 | tf_op jit(solution)/shard_map/ppermute | solution.py:32
  200.1 20.7 %collective-permute-start.38 = (bf16[2048,128]{1,0:T(8,128)(2,1)}, bf16[2048,128]{1,0:T(8,128)(2,1)S(1)}, u32[]{:S(2)}, u32[]{:S(2)}) collective-permute-start(bf16[2048,128]{1,0:T(8,128)(2,1)} %get-tuple-element.141.refs_8_), channel_id=1, source_target_pairs={{0,16},{16,0},{1,17},{17,1},{2,18},{18,2},{3,19},{19,3},{4,20},{20... | collective-permute-start | bytes 1572872 | tf_op jit(solution)/shard_map/ppermute | solution.py:37
  210.3 21.7 %collective-permute-start.39 = (bf16[2048,128]{1,0:T(8,128)(2,1)}, bf16[2048,128]{1,0:T(8,128)(2,1)S(1)}, u32[]{:S(2)}, u32[]{:S(2)}) collective-permute-start(bf16[2048,128]{1,0:T(8,128)(2,1)} %get-tuple-element.146.refs_6_), channel_id=1, source_target_pairs={{0,16},{16,0},{1,17},{17,1},{2,18},{18,2},{3,19},{19,3},{4,20},{20... | collective-permute-start | bytes 1572872 | tf_op jit(solution)/shard_map/ppermute | solution.py:37
  222.3 23.8 %collective-permute-start.44 = (bf16[2,4,1024]{2,1,0:T(4,128)(2,1)S(1)}, bf16[2,4,1024]{2,1,0:T(4,128)(2,1)S(1)}, u32[]{:S(2)}, u32[]{:S(2)}) collective-permute-start(bf16[2,4,1024]{2,1,0:T(4,128)(2,1)S(1)} %broadcast_select_fusion.1), channel_id=1, source_target_pairs={{0,8},{4,12},{8,0},{12,4},{1,9},{5,13},{9,1},{13,5},{2,10},{6,14},... | collective-permute-start | bytes 49160 | tf_op jit(solution)/shard_map/ppermute | solution.py:37
  224.1 23.0 %collective-permute-start.40 = (bf16[2048,128]{1,0:T(8,128)(2,1)}, bf16[2048,128]{1,0:T(8,128)(2,1)S(1)}, u32[]{:S(2)}, u32[]{:S(2)}) collective-permute-start(bf16[2048,128]{1,0:T(8,128)(2,1)} %get-tuple-element.148.refs_1_), channel_id=1, source_target_pairs={{0,16},{16,0},{1,17},{17,1},{2,18},{18,2},{3,19},{19,3},{4,20},{20... | collective-permute-start | bytes 1572872 | tf_op jit(solution)/shard_map/ppermute | solution.py:37
  246.2 17.7 %collective-permute-start.45 = (bf16[1,4,1024]{2,1,0:T(4,128)(2,1)S(1)}, bf16[1,4,1024]{2,1,0:T(4,128)(2,1)S(1)}, u32[]{:S(2)}, u32[]{:S(2)}) collective-permute-start(bf16[1,4,1024]{2,1,0:T(4,128)(2,1)S(1)} %broadcast_select_fusion.2), channel_id=1, source_target_pairs={{0,4},{4,0},{8,12},{12,8},{1,5},{5,1},{9,13},{13,9},{2,6},{6,2},{1... | collective-permute-start | bytes 24584 | tf_op jit(solution)/shard_map/ppermute | solution.py:37
  253.0 14.0 %copy-start.1 = (s32[8]{0:T(128)S(1)}, s32[8]{0:T(128)}, u32[]{:S(2)}) copy-start(s32[8]{0:T(128)} %param.16) | copy-start | bytes 100
  261.9 2.5 collective-permute-start.41
  261.9 3.6 %collective-permute-start.42 = (f32[2,384]{1,0:T(2,128)S(1)}, f32[2,384]{1,0:T(2,128)S(1)}, u32[]{:S(2)}, u32[]{:S(2)}) collective-permute-start(f32[2,384]{1,0:T(2,128)S(1)} %bitcast.105), channel_id=1, source_target_pairs={{0,2},{1,3},{2,0},{3,1},{4,6},{5,7},{6,4},{7,5},{8,10},{9,11},{10,... | collective-permute-start | bytes 9224 | tf_op jit(solution)/shard_map/ppermute | solution.py:37
  263.4 3.0 %collective-permute-start.43 = (f32[2,384]{1,0:T(2,128)S(1)}, f32[2,384]{1,0:T(2,128)S(1)}, u32[]{:S(2)}, u32[]{:S(2)}) collective-permute-start(f32[2,384]{1,0:T(2,128)S(1)} %bitcast.106), channel_id=1, source_target_pairs={{0,3},{1,2},{2,1},{3,0},{4,7},{5,6},{6,5},{7,4},{8,11},{9,10},{10,... | collective-permute-start | bytes 9224 | tf_op jit(solution)/shard_map/ppermute | solution.py:37
  (37 other events, 73.3 us)
